TPU v7x, 512 devices: a whole 4x4x16 slice. The times are simulated.
512 devices in a mesh: group: 64 (over z, x), local: 8 (over y, core).
Axes of the slice: x: 4, y: 4, z: 16, core: 2. Of those that a mesh axis runs over, the one named last changes fastest.
Arguments:
- layer_input: bfloat16 [8192, 3584], P('group', 'local'), may hold values from -6 to 6
- out_grad: bfloat16 [8192, 3584], P('group', 'local'), may hold values from -6 to 6
- expert_ids: int32 [8192, 2], P('group'), may hold values from 0 to 63, all different within a row; in each aligned block of 128 rows (0 to 127, 128 to 255, ...) at most 8 rows name the same one
- gate_probs: float32 [8192, 2], P('group'), may hold values from 0.05 to 1
- w_gate: bfloat16 [64, 3584, 1024], P('group', None, 'local'), may hold values from -0.09375 to 0.09375
- w_up: bfloat16 [64, 3584, 1024], P('group', None, 'local'), may hold values from -0.09375 to 0.09375
- w_down: bfloat16 [64, 1024, 3584], P('group', 'local'), may hold values from -0.1875 to 0.1875
Outputs:
- input_grad: bfloat16 [8192, 3584], P('group', 'local')
Inputs may be any that keep to these rules, and one draw needn't show every extreme that they name: `expert_ids`: each token names 2 different experts. Among the 128 tokens held by one index of group, at most 8 name any one expert, a bound that some block reaches of them.
All inputs are finite; a program needn't handle non-finite values.
Results may differ from a plain program's by a relative error of at most 0.019.
Values may be sent and summed in bfloat16 or wider, within the bound.
No kernel may reach another device: no remote copies, remote signals or barrier semaphores. Data moves between devices by JAX's collectives and lax.ppermute only.
A program may use at most 64 MiB of HBM per device.

v0:
```python
import jax
import jax.numpy as jnp
from jax import lax
from jax.sharding import PartitionSpec as P


def silu_backward(gate_act, up_act, hidden_grad):
    sigmoid_gate = jax.nn.sigmoid(gate_act)
    silu_value = gate_act * sigmoid_gate
    gate_grad = hidden_grad * up_act * sigmoid_gate * (1.0 + gate_act * (1.0 - sigmoid_gate))
    return (gate_grad.astype(jnp.bfloat16), (hidden_grad * silu_value).astype(jnp.bfloat16))


def contract_last(left, right):
    return lax.dot_general(
        left, right, (((1,), (1,)), ((), ())), preferred_element_type=jnp.float32
    )


def shards(layer_input, out_grad, expert_ids, gate_probs, w_gate, w_up, w_down):
    groups = lax.axis_size("group")
    token_count = layer_input.shape[0]
    top_count = expert_ids.shape[1]
    capacity = max(4, 2 * token_count * top_count // groups)
    slot_rows = groups * capacity
    gate_w = w_gate[0]
    up_w = w_up[0]
    down_w = w_down[0]
    flat_ids = expert_ids.reshape(-1)
    matches = (flat_ids[:, None] == jnp.arange(groups, dtype=jnp.int32)[None, :]).astype(jnp.int32)
    slot_ranks = jnp.sum(matches * jnp.cumsum(matches, axis=0), axis=1) - 1
    slot_index = flat_ids * capacity + slot_ranks
    pair_token = jnp.arange(token_count * top_count, dtype=jnp.int32) // top_count

    def scatter_rows(source):
        buffer = jnp.zeros((slot_rows, source.shape[1]), source.dtype)
        return (
            buffer.at[slot_index].set(source[pair_token]).reshape(groups, capacity, source.shape[1])
        )

    full_in, full_grad = (
        lax.all_gather(layer_input, "local", axis=1, tiled=True),
        lax.all_gather(out_grad, "local", axis=1, tiled=True),
    )
    recv_in, recv_grad = (
        lax.all_to_all(scatter_rows(full_in), "group", split_axis=0, concat_axis=0, tiled=True),
        lax.all_to_all(scatter_rows(full_grad), "group", split_axis=0, concat_axis=0, tiled=True),
    )
    recv_in = recv_in.reshape(slot_rows, -1)
    recv_grad = recv_grad.reshape(slot_rows, -1)
    gate_act = jnp.dot(recv_in, gate_w, preferred_element_type=jnp.float32)
    up_act = jnp.dot(recv_in, up_w, preferred_element_type=jnp.float32)
    hidden_grad = contract_last(recv_grad, down_w)
    gate_grad, up_grad = silu_backward(gate_act, up_act, hidden_grad)
    partial_sum = contract_last(gate_grad, gate_w) + contract_last(up_grad, up_w)
    flat_probs = gate_probs.reshape(-1, 1)
    summed = lax.psum_scatter(
        partial_sum.astype(jnp.bfloat16), "local", scatter_dimension=1, tiled=True
    ).astype(jnp.float32)
    returned = lax.all_to_all(
        summed.reshape(groups, capacity, -1).astype(jnp.bfloat16),
        "group",
        split_axis=0,
        concat_axis=0,
        tiled=True,
    ).astype(jnp.float32)
    rows_back = returned.reshape(slot_rows, -1)[slot_index] * flat_probs
    result = jnp.sum(rows_back.reshape(token_count, top_count, -1), axis=1)
    return result.astype(jnp.bfloat16)


def solution(mesh):
    placed = (
        P("group", "local"),
        P("group", "local"),
        P("group", None),
        P("group", None),
        P("group", None, "local"),
        P("group", None, "local"),
        P("group", "local", None),
    )
    return jax.shard_map(
        shards, mesh=mesh, in_specs=placed, out_specs=P("group", "local"), check_vma=False
    )
```

profile of v0, /device:TPU:1, one launch (start us, length us, event | category | flops | bytes accessed | tf_op | source)
XLA Modules:
  0.0 502.3 jit_solution(9156982677188269978)
XLA Ops:
  6.5 0.9 copy.30
  7.7 0.7 broadcast_multiply_fusion
  8.4 0.6 reduce-window.6
  9.6 20.5 %all_gather.7 = bf16[128,3584]{0,1:T(8,128)(2,1)S(1)} all-gather(bf16[128,448]{0,1:T(8,128)(2,1)} %param.7), channel_id=1, replica_groups=mesh['group'=64,'local'=8] {'local'}, dimensions={1}, use_global_device_ids=true | all-gather | bytes 1032192 | tf_op jit(solution)/shard_map/all_gather | solution.py:42
  30.2 0.5 copy.34
  30.7 10.9 %scatter_custom_fusion.1 = bf16[512,3584]{1,0:T(8,128)(2,1)} fusion(s32[256]{0:T(256)S(1)} %bitcast.58, bf16[128,3584]{1,0:T(8,128)(2,1)S(1)} %copy.34, s32[1024]{0:T(1024)S(1)} %pad_clamp_fusion.1, bf16[]{:T(256)} %constant.27.clone.1), kind=kCustom, calls=%fused_computation.12 | custom fusion | bytes 3670018 | tf_op jit(solution)/shard_map/scatter | solution.py:38
  41.6 13.9 %all-to-all-start.1 = ((bf16[64,8,3584]{2,1,0:T(8,128)(2,1)}), bf16[64,8,3584]{2,1,0:T(8,128)(2,1)}, u32[]{:S(2)}, u32[]{:S(2)}) async-start(bf16[64,8,3584]{2,1,0:T(8,128)(2,1)} %bitcast.57), calls=%async_computation.1 | async-start | bytes 7340032 | tf_op jit(solution)/shard_map/all_to_all | solution.py:46
  55.5 13.8 %all_gather.6 = bf16[128,3584]{0,1:T(8,128)(2,1)S(1)} all-gather(bf16[128,448]{0,1:T(8,128)(2,1)S(1)} %copy-done.3), channel_id=1, replica_groups=mesh['group'=64,'local'=8] {'local'}, dimensions={1}, use_global_device_ids=true | all-gather | bytes 1032192 | tf_op jit(solution)/shard_map/all_gather | solution.py:43
  69.3 0.5 copy.33
  69.8 10.8 %scatter_custom_fusion = bf16[512,3584]{1,0:T(8,128)(2,1)} fusion(s32[256]{0:T(256)S(1)} %bitcast.59, bf16[128,3584]{1,0:T(8,128)(2,1)S(1)} %copy.33, s32[1024]{0:T(1024)S(1)} %pad_clamp_fusion.1, bf16[]{:T(256)} %constant.27.clone.1), kind=kCustom, calls=%fused_computation.14 | custom fusion | bytes 3670018 | tf_op jit(solution)/shard_map/scatter | solution.py:38
  80.7 136.7 %all-to-all-done.1 = bf16[64,8,3584]{2,1,0:T(8,128)(2,1)} async-done(((bf16[64,8,3584]{2,1,0:T(8,128)(2,1)}), bf16[64,8,3584]{2,1,0:T(8,128)(2,1)}, u32[]{:S(2)}, u32[]{:S(2)}) %all-to-all-start.1) | async-done | bytes 3670048 | tf_op jit(solution)/shard_map/all_to_all | solution.py:46
  217.3 11.3 %all-to-all-start = ((bf16[64,8,3584]{2,1,0:T(8,128)(2,1)}), bf16[64,8,3584]{2,1,0:T(8,128)(2,1)}, u32[]{:S(2)}, u32[]{:S(2)}) async-start(bf16[64,8,3584]{2,1,0:T(8,128)(2,1)} %bitcast.56), calls=%async_computation | async-start | bytes 7340032 | tf_op jit(solution)/shard_map/all_to_all | solution.py:47
  228.7 3.2 fusion
  231.9 158.3 %all-to-all-done = bf16[64,8,3584]{2,1,0:T(8,128)(2,1)} async-done(((bf16[64,8,3584]{2,1,0:T(8,128)(2,1)}), bf16[64,8,3584]{2,1,0:T(8,128)(2,1)}, u32[]{:S(2)}, u32[]{:S(2)}) %all-to-all-start) | async-done | bytes 3670048 | tf_op jit(solution)/shard_map/all_to_all | solution.py:47
  390.1 3.1 fusion.4
  393.3 9.0 %fusion.25 = f32[512,3584]{0,1:T(8,128)} fusion(f32[512,128]{1,0:T(8,128)S(1)} %fusion.4, bf16[64,8,3584]{2,1,0:T(8,128)(2,1)} %all-to-all-done.1, bf16[1,3584,128]{2,1,0:T(8,128)(2,1)S(1)} %copy-done.1, bf16[1,3584,128]{2,1,0:T(8,128)(2,1)S(1)} %copy-done, f32[512,128]{1,0:T(8,128)S(1)} %fusion), kind=kOutput, calls=%fused_computation.22 | convolution fusion | flops 940179456 | bytes 13369344 | tf_op jit(solution)/shard_map/dot_general | solution.py:15
  402.3 6.2 %add_convert_fusion = bf16[512,3584]{0,1:T(8,128)(2,1)} fusion(f32[512,3584]{0,1:T(8,128)} %fusion.25, bf16[1,3584,128]{2,1,0:T(8,128)(2,1)S(1)} %copy-done, f32[512,128]{1,0:T(8,128)S(1)} %fusion.4, f32[512,128]{1,0:T(8,128)S(1)} %fusion), kind=kOutput, calls=%fused_computation.5 | convolution fusion | flops 473825280 | bytes 12451840 | tf_op jit(solution)/shard_map/dot_general | solution.py:15
  408.5 40.0 %reduce-scatter.2.cloned.1.call-done = bf16[512,448]{0,1:T(8,128)(2,1)} async-done(((bf16[512,3584]{0,1:T(8,128)(2,1)}), bf16[512,448]{0,1:T(8,128)(2,1)}) %reduce-scatter.2.cloned.1.call-update) | async-done | bytes 458768 | tf_op jit(solution)/shard_map/reduce_scatter | solution.py:57
  448.4 2.0 copy.35
  450.5 14.4 %all-to-all-start.2 = ((bf16[64,8,448]{2,1,0:T(8,128)(2,1)}), bf16[64,8,448]{2,1,0:T(8,128)(2,1)S(1)}, u32[]{:S(2)}, u32[]{:S(2)}) async-start(bf16[64,8,448]{2,1,0:T(8,128)(2,1)} %bitcast.11), calls=%async_computation.3 | async-start | bytes 1048576 | tf_op jit(solution)/shard_map/all_to_all | solution.py:60
  465.0 27.5 %all-to-all-done.2 = bf16[64,8,448]{2,1,0:T(8,128)(2,1)S(1)} async-done(((bf16[64,8,448]{2,1,0:T(8,128)(2,1)}), bf16[64,8,448]{2,1,0:T(8,128)(2,1)S(1)}, u32[]{:S(2)}, u32[]{:S(2)}) %all-to-all-start.2) | async-done | bytes 458784 | tf_op jit(solution)/shard_map/all_to_all | solution.py:60
  492.6 1.0 gather_fusion
  493.9 0.7 multiply_reduce_fusion
  494.7 0.8 copy.37
  (29 shorter events, 1.6 us)
Async XLA Ops:
  6.5 386.7 %copy-start = (bf16[1,3584,128]{2,1,0:T(8,128)(2,1)S(1)}, bf16[1,3584,128]{2,1,0:T(8,128)(2,1)}, u32[]{:S(2)}) copy-start(bf16[1,3584,128]{2,1,0:T(8,128)(2,1)} %param.12) | copy-start | bytes 2752516
  41.6 13.9 %copy-start.3 = (bf16[128,448]{0,1:T(8,128)(2,1)S(1)}, bf16[128,448]{0,1:T(8,128)(2,1)}, u32[]{:S(2)}) copy-start(bf16[128,448]{0,1:T(8,128)(2,1)} %param.8) | copy-start | bytes 344068
  41.6 175.7 %all-to-all-start.1 = ((bf16[64,8,3584]{2,1,0:T(8,128)(2,1)}), bf16[64,8,3584]{2,1,0:T(8,128)(2,1)}, u32[]{:S(2)}, u32[]{:S(2)}) async-start(bf16[64,8,3584]{2,1,0:T(8,128)(2,1)} %bitcast.57), calls=%async_computation.1 | async-start | bytes 7340032 | tf_op jit(solution)/shard_map/all_to_all | solution.py:46
  217.3 11.3 %copy-start.1 = (bf16[1,3584,128]{2,1,0:T(8,128)(2,1)S(1)}, bf16[1,3584,128]{2,1,0:T(8,128)(2,1)}, u32[]{:S(2)}) copy-start(bf16[1,3584,128]{2,1,0:T(8,128)(2,1)} %param.11) | copy-start | bytes 2752516
  217.3 172.8 %all-to-all-start = ((bf16[64,8,3584]{2,1,0:T(8,128)(2,1)}), bf16[64,8,3584]{2,1,0:T(8,128)(2,1)}, u32[]{:S(2)}, u32[]{:S(2)}) async-start(bf16[64,8,3584]{2,1,0:T(8,128)(2,1)} %bitcast.56), calls=%async_computation | async-start | bytes 7340032 | tf_op jit(solution)/shard_map/all_to_all | solution.py:47
  228.6 161.5 %copy-start.2 = (bf16[1,128,3584]{2,1,0:T(8,128)(2,1)S(1)}, bf16[1,128,3584]{2,1,0:T(8,128)(2,1)}, u32[]{:S(2)}) copy-start(bf16[1,128,3584]{2,1,0:T(8,128)(2,1)} %param.13) | copy-start | bytes 2752516
  228.6 219.8 %reduce-scatter.2.cloned.1.call-start = ((), (), s32[]{:S(2)}) async-start(), calls=%async_computation.4 | async-start | bytes 4128768 | tf_op jit(solution)/shard_map/reduce_scatter | solution.py:57
  408.5 56.4 %copy-start.4 = (f32[128,2]{0,1:T(2,128)S(1)}, f32[128,2]{0,1:T(2,128)}, u32[]{:S(2)}) copy-start(f32[128,2]{0,1:T(2,128)} %param.10) | copy-start | bytes 3076
  450.5 42.0 %all-to-all-start.2 = ((bf16[64,8,448]{2,1,0:T(8,128)(2,1)}), bf16[64,8,448]{2,1,0:T(8,128)(2,1)S(1)}, u32[]{:S(2)}, u32[]{:S(2)}) async-start(bf16[64,8,448]{2,1,0:T(8,128)(2,1)} %bitcast.11), calls=%async_computation.3 | async-start | bytes 1048576 | tf_op jit(solution)/shard_map/all_to_all | solution.py:60
Sparse Core Ops, SparseCore 0:
  408.6 39.7 reduce-scatter.1
where the time goes:
time: 508 us; the launch traced here: 502 us
  waiting for transfers between devices  362 us (71%)
  starting transfers between devices  39.6 us (8%)
  blocking collectives  34.4 us (7%)
  local copies, waits for them, and re-layouts  28.6 us (6%)
  matrix products  21.5 us (4%)
  between operations  13.6 us (3%)
    all_to_all x1, waiting for transfers between devices, shards(): lax.all_to_all(scatter_rows(full_grad), 'group', split_axis=0, concat_axi...  158 us
    all_to_all x1, waiting for transfers between devices, shards(): lax.all_to_all(scatter_rows(full_in), 'group', split_axis=0, concat_axis=...  137 us
    reduce_scatter x1, waiting for transfers between devices, shards(): lax.psum_scatter(partial_sum.astype(jnp.bfloat16), 'local', scatter_dimen...  40 us
    all_to_all x1, waiting for transfers between devices, shards(): lax.all_to_all(summed.reshape(groups, capacity, -1).astype(jnp.bfloat16),...  27.5 us
    scatter x2, local copies, waits for them, and re-layouts, scatter_rows(): buffer.at[slot_index].set(source[pair_token])  21.7 us
    all_gather x1, blocking collectives, shards(): lax.all_gather(layer_input, 'local', axis=1, tiled=True)  20.5 us
    dot_general x3, matrix products, contract_last(): lax.dot_general(left, right, (((1,), (1,)), ((), ())), preferred_element_...  18.3 us
    all_to_all x1, starting transfers between devices, shards(): lax.all_to_all(summed.reshape(groups, capacity, -1).astype(jnp.bfloat16),...  14.4 us
  transfers between devices with their start and end apart: 4, of which 4 were waited for; matrix products, arithmetic and copies ran while one was open for 3% of the time, Pallas kernels for 0%

commit v1 on v0

v1 whole, which is shorter than its diff:
```python
import jax
import jax.numpy as jnp
from jax import lax
from jax.sharding import Mesh, PartitionSpec as P

N_Z, N_X, N_Y, N_C = 16, 4, 4, 2
GROUP = ("z", "x")
LOCAL = ("y", "c")
SLOTS = 4


def dot(left, right, left_dim, right_dim):
    return lax.dot_general(
        left, right, (((left_dim,), (right_dim,)), ((), ())), preferred_element_type=jnp.float32
    )


def shift(value, axis, step, size):
    return lax.ppermute(value, axis, [(i, (i + step) % size) for i in range(size)])


def shards(layer_input, out_grad, expert_ids, gate_probs, w_gate, w_up, w_down):
    bf16 = jnp.bfloat16
    groups = N_Z * N_X
    tokens, width = layer_input.shape
    rows = groups * SLOTS
    chip = N_C * width
    core = lax.axis_index("c")
    here = lax.axis_index("y")

    own = jnp.stack([layer_input.T, out_grad.T])
    both = lax.all_gather(own, "c", axis=1, tiled=True).reshape(2 * chip, tokens)

    first, second = expert_ids[:, 0], expert_ids[:, 1]
    position = jnp.arange(tokens, dtype=jnp.int32)
    before = position[None, :] < position[:, None]

    def rank(ids):
        same = (ids[:, None] == first[None, :]) | (ids[:, None] == second[None, :])
        return jnp.sum((same & before).astype(jnp.int32), axis=1)

    def slot_of(ids):
        place = rank(ids) - SLOTS * core
        return jnp.where((place >= 0) & (place < SLOTS), ids * SLOTS + place, -1)

    slot_ids = jnp.arange(rows, dtype=jnp.int32)
    hit_first = slot_of(first)[None, :] == slot_ids[:, None]
    hit_second = slot_of(second)[None, :] == slot_ids[:, None]
    select = (hit_first | hit_second).astype(bf16)
    weight = jnp.where(hit_first, gate_probs[:, 0][None, :], 0.0) + jnp.where(
        hit_second, gate_probs[:, 1][None, :], 0.0
    )
    weight_high = weight.astype(bf16)
    weight_low = (weight - weight_high.astype(jnp.float32)).astype(bf16)
    weights = jnp.concatenate([weight_high, weight_low], axis=1)

    send = dot(select, both, 1, 1).astype(bf16).reshape(groups, SLOTS, 2 * chip)
    send, w_gate, w_up, w_down = lax.optimization_barrier((send, w_gate, w_up, w_down))
    recv = lax.all_to_all(send, GROUP, split_axis=0, concat_axis=0, tiled=True)

    mats = jnp.stack([w_gate[0], w_up[0], w_down[0].T])

    def part(step):
        return lax.dynamic_slice_in_dim(mats, chip * ((here + step) % N_Y), chip, axis=1)

    blocks = jnp.stack([part(0)] + [shift(part(d), "y", d, N_Y) for d in range(1, N_Y)])
    other = shift(blocks, "c", 1, N_C)
    full = [
        jnp.concatenate([blocks[d], other[d]], axis=2) for d in range(N_Y)
    ]

    recv = recv.reshape(rows, 2 * chip)
    rows_in, rows_grad = recv[:, :chip], recv[:, chip:]

    def partial(d):
        return jnp.stack(
            [dot(rows_in, full[d][0], 1, 0), dot(rows_in, full[d][1], 1, 0), dot(rows_grad, full[d][2], 1, 0)]
        )

    sums = partial(0)
    for d in range(1, N_Y):
        sums = sums + shift(partial(d).astype(bf16), "y", -d, N_Y).astype(jnp.float32)
    gate_act, up_act, hidden_grad = sums[0], sums[1], sums[2]
    sigmoid_gate = jax.nn.sigmoid(gate_act)
    gate_grad = hidden_grad * up_act * sigmoid_gate * (1.0 + gate_act * (1.0 - sigmoid_gate))
    up_grad = hidden_grad * gate_act * sigmoid_gate
    grads = jnp.stack([gate_grad.astype(bf16), up_grad.astype(bf16)])
    back = jnp.zeros((rows, chip), jnp.float32)
    for d in range(N_Y):
        theirs = shift(grads, "y", d, N_Y) if d else grads
        back = back + dot(theirs[0], full[d][0], 1, 1) + dot(theirs[1], full[d][1], 1, 1)

    returned = lax.all_to_all(
        back.astype(bf16).reshape(groups, SLOTS, chip), GROUP, split_axis=0, concat_axis=0, tiled=True
    ).reshape(rows, chip)
    mixed = dot(returned, weights, 0, 0)
    mixed = (mixed[:, :tokens] + mixed[:, tokens:]).reshape(N_C, width, tokens)
    mine = lax.dynamic_index_in_dim(mixed, core, 0, keepdims=False)
    sibling = lax.dynamic_index_in_dim(mixed, 1 - core, 0, keepdims=False)
    result = mine + shift(sibling, "c", 1, N_C)
    return result.astype(bf16).T


def solution(mesh):
    split = Mesh(mesh.devices.reshape(N_Z, N_X, N_Y, N_C), GROUP + LOCAL)
    placed = (
        P(GROUP, LOCAL),
        P(GROUP, LOCAL),
        P(GROUP, None),
        P(GROUP, None),
        P(GROUP, None, LOCAL),
        P(GROUP, None, LOCAL),
        P(GROUP, LOCAL, None),
    )
    return jax.shard_map(
        shards, mesh=split, in_specs=placed, out_specs=P(GROUP, LOCAL), check_vma=False
    )
```

time: 508 us -> 184 us (0.36)
  waiting for transfers between devices: 362 us -> 84.2 us
  starting transfers between devices: 39.6 us -> 66.6 us
  blocking collectives: 34.4 us -> 8.64 us
  local copies, waits for them, and re-layouts: 28.6 us -> 9.55 us
  matrix products: 21.5 us -> 8.25 us
  between operations: 13.6 us -> 0.52 us
    all_to_all x3 -> x2, waiting for transfers between devices: 322 us -> 48.7 us  [the longest x1 26.4 us: shards(): lax.all_to_all(back.astype(bf16).reshape(groups, SLOTS, chip), GROUP, spl...]
    reduce_scatter x1 -> x0, waiting for transfers between devices: 40 us -> none  [shards(): lax.psum_scatter(partial_sum.astype(jnp.bfloat16), 'local', scatter_dimen...]
    ppermute x0 -> x11, starting transfers between devices: none -> 36.3 us  [shift(): lax.ppermute(value, axis, [(i, (i + step) % size) for i in range(size)])]
    ppermute x0 -> x11, waiting for transfers between devices: none -> 35.5 us  [shift(): lax.ppermute(value, axis, [(i, (i + step) % size) for i in range(size)])]
    all_gather x2 -> x1, blocking collectives: 34.4 us -> 8.64 us  [shards(): lax.all_gather(own, 'c', axis=1, tiled=True).reshape(2 * chip, tokens)]
    scatter x2 -> x0, local copies, waits for them, and re-layouts: 21.7 us -> none  [scatter_rows(): buffer.at[slot_index].set(source[pair_token])]
    dot_general x4 -> x22, matrix products: 21.5 us -> 8.25 us  [dot(): lax.dot_general(left, right, (((left_dim,), (right_dim,)), ((), ())), pre...]
    all_to_all x3 -> x2, starting transfers between devices: 39.5 us -> 30.3 us  [the longest x1 15.4 us: shards(): recv = lax.all_to_all(send, GROUP, split_axis=0, concat_axis=0, tiled=True)]
  transfers between devices with their start and end apart: 4 -> 13, of which waited for: 4 -> 10; matrix products, arithmetic and copies ran while one was open for 3% -> 4% of each run, Pallas kernels for 0% -> 0%
where the time goes in v1:
time: 184 us; the launch traced here: 183 us
  waiting for transfers between devices  84.2 us (46%)
  starting transfers between devices  66.6 us (36%)
  local copies, waits for them, and re-layouts  9.55 us (5%)
  blocking collectives  8.64 us (5%)
  matrix products  8.25 us (4%)
  other arithmetic  5.06 us (3%)
    ppermute x11, starting transfers between devices, shift(): lax.ppermute(value, axis, [(i, (i + step) % size) for i in range(size)])  36.3 us
    ppermute x11, waiting for transfers between devices, shift(): lax.ppermute(value, axis, [(i, (i + step) % size) for i in range(size)])  35.5 us
    all_to_all x1, waiting for transfers between devices, shards(): lax.all_to_all(back.astype(bf16).reshape(groups, SLOTS, chip), GROUP, spl...  26.4 us
    all_to_all x1, waiting for transfers between devices, shards(): recv = lax.all_to_all(send, GROUP, split_axis=0, concat_axis=0, tiled=True)  22.3 us
    all_to_all x1, starting transfers between devices, shards(): recv = lax.all_to_all(send, GROUP, split_axis=0, concat_axis=0, tiled=True)  15.4 us
    all_to_all x1, starting transfers between devices, shards(): lax.all_to_all(back.astype(bf16).reshape(groups, SLOTS, chip), GROUP, spl...  14.8 us
    all_gather x1, blocking collectives, shards(): lax.all_gather(own, 'c', axis=1, tiled=True).reshape(2 * chip, tokens)  8.64 us
    dot_general x22, matrix products, dot(): lax.dot_general(left, right, (((left_dim,), (right_dim,)), ((), ())), pre...  8.25 us
  transfers between devices with their start and end apart: 13, of which 10 were waited for; matrix products, arithmetic and copies ran while one was open for 4% of the time, Pallas kernels for 0%

profile of v1, /device:TPU:1, one launch (start us, length us, event | category | flops | bytes accessed | tf_op | source)
XLA Modules:
  0.0 182.8 jit_solution(13308187228344065510)
XLA Ops:
  1.7 8.6 %all_gather.3 = bf16[2,896,128]{2,1,0:T(8,128)(2,1)S(1)} all-gather(bf16[2,448,128]{2,1,0:T(8,128)(2,1)S(1)} %pad_maximum_fusion.10), channel_id=1, replica_groups=mesh['z'=16,'x'=4,'y'=4,'c'=2] {'c'}, dimensions={1}, use_global_device_ids=true | all-gather | bytes 688128 | tf_op jit(solution)/shard_map/all_gather | solution.py:32
  17.6 1.9 %collective-permute-start = (bf16[3,896,128]{1,2,0:T(8,128)(2,1)}, bf16[3,896,128]{1,2,0:T(8,128)(2,1)S(1)}, u32[]{:S(2)}, u32[]{:S(2)}) collective-permute-start(bf16[3,896,128]{1,2,0:T(8,128)(2,1)} %get-tuple-element.22), channel_id=1, source_target_pairs={{0,2},{2,4},{4,6},{6,0},{1,3},{3,5},{5,7},{7,1},{8,10},{10,12},{12... | collective-permute-start | bytes 2064392 | tf_op jit(solution)/shard_map/ppermute | solution.py:19
  19.5 1.9 %collective-permute-start.1 = (bf16[3,896,128]{1,2,0:T(8,128)(2,1)}, bf16[3,896,128]{1,2,0:T(8,128)(2,1)S(1)}, u32[]{:S(2)}, u32[]{:S(2)}) collective-permute-start(bf16[3,896,128]{1,2,0:T(8,128)(2,1)} %get-tuple-element.21), channel_id=1, source_target_pairs={{0,4},{2,6},{4,0},{6,2},{1,5},{3,7},{5,1},{7,3},{8,12},{10,14},{12... | collective-permute-start | bytes 2064392 | tf_op jit(solution)/shard_map/ppermute | solution.py:19
  21.4 4.6 %collective-permute-start.2 = (bf16[3,896,128]{1,2,0:T(8,128)(2,1)S(1)}, bf16[3,896,128]{1,2,0:T(8,128)(2,1)S(1)}, u32[]{:S(2)}, u32[]{:S(2)}) collective-permute-start(bf16[3,896,128]{1,2,0:T(8,128)(2,1)S(1)} %get-tuple-element.20), channel_id=1, source_target_pairs={{0,6},{2,0},{4,2},{6,4},{1,7},{3,1},{5,3},{7,5},{8,14},{10,8},{12,... | collective-permute-start | bytes 2064392 | tf_op jit(solution)/shard_map/ppermute | solution.py:19
  26.0 15.4 %all-to-all-start = ((bf16[64,4,1792]{2,1,0:T(4,128)(2,1)}), bf16[64,4,1792]{2,1,0:T(4,128)(2,1)}, u32[]{:S(2)}, u32[]{:S(2)}) async-start(bf16[64,4,1792]{2,1,0:T(4,128)(2,1)} %reshape.51), calls=%async_computation | async-start | bytes 1835008 | tf_op jit(solution)/shard_map/all_to_all | solution.py:59
  41.4 10.9 %collective-permute-done = bf16[3,896,128]{1,2,0:T(8,128)(2,1)S(1)} collective-permute-done((bf16[3,896,128]{1,2,0:T(8,128)(2,1)}, bf16[3,896,128]{1,2,0:T(8,128)(2,1)S(1)}, u32[]{:S(2)}, u32[]{:S(2)}) %collective-permute-start) | collective-permute-done | bytes 688160 | tf_op jit(solution)/shard_map/ppermute | solution.py:19
  52.4 2.2 %collective-permute-done.2 = bf16[3,896,128]{1,2,0:T(8,128)(2,1)S(1)} collective-permute-done((bf16[3,896,128]{1,2,0:T(8,128)(2,1)S(1)}, bf16[3,896,128]{1,2,0:T(8,128)(2,1)S(1)}, u32[]{:S(2)}, u32[]{:S(2)}) %collective-permute-start.2) | collective-permute-done | bytes 688160 | tf_op jit(solution)/shard_map/ppermute | solution.py:19
  55.4 3.3 %collective-permute-start.3 = (bf16[4,3,896,128]{2,3,1,0:T(8,128)(2,1)S(1)}, bf16[4,3,896,128]{2,3,1,0:T(8,128)(2,1)S(1)}, u32[]{:S(2)}, u32[]{:S(2)}) collective-permute-start(bf16[4,3,896,128]{2,3,1,0:T(8,128)(2,1)S(1)} %pad_maximum_fusion.1), channel_id=1, source_target_pairs={{0,1},{1,0},{2,3},{3,2},{4,5},{5,4},{6,7},{7,6},{8,9},{9,8},{10,11... | collective-permute-start | bytes 8257544 | tf_op jit(solution)/shard_map/ppermute | solution.py:19
  58.7 4.7 %collective-permute-done.3 = bf16[4,3,896,128]{2,3,1,0:T(8,128)(2,1)S(1)} collective-permute-done((bf16[4,3,896,128]{2,3,1,0:T(8,128)(2,1)S(1)}, bf16[4,3,896,128]{2,3,1,0:T(8,128)(2,1)S(1)}, u32[]{:S(2)}, u32[]{:S(2)}) %collective-permute-start.3) | collective-permute-done | bytes 2752544 | tf_op jit(solution)/shard_map/ppermute | solution.py:19
  64.8 22.3 %all-to-all-done = bf16[64,4,1792]{2,1,0:T(4,128)(2,1)} async-done(((bf16[64,4,1792]{2,1,0:T(4,128)(2,1)}), bf16[64,4,1792]{2,1,0:T(4,128)(2,1)}, u32[]{:S(2)}, u32[]{:S(2)}) %all-to-all-start) | async-done | bytes 917536 | tf_op jit(solution)/shard_map/all_to_all | solution.py:59
  87.2 1.6 reshape.52
  91.0 2.0 %collective-permute-start.4 = (bf16[3,256,256]{2,1,0:T(8,128)(2,1)S(1)}, bf16[3,256,256]{2,1,0:T(8,128)(2,1)S(1)}, u32[]{:S(2)}, u32[]{:S(2)}) collective-permute-start(bf16[3,256,256]{2,1,0:T(8,128)(2,1)S(1)} %pad_maximum_fusion.6), channel_id=1, source_target_pairs={{0,6},{2,0},{4,2},{6,4},{1,7},{3,1},{5,3},{7,5},{8,14},{10,8},{12,... | collective-permute-start | bytes 1179656 | tf_op jit(solution)/shard_map/ppermute | solution.py:19
  94.0 4.0 %collective-permute-start.5 = (bf16[3,256,256]{2,1,0:T(8,128)(2,1)S(1)}, bf16[3,256,256]{2,1,0:T(8,128)(2,1)S(1)}, u32[]{:S(2)}, u32[]{:S(2)}) collective-permute-start(bf16[3,256,256]{2,1,0:T(8,128)(2,1)S(1)} %pad_maximum_fusion.7), channel_id=1, source_target_pairs={{0,4},{2,6},{4,0},{6,2},{1,5},{3,7},{5,1},{7,3},{8,12},{10,14},{12... | collective-permute-start | bytes 1179656 | tf_op jit(solution)/shard_map/ppermute | solution.py:19
  99.2 1.9 %collective-permute-start.6 = (bf16[3,256,256]{2,1,0:T(8,128)(2,1)S(1)}, bf16[3,256,256]{2,1,0:T(8,128)(2,1)S(1)}, u32[]{:S(2)}, u32[]{:S(2)}) collective-permute-start(bf16[3,256,256]{2,1,0:T(8,128)(2,1)S(1)} %pad_maximum_fusion.8), channel_id=1, source_target_pairs={{0,2},{2,4},{4,6},{6,0},{1,3},{3,5},{5,7},{7,1},{8,10},{10,12},{12... | collective-permute-start | bytes 1179656 | tf_op jit(solution)/shard_map/ppermute | solution.py:19
  102.1 1.9 %collective-permute-done.5 = bf16[3,256,256]{2,1,0:T(8,128)(2,1)S(1)} collective-permute-done((bf16[3,256,256]{2,1,0:T(8,128)(2,1)S(1)}, bf16[3,256,256]{2,1,0:T(8,128)(2,1)S(1)}, u32[]{:S(2)}, u32[]{:S(2)}) %collective-permute-start.5) | collective-permute-done | bytes 393248 | tf_op jit(solution)/shard_map/ppermute | solution.py:19
  104.0 10.3 %collective-permute-done.6 = bf16[3,256,256]{2,1,0:T(8,128)(2,1)S(1)} collective-permute-done((bf16[3,256,256]{2,1,0:T(8,128)(2,1)S(1)}, bf16[3,256,256]{2,1,0:T(8,128)(2,1)S(1)}, u32[]{:S(2)}, u32[]{:S(2)}) %collective-permute-start.6) | collective-permute-done | bytes 393248 | tf_op jit(solution)/shard_map/ppermute | solution.py:19
  115.0 1.9 %collective-permute-start.7 = (bf16[2,256,256]{2,1,0:T(8,128)(2,1)S(1)}, bf16[2,256,256]{2,1,0:T(8,128)(2,1)S(1)}, u32[]{:S(2)}, u32[]{:S(2)}) collective-permute-start(bf16[2,256,256]{2,1,0:T(8,128)(2,1)S(1)} %pad_maximum_fusion.9), channel_id=1, source_target_pairs={{0,2},{2,4},{4,6},{6,0},{1,3},{3,5},{5,7},{7,1},{8,10},{10,12},{12... | collective-permute-start | bytes 786440 | tf_op jit(solution)/shard_map/ppermute | solution.py:19
  116.9 4.0 %collective-permute-start.8 = (bf16[2,256,256]{2,1,0:T(8,128)(2,1)S(1)}, bf16[2,256,256]{2,1,0:T(8,128)(2,1)S(1)}, u32[]{:S(2)}, u32[]{:S(2)}) collective-permute-start(bf16[2,256,256]{2,1,0:T(8,128)(2,1)S(1)} %pad_maximum_fusion.9), channel_id=1, source_target_pairs={{0,4},{2,6},{4,0},{6,2},{1,5},{3,7},{5,1},{7,3},{8,12},{10,14},{12... | collective-permute-start | bytes 786440 | tf_op jit(solution)/shard_map/ppermute | solution.py:19
  120.9 4.0 %collective-permute-start.9 = (bf16[2,256,256]{2,1,0:T(8,128)(2,1)S(1)}, bf16[2,256,256]{2,1,0:T(8,128)(2,1)S(1)}, u32[]{:S(2)}, u32[]{:S(2)}) collective-permute-start(bf16[2,256,256]{2,1,0:T(8,128)(2,1)S(1)} %pad_maximum_fusion.9), channel_id=1, source_target_pairs={{0,6},{2,0},{4,2},{6,4},{1,7},{3,1},{5,3},{7,5},{8,14},{10,8},{12,... | collective-permute-start | bytes 786440 | tf_op jit(solution)/shard_map/ppermute | solution.py:19
  125.2 2.4 %collective-permute-done.8 = bf16[2,256,256]{2,1,0:T(8,128)(2,1)S(1)} collective-permute-done((bf16[2,256,256]{2,1,0:T(8,128)(2,1)S(1)}, bf16[2,256,256]{2,1,0:T(8,128)(2,1)S(1)}, u32[]{:S(2)}, u32[]{:S(2)}) %collective-permute-start.8) | collective-permute-done | bytes 262176 | tf_op jit(solution)/shard_map/ppermute | solution.py:19
  128.2 1.9 %collective-permute-done.9 = bf16[2,256,256]{2,1,0:T(8,128)(2,1)S(1)} collective-permute-done((bf16[2,256,256]{2,1,0:T(8,128)(2,1)S(1)}, bf16[2,256,256]{2,1,0:T(8,128)(2,1)S(1)}, u32[]{:S(2)}, u32[]{:S(2)}) %collective-permute-start.9) | collective-permute-done | bytes 262176 | tf_op jit(solution)/shard_map/ppermute | solution.py:19
  132.4 14.8 %all-to-all-start.1 = ((bf16[64,4,896]{2,1,0:T(4,128)(2,1)}), bf16[64,4,896]{2,1,0:T(4,128)(2,1)S(1)}, u32[]{:S(2)}, u32[]{:S(2)}) async-start(bf16[64,4,896]{2,1,0:T(4,128)(2,1)} %reshape.53), calls=%async_computation.1 | async-start | bytes 917504 | tf_op jit(solution)/shard_map/all_to_all | solution.py:93
  147.3 26.4 %all-to-all-done.1 = bf16[64,4,896]{2,1,0:T(4,128)(2,1)S(1)} async-done(((bf16[64,4,896]{2,1,0:T(4,128)(2,1)}), bf16[64,4,896]{2,1,0:T(4,128)(2,1)S(1)}, u32[]{:S(2)}, u32[]{:S(2)}) %all-to-all-start.1) | async-done | bytes 458784 | tf_op jit(solution)/shard_map/all_to_all | solution.py:93
  174.2 6.8 %collective-permute-start.10 = (f32[448,128]{1,0:T(8,128)S(1)}, f32[448,128]{1,0:T(8,128)S(1)}, u32[]{:S(2)}, u32[]{:S(2)}) collective-permute-start(f32[448,128]{1,0:T(8,128)S(1)} %dynamic-slice_bitcast_fusion), channel_id=1, source_target_pairs={{0,1},{1,0},{2,3},{3,2},{4,5},{5,4},{6,7},{7,6},{8,9},{9,8},{10,11... | collective-permute-start | bytes 688136 | tf_op jit(solution)/shard_map/ppermute | solution.py:19
  (70 shorter events, 22.3 us)
Async XLA Ops:
  11.3 1.6 copy-start.7
  12.9 1.2 copy-start.8
  17.6 34.8 %collective-permute-start = (bf16[3,896,128]{1,2,0:T(8,128)(2,1)}, bf16[3,896,128]{1,2,0:T(8,128)(2,1)S(1)}, u32[]{:S(2)}, u32[]{:S(2)}) collective-permute-start(bf16[3,896,128]{1,2,0:T(8,128)(2,1)} %get-tuple-element.22), channel_id=1, source_target_pairs={{0,2},{2,4},{4,6},{6,0},{1,3},{3,5},{5,7},{7,1},{8,10},{10,12},{12... | collective-permute-start | bytes 2064392 | tf_op jit(solution)/shard_map/ppermute | solution.py:19
  19.5 32.9 %collective-permute-start.1 = (bf16[3,896,128]{1,2,0:T(8,128)(2,1)}, bf16[3,896,128]{1,2,0:T(8,128)(2,1)S(1)}, u32[]{:S(2)}, u32[]{:S(2)}) collective-permute-start(bf16[3,896,128]{1,2,0:T(8,128)(2,1)} %get-tuple-element.21), channel_id=1, source_target_pairs={{0,4},{2,6},{4,0},{6,2},{1,5},{3,7},{5,1},{7,3},{8,12},{10,14},{12... | collective-permute-start | bytes 2064392 | tf_op jit(solution)/shard_map/ppermute | solution.py:19
  21.4 33.2 %collective-permute-start.2 = (bf16[3,896,128]{1,2,0:T(8,128)(2,1)S(1)}, bf16[3,896,128]{1,2,0:T(8,128)(2,1)S(1)}, u32[]{:S(2)}, u32[]{:S(2)}) collective-permute-start(bf16[3,896,128]{1,2,0:T(8,128)(2,1)S(1)} %get-tuple-element.20), channel_id=1, source_target_pairs={{0,6},{2,0},{4,2},{6,4},{1,7},{3,1},{5,3},{7,5},{8,14},{10,8},{12,... | collective-permute-start | bytes 2064392 | tf_op jit(solution)/shard_map/ppermute | solution.py:19
  26.0 61.2 %all-to-all-start = ((bf16[64,4,1792]{2,1,0:T(4,128)(2,1)}), bf16[64,4,1792]{2,1,0:T(4,128)(2,1)}, u32[]{:S(2)}, u32[]{:S(2)}) async-start(bf16[64,4,1792]{2,1,0:T(4,128)(2,1)} %reshape.51), calls=%async_computation | async-start | bytes 1835008 | tf_op jit(solution)/shard_map/all_to_all | solution.py:59
  52.4 2.7 %copy-start.3 = (bf16[3,896,128]{1,2,0:T(8,128)(2,1)}, bf16[3,896,128]{1,2,0:T(8,128)(2,1)S(1)}, u32[]{:S(2)}) copy-start(bf16[3,896,128]{1,2,0:T(8,128)(2,1)S(1)} %collective-permute-done.1) | copy-start | bytes 2064388
  54.6 0.8 copy-start.1
  55.4 8.0 %collective-permute-start.3 = (bf16[4,3,896,128]{2,3,1,0:T(8,128)(2,1)S(1)}, bf16[4,3,896,128]{2,3,1,0:T(8,128)(2,1)S(1)}, u32[]{:S(2)}, u32[]{:S(2)}) collective-permute-start(bf16[4,3,896,128]{2,3,1,0:T(8,128)(2,1)S(1)} %pad_maximum_fusion.1), channel_id=1, source_target_pairs={{0,1},{1,0},{2,3},{3,2},{4,5},{5,4},{6,7},{7,6},{8,9},{9,8},{10,11... | collective-permute-start | bytes 8257544 | tf_op jit(solution)/shard_map/ppermute | solution.py:19
  88.8 1.4 copy-start
  90.5 2.4 %copy-start.4 = (bf16[3,896,128]{1,2,0:T(8,128)(2,1)S(1)}, bf16[3,896,128]{1,2,0:T(8,128)(2,1)}, u32[]{:S(2)}) copy-start(bf16[3,896,128]{1,2,0:T(8,128)(2,1)} %copy-done.3) | copy-start | bytes 2064388
  90.5 2.4 %copy-start.6 = (bf16[3,896,128]{1,2,0:T(8,128)(2,1)S(1)}, bf16[3,896,128]{1,2,0:T(8,128)(2,1)}, u32[]{:S(2)}) copy-start(bf16[3,896,128]{1,2,0:T(8,128)(2,1)} %get-tuple-element.17) | copy-start | bytes 2064388
  91.0 11.1 %collective-permute-start.4 = (bf16[3,256,256]{2,1,0:T(8,128)(2,1)S(1)}, bf16[3,256,256]{2,1,0:T(8,128)(2,1)S(1)}, u32[]{:S(2)}, u32[]{:S(2)}) collective-permute-start(bf16[3,256,256]{2,1,0:T(8,128)(2,1)S(1)} %pad_maximum_fusion.6), channel_id=1, source_target_pairs={{0,6},{2,0},{4,2},{6,4},{1,7},{3,1},{5,3},{7,5},{8,14},{10,8},{12,... | collective-permute-start | bytes 1179656 | tf_op jit(solution)/shard_map/ppermute | solution.py:19
  93.6 4.5 %copy-start.2 = (bf16[3,896,128]{1,2,0:T(8,128)(2,1)S(1)}, bf16[3,896,128]{1,2,0:T(8,128)(2,1)}, u32[]{:S(2)}) copy-start(bf16[3,896,128]{1,2,0:T(8,128)(2,1)} %copy-done.1) | copy-start | bytes 2064388
  93.6 4.5 %copy-start.5 = (bf16[3,896,128]{1,2,0:T(8,128)(2,1)S(1)}, bf16[3,896,128]{1,2,0:T(8,128)(2,1)}, u32[]{:S(2)}) copy-start(bf16[3,896,128]{1,2,0:T(8,128)(2,1)} %get-tuple-element.16) | copy-start | bytes 2064388
  94.0 10.0 %collective-permute-start.5 = (bf16[3,256,256]{2,1,0:T(8,128)(2,1)S(1)}, bf16[3,256,256]{2,1,0:T(8,128)(2,1)S(1)}, u32[]{:S(2)}, u32[]{:S(2)}) collective-permute-start(bf16[3,256,256]{2,1,0:T(8,128)(2,1)S(1)} %pad_maximum_fusion.7), channel_id=1, source_target_pairs={{0,4},{2,6},{4,0},{6,2},{1,5},{3,7},{5,1},{7,3},{8,12},{10,14},{12... | collective-permute-start | bytes 1179656 | tf_op jit(solution)/shard_map/ppermute | solution.py:19
  99.2 15.2 %collective-permute-start.6 = (bf16[3,256,256]{2,1,0:T(8,128)(2,1)S(1)}, bf16[3,256,256]{2,1,0:T(8,128)(2,1)S(1)}, u32[]{:S(2)}, u32[]{:S(2)}) collective-permute-start(bf16[3,256,256]{2,1,0:T(8,128)(2,1)S(1)} %pad_maximum_fusion.8), channel_id=1, source_target_pairs={{0,2},{2,4},{4,6},{6,0},{1,3},{3,5},{5,7},{7,1},{8,10},{10,12},{12... | collective-permute-start | bytes 1179656 | tf_op jit(solution)/shard_map/ppermute | solution.py:19
  115.0 15.7 %collective-permute-start.7 = (bf16[2,256,256]{2,1,0:T(8,128)(2,1)S(1)}, bf16[2,256,256]{2,1,0:T(8,128)(2,1)S(1)}, u32[]{:S(2)}, u32[]{:S(2)}) collective-permute-start(bf16[2,256,256]{2,1,0:T(8,128)(2,1)S(1)} %pad_maximum_fusion.9), channel_id=1, source_target_pairs={{0,2},{2,4},{4,6},{6,0},{1,3},{3,5},{5,7},{7,1},{8,10},{10,12},{12... | collective-permute-start | bytes 786440 | tf_op jit(solution)/shard_map/ppermute | solution.py:19
  116.9 10.6 %collective-permute-start.8 = (bf16[2,256,256]{2,1,0:T(8,128)(2,1)S(1)}, bf16[2,256,256]{2,1,0:T(8,128)(2,1)S(1)}, u32[]{:S(2)}, u32[]{:S(2)}) collective-permute-start(bf16[2,256,256]{2,1,0:T(8,128)(2,1)S(1)} %pad_maximum_fusion.9), channel_id=1, source_target_pairs={{0,4},{2,6},{4,0},{6,2},{1,5},{3,7},{5,1},{7,3},{8,12},{10,14},{12... | collective-permute-start | bytes 786440 | tf_op jit(solution)/shard_map/ppermute | solution.py:19
  120.9 9.2 %collective-permute-start.9 = (bf16[2,256,256]{2,1,0:T(8,128)(2,1)S(1)}, bf16[2,256,256]{2,1,0:T(8,128)(2,1)S(1)}, u32[]{:S(2)}, u32[]{:S(2)}) collective-permute-start(bf16[2,256,256]{2,1,0:T(8,128)(2,1)S(1)} %pad_maximum_fusion.9), channel_id=1, source_target_pairs={{0,6},{2,0},{4,2},{6,4},{1,7},{3,1},{5,3},{7,5},{8,14},{10,8},{12,... | collective-permute-start | bytes 786440 | tf_op jit(solution)/shard_map/ppermute | solution.py:19
  131.5 15.7 %copy-start.9 = (f32[128,2]{0,1:T(2,128)S(1)}, f32[128,2]{0,1:T(2,128)}, u32[]{:S(2)}) copy-start(f32[128,2]{0,1:T(2,128)} %param.10) | copy-start | bytes 3076
  132.4 41.3 %all-to-all-start.1 = ((bf16[64,4,896]{2,1,0:T(4,128)(2,1)}), bf16[64,4,896]{2,1,0:T(4,128)(2,1)S(1)}, u32[]{:S(2)}, u32[]{:S(2)}) async-start(bf16[64,4,896]{2,1,0:T(4,128)(2,1)} %reshape.53), calls=%async_computation.1 | async-start | bytes 917504 | tf_op jit(solution)/shard_map/all_to_all | solution.py:93
  174.2 7.9 %collective-permute-start.10 = (f32[448,128]{1,0:T(8,128)S(1)}, f32[448,128]{1,0:T(8,128)S(1)}, u32[]{:S(2)}, u32[]{:S(2)}) collective-permute-start(f32[448,128]{1,0:T(8,128)S(1)} %dynamic-slice_bitcast_fusion), channel_id=1, source_target_pairs={{0,1},{1,0},{2,3},{3,2},{4,5},{5,4},{6,7},{7,6},{8,9},{9,8},{10,11... | collective-permute-start | bytes 688136 | tf_op jit(solution)/shard_map/ppermute | solution.py:19

commit v2 on v1

v2 whole, which is shorter than its diff:
```python
import jax
import jax.numpy as jnp
from jax import lax
from jax.experimental import pallas as pl
from jax.experimental.pallas import tpu as pltpu
from jax.sharding import Mesh, PartitionSpec as P

N_Z, N_X, N_Y, N_C = 16, 4, 4, 2
GROUP = ("z", "x")
LOCAL = ("y", "c")
SLOTS = 4
BF16 = jnp.bfloat16
F32 = jnp.float32


def dot(left, right, left_dim, right_dim):
    return lax.dot_general(
        left, right, (((left_dim,), (right_dim,)), ((), ())), preferred_element_type=F32
    )


def shift(value, axis, step, size):
    return lax.ppermute(value, axis, [(i, (i + step) % size) for i in range(size)])


def iota(rows, columns, axis):
    return lax.broadcasted_iota(jnp.int32, (rows, columns), axis)


def ones_where(condition):
    return jnp.where(condition, 1.0, 0.0).astype(BF16)


def routing(ids_ref, experts):
    tokens = ids_ref.shape[1]
    expert = iota(experts, tokens, 0)
    first = ids_ref[0:1, :] == expert
    second = ids_ref[1:2, :] == expert
    named = ones_where(first | second)
    earlier = ones_where(iota(tokens, tokens, 0) < iota(tokens, tokens, 1))
    ranks = dot(named, earlier, 1, 0)
    return first, second, named, ranks.astype(BF16)


def dispatch_kernel(core_ref, ids_ref, both_ref, send_ref):
    chunk = 2 * SLOTS
    rows = send_ref.shape[0]
    experts, tokens = rows // chunk, ids_ref.shape[1]
    _, _, named, ranks = routing(ids_ref, experts)
    spread = ones_where(iota(rows, experts, 0) // chunk == iota(rows, experts, 1))
    spread_named = dot(spread, named, 1, 0)
    spread_ranks = dot(spread, ranks, 1, 0)
    place = iota(rows, tokens, 0) % chunk
    wanted = (place % SLOTS + SLOTS * core_ref[0]).astype(F32)
    chosen = (spread_named > 0.5) & (spread_ranks == wanted)
    select = jnp.concatenate(
        [ones_where(chosen & (place < SLOTS)), ones_where(chosen & (place >= SLOTS))], axis=1
    )
    send_ref[...] = dot(select, both_ref[...], 1, 1).astype(BF16)


def weight_kernel(core_ref, ids_ref, probs_ref, weight_ref):
    rows = weight_ref.shape[0]
    experts, tokens = rows // SLOTS, ids_ref.shape[1]
    first, second, named, ranks = routing(ids_ref, experts)
    probs = jnp.where(first, probs_ref[0:1, :], 0.0) + jnp.where(second, probs_ref[1:2, :], 0.0)
    high = probs.astype(BF16)
    low = (probs - high.astype(F32)).astype(BF16)
    spread = ones_where(iota(rows, experts, 0) // SLOTS == iota(rows, experts, 1))
    wanted = (iota(rows, tokens, 0) % SLOTS + SLOTS * core_ref[0]).astype(F32)
    chosen = (dot(spread, named, 1, 0) > 0.5) & (dot(spread, ranks, 1, 0) == wanted)
    parts = [jnp.where(chosen, dot(spread, part, 1, 0), 0.0).astype(BF16) for part in (high, low)]
    weight_ref[...] = jnp.concatenate(parts, axis=1)


def call(kernel, shape, arrays, flops):
    whole = pl.BlockSpec(memory_space=pltpu.VMEM)
    return pl.pallas_call(
        kernel,
        out_shape=jax.ShapeDtypeStruct(shape, BF16),
        in_specs=[pl.BlockSpec(memory_space=pltpu.SMEM)] + [whole] * (len(arrays) - 1),
        out_specs=whole,
        compiler_params=pltpu.CompilerParams(vmem_limit_bytes=24 * 1024 * 1024),
        cost_estimate=pl.CostEstimate(flops=flops, bytes_accessed=2 * shape[0] * shape[1], transcendentals=0),
    )(*arrays)


def shards(layer_input, out_grad, expert_ids, gate_probs, w_gate, w_up, w_down):
    groups = N_Z * N_X
    tokens, width = layer_input.shape
    rows = groups * SLOTS
    chip = N_C * width
    core = lax.axis_index("c")
    here = lax.axis_index("y")
    core_ref = core.astype(jnp.int32).reshape(1)

    own = jnp.concatenate([layer_input.T, out_grad.T], axis=1)
    both = lax.all_gather(own, "c", axis=0, tiled=True)
    send = call(
        dispatch_kernel, (2 * rows, chip), (core_ref, expert_ids.T, both), 4 * rows * chip * tokens
    ).reshape(groups, 2 * SLOTS, chip)
    weights = call(weight_kernel, (rows, 2 * tokens), (core_ref, expert_ids.T, gate_probs.T), rows * tokens * 256)

    send, w_gate, w_up, w_down = lax.optimization_barrier((send, w_gate, w_up, w_down))
    recv = lax.all_to_all(send, GROUP, split_axis=0, concat_axis=0, tiled=True).reshape(2 * rows, chip)

    mats = jnp.stack([w_gate[0], w_up[0], w_down[0].T])

    def part(step):
        return lax.dynamic_slice_in_dim(mats, chip * ((here + step) % N_Y), chip, axis=1)

    blocks = [part(0)] + [shift(part(d), "y", d, N_Y) for d in range(1, N_Y)]
    full = [jnp.concatenate([block, shift(block, "c", 1, N_C)], axis=2) for block in blocks]

    source = 2 * SLOTS * (iota(rows, 2 * rows, 0) // SLOTS) + iota(rows, 2 * rows, 0) % SLOTS
    place = iota(rows, 2 * rows, 1)
    rows_in = dot(ones_where(place == source), recv, 1, 0).astype(BF16)
    rows_grad = dot(ones_where(place == source + SLOTS), recv, 1, 0).astype(BF16)

    def partial(d):
        return jnp.stack(
            [dot(rows_in, full[d][0], 1, 0), dot(rows_in, full[d][1], 1, 0), dot(rows_grad, full[d][2], 1, 0)]
        )

    sums = partial(0)
    for d in (2, 1, 3):
        sums = sums + shift(partial(d).astype(BF16), "y", -d, N_Y).astype(F32)
    gate_act, up_act, hidden_grad = sums[0], sums[1], sums[2]
    sigmoid_gate = jax.nn.sigmoid(gate_act)
    gate_grad = hidden_grad * up_act * sigmoid_gate * (1.0 + gate_act * (1.0 - sigmoid_gate))
    up_grad = hidden_grad * gate_act * sigmoid_gate
    grads = jnp.stack([gate_grad.astype(BF16), up_grad.astype(BF16)])
    back = jnp.zeros((rows, chip), F32)
    for d in range(N_Y):
        theirs = shift(grads, "y", d, N_Y) if d else grads
        back = back + dot(theirs[0], full[d][0], 1, 1) + dot(theirs[1], full[d][1], 1, 1)

    returned = lax.all_to_all(
        back.astype(BF16).reshape(groups, SLOTS, chip), GROUP, split_axis=0, concat_axis=0, tiled=True
    ).reshape(rows, chip)
    mixed = dot(returned, weights, 0, 0)
    mixed = (mixed[:, :tokens] + mixed[:, tokens:]).reshape(N_C, width, tokens)
    mine = lax.dynamic_index_in_dim(mixed, core, 0, keepdims=False)
    sibling = lax.dynamic_index_in_dim(mixed, 1 - core, 0, keepdims=False)
    result = mine + shift(sibling, "c", 1, N_C)
    return result.astype(BF16).T


def solution(mesh):
    split = Mesh(mesh.devices.reshape(N_Z, N_X, N_Y, N_C), GROUP + LOCAL)
    placed = (
        P(GROUP, LOCAL),
        P(GROUP, LOCAL),
        P(GROUP, None),
        P(GROUP, None),
        P(GROUP, None, LOCAL),
        P(GROUP, None, LOCAL),
        P(GROUP, LOCAL, None),
    )
    return jax.shard_map(
        shards, mesh=split, in_specs=placed, out_specs=P(GROUP, LOCAL), check_vma=False
    )
```

time: 184 us -> 173 us (0.940)
  waiting for transfers between devices: 84.2 us -> 57.5 us
  starting transfers between devices: 66.6 us -> 81.1 us
  local copies, waits for them, and re-layouts: 9.55 us -> 5.92 us
  matrix products: 8.25 us -> 10.6 us
  Pallas kernels: 0 us -> 1.97 us
    all_to_all x2, waiting for transfers between devices: 48.7 us -> 26.5 us  [the longest x1 25.8 us: shards(): lax.all_to_all(back.astype(BF16).reshape(groups, SLOTS, chip), GROUP, spl...]
    ppermute x11 -> x14, starting transfers between devices: 36.3 us -> 52.5 us  [shift(): lax.ppermute(value, axis, [(i, (i + step) % size) for i in range(size)])]
    ppermute x11 -> x14, waiting for transfers between devices: 35.5 us -> 31 us  [shift(): lax.ppermute(value, axis, [(i, (i + step) % size) for i in range(size)])]
    reshape x4 -> x2, local copies, waits for them, and re-layouts: 3.8 us -> 0.99 us  [the longest x1 0.88 us: shards(): back.astype(BF16).reshape(groups, SLOTS, chip)]
    dot_general x22 -> x23, matrix products: 8.25 us -> 10.6 us  [dot(): lax.dot_general(left, right, (((left_dim,), (right_dim,)), ((), ())), pre...]
    unnamed x20 -> x21, local copies, waits for them, and re-layouts: 1.09 us -> 3.31 us
    pallas_call x0 -> x2, Pallas kernels: none -> 1.97 us  [call(): pl.pallas_call(kernel, out_shape=jax.ShapeDtypeStruct(shape, BF16), in_sp...]
  transfers between devices with their start and end apart: 13 -> 16, of which waited for: 10 -> 9; matrix products, arithmetic and copies ran while one was open for 4% -> 7% of each run, Pallas kernels for 0% -> 0%
where the time goes in v2:
time: 173 us; the launch traced here: 170 us
  starting transfers between devices  81.1 us (47%)
  waiting for transfers between devices  57.5 us (33%)
  matrix products  10.6 us (6%)
  blocking collectives  8.64 us (5%)
  local copies, waits for them, and re-layouts  5.92 us (3%)
  other arithmetic  3.64 us (2%)
  Pallas kernels  1.97 us (1%)
    ppermute x14, starting transfers between devices, shift(): lax.ppermute(value, axis, [(i, (i + step) % size) for i in range(size)])  52.5 us
    ppermute x14, waiting for transfers between devices, shift(): lax.ppermute(value, axis, [(i, (i + step) % size) for i in range(size)])  31 us
    all_to_all x1, waiting for transfers between devices, shards(): lax.all_to_all(back.astype(BF16).reshape(groups, SLOTS, chip), GROUP, spl...  25.8 us
    all_to_all x1, starting transfers between devices, shards(): lax.all_to_all(back.astype(BF16).reshape(groups, SLOTS, chip), GROUP, spl...  15.5 us
    all_to_all x1, starting transfers between devices, shards(): lax.all_to_all(send, GROUP, split_axis=0, concat_axis=0, tiled=True)  13.1 us
    dot_general x23, matrix products, dot(): lax.dot_general(left, right, (((left_dim,), (right_dim,)), ((), ())), pre...  10.6 us
    all_gather x1, blocking collectives, shards(): both = lax.all_gather(own, 'c', axis=0, tiled=True)  8.64 us
  transfers between devices with their start and end apart: 16, of which 9 were waited for; matrix products, arithmetic and copies ran while one was open for 7% of the time, Pallas kernels for 0%

profile of v2, /device:TPU:1, one launch (start us, length us, event | category | flops | bytes accessed | tf_op | source)
XLA Modules:
  0.0 170.0 jit_solution(2347608990551606036)
XLA Ops:
  1.0 8.6 %all_gather.3.both_ref = bf16[896,256]{1,0:T(8,128)(2,1)S(1)} all-gather(bf16[448,256]{1,0:T(8,128)(2,1)S(1)} %pad_maximum_fusion.6), channel_id=1, replica_groups=mesh['z'=16,'x'=4,'y'=4,'c'=2] {'c'}, dimensions={0}, use_global_device_ids=true | all-gather | bytes 688128 | tf_op jit(solution)/shard_map/all_gather | solution.py:98
  11.9 13.1 %all-to-all-start = ((bf16[64,8,896]{2,1,0:T(8,128)(2,1)}), bf16[64,8,896]{2,1,0:T(8,128)(2,1)}, u32[]{:S(2)}, u32[]{:S(2)}) async-start(bf16[64,8,896]{2,1,0:T(8,128)(2,1)} %bitcast.4), calls=%async_computation | async-start | bytes 1835008 | tf_op jit(solution)/shard_map/all_to_all | solution.py:105
  28.6 4.8 %collective-permute-start.1 = (bf16[3,896,128]{1,2,0:T(8,128)(2,1)S(1)}, bf16[3,896,128]{1,2,0:T(8,128)(2,1)S(1)}, u32[]{:S(2)}, u32[]{:S(2)}) collective-permute-start(bf16[3,896,128]{1,2,0:T(8,128)(2,1)S(1)} %get-tuple-element.13), channel_id=1, source_target_pairs={{0,4},{2,6},{4,0},{6,2},{1,5},{3,7},{5,1},{7,3},{8,12},{10,14},{12... | collective-permute-start | bytes 2064392 | tf_op jit(solution)/shard_map/ppermute | solution.py:23
  33.4 2.3 %collective-permute-start.4 = (bf16[3,896,128]{1,2,0:T(8,128)(2,1)S(1)}, bf16[3,896,128]{1,2,0:T(8,128)(2,1)S(1)}, u32[]{:S(2)}, u32[]{:S(2)}) collective-permute-start(bf16[3,896,128]{1,2,0:T(8,128)(2,1)S(1)} %get-tuple-element.15), channel_id=1, source_target_pairs={{0,2},{2,4},{4,6},{6,0},{1,3},{3,5},{5,7},{7,1},{8,10},{10,12},{12... | collective-permute-start | bytes 2064392 | tf_op jit(solution)/shard_map/ppermute | solution.py:23
  35.7 4.2 %collective-permute-start.7 = (bf16[3,896,128]{1,2,0:T(8,128)(2,1)S(1)}, bf16[3,896,128]{1,2,0:T(8,128)(2,1)S(1)}, u32[]{:S(2)}, u32[]{:S(2)}) collective-permute-start(bf16[3,896,128]{1,2,0:T(8,128)(2,1)S(1)} %get-tuple-element.14), channel_id=1, source_target_pairs={{0,6},{2,0},{4,2},{6,4},{1,7},{3,1},{5,3},{7,5},{8,14},{10,8},{12,... | collective-permute-start | bytes 2064392 | tf_op jit(solution)/shard_map/ppermute | solution.py:23
  39.9 3.4 %collective-permute-start = (bf16[3,896,128]{1,2,0:T(8,128)(2,1)S(1)}, bf16[3,896,128]{1,2,0:T(8,128)(2,1)S(1)}, u32[]{:S(2)}, u32[]{:S(2)}) collective-permute-start(bf16[3,896,128]{1,2,0:T(8,128)(2,1)S(1)} %get-tuple-element.16), channel_id=1, source_target_pairs={{0,1},{1,0},{2,3},{3,2},{4,5},{5,4},{6,7},{7,6},{8,9},{9,8},{10,11... | collective-permute-start | bytes 2064392 | tf_op jit(solution)/shard_map/ppermute | solution.py:23
  43.3 5.1 %collective-permute-done.1 = bf16[3,896,128]{1,2,0:T(8,128)(2,1)S(1)} collective-permute-done((bf16[3,896,128]{1,2,0:T(8,128)(2,1)S(1)}, bf16[3,896,128]{1,2,0:T(8,128)(2,1)S(1)}, u32[]{:S(2)}, u32[]{:S(2)}) %collective-permute-start.1) | collective-permute-done | bytes 688160 | tf_op jit(solution)/shard_map/ppermute | solution.py:23
  48.4 4.5 %collective-permute-start.2 = (bf16[3,896,128]{1,2,0:T(8,128)(2,1)S(1)}, bf16[3,896,128]{1,2,0:T(8,128)(2,1)S(1)}, u32[]{:S(2)}, u32[]{:S(2)}) collective-permute-start(bf16[3,896,128]{1,2,0:T(8,128)(2,1)S(1)} %collective-permute-done.1), channel_id=1, source_target_pairs={{0,1},{1,0},{2,3},{3,2},{4,5},{5,4},{6,7},{7,6},{8,9},{9,8},{10,11... | collective-permute-start | bytes 2064392 | tf_op jit(solution)/shard_map/ppermute | solution.py:23
  52.9 11.3 %collective-permute-done.4 = bf16[3,896,128]{1,2,0:T(8,128)(2,1)S(1)} collective-permute-done((bf16[3,896,128]{1,2,0:T(8,128)(2,1)S(1)}, bf16[3,896,128]{1,2,0:T(8,128)(2,1)S(1)}, u32[]{:S(2)}, u32[]{:S(2)}) %collective-permute-start.4) | collective-permute-done | bytes 688160 | tf_op jit(solution)/shard_map/ppermute | solution.py:23
  64.2 2.3 %collective-permute-start.5 = (bf16[3,896,128]{1,2,0:T(8,128)(2,1)S(1)}, bf16[3,896,128]{1,2,0:T(8,128)(2,1)S(1)}, u32[]{:S(2)}, u32[]{:S(2)}) collective-permute-start(bf16[3,896,128]{1,2,0:T(8,128)(2,1)S(1)} %collective-permute-done.4), channel_id=1, source_target_pairs={{0,1},{1,0},{2,3},{3,2},{4,5},{5,4},{6,7},{7,6},{8,9},{9,8},{10,11... | collective-permute-start | bytes 2064392 | tf_op jit(solution)/shard_map/ppermute | solution.py:23
  66.5 2.0 %collective-permute-start.8 = (bf16[3,896,128]{1,2,0:T(8,128)(2,1)S(1)}, bf16[3,896,128]{1,2,0:T(8,128)(2,1)S(1)}, u32[]{:S(2)}, u32[]{:S(2)}) collective-permute-start(bf16[3,896,128]{1,2,0:T(8,128)(2,1)S(1)} %collective-permute-done.7), channel_id=1, source_target_pairs={{0,1},{1,0},{2,3},{3,2},{4,5},{5,4},{6,7},{7,6},{8,9},{9,8},{10,11... | collective-permute-start | bytes 2064392 | tf_op jit(solution)/shard_map/ppermute | solution.py:23
  71.3 1.9 %convolution_convert_fusion.1 = bf16[256,896]{1,0:T(8,128)(2,1)S(1)} fusion(bf16[64,8,896]{2,1,0:T(8,128)(2,1)} %all-to-all-done, s32[256]{0:T(256)S(1)} %get-tuple-element.22, s32[256]{0:T(256)S(1)} %get-tuple-element.23, s32[256]{0:T(256)S(1)} %get-tuple-element.21, s32[256]{0:T(256)S(1)} %get-tuple-element.24, pred[256]{0:T(512)(128)(4,1)S(1)} %get-tuple-element.19, ...), kind=kOutput, calls=%fused_computation.14 | convolution fusion | flops 236027904 | bytes 1380864 | tf_op jit(solution)/shard_map/dot_general | solution.py:17
  77.7 4.8 %collective-permute-start.3 = (bf16[3,256,256]{2,1,0:T(8,128)(2,1)S(1)}, bf16[3,256,256]{2,1,0:T(8,128)(2,1)S(1)}, u32[]{:S(2)}, u32[]{:S(2)}) collective-permute-start(bf16[3,256,256]{2,1,0:T(8,128)(2,1)S(1)} %pad_maximum_fusion.2), channel_id=1, source_target_pairs={{0,4},{2,6},{4,0},{6,2},{1,5},{3,7},{5,1},{7,3},{8,12},{10,14},{12... | collective-permute-start | bytes 1179656 | tf_op jit(solution)/shard_map/ppermute | solution.py:23
  82.6 2.7 %collective-permute-start.6 = (bf16[3,256,256]{2,1,0:T(8,128)(2,1)S(1)}, bf16[3,256,256]{2,1,0:T(8,128)(2,1)S(1)}, u32[]{:S(2)}, u32[]{:S(2)}) collective-permute-start(bf16[3,256,256]{2,1,0:T(8,128)(2,1)S(1)} %pad_maximum_fusion.3), channel_id=1, source_target_pairs={{0,6},{2,0},{4,2},{6,4},{1,7},{3,1},{5,3},{7,5},{8,14},{10,8},{12,... | collective-permute-start | bytes 1179656 | tf_op jit(solution)/shard_map/ppermute | solution.py:23
  86.4 2.6 %collective-permute-start.9 = (bf16[3,256,256]{2,1,0:T(8,128)(2,1)S(1)}, bf16[3,256,256]{2,1,0:T(8,128)(2,1)S(1)}, u32[]{:S(2)}, u32[]{:S(2)}) collective-permute-start(bf16[3,256,256]{2,1,0:T(8,128)(2,1)S(1)} %pad_maximum_fusion.4), channel_id=1, source_target_pairs={{0,2},{2,4},{4,6},{6,0},{1,3},{3,5},{5,7},{7,1},{8,10},{10,12},{12... | collective-permute-start | bytes 1179656 | tf_op jit(solution)/shard_map/ppermute | solution.py:23
  90.0 7.9 %collective-permute-done.6 = bf16[3,256,256]{2,1,0:T(8,128)(2,1)S(1)} collective-permute-done((bf16[3,256,256]{2,1,0:T(8,128)(2,1)S(1)}, bf16[3,256,256]{2,1,0:T(8,128)(2,1)S(1)}, u32[]{:S(2)}, u32[]{:S(2)}) %collective-permute-start.6) | collective-permute-done | bytes 393248 | tf_op jit(solution)/shard_map/ppermute | solution.py:23
  98.2 4.0 %collective-permute-start.10 = (bf16[2,256,256]{2,1,0:T(8,128)(2,1)S(1)}, bf16[2,256,256]{2,1,0:T(8,128)(2,1)S(1)}, u32[]{:S(2)}, u32[]{:S(2)}) collective-permute-start(bf16[2,256,256]{2,1,0:T(8,128)(2,1)S(1)} %pad_maximum_fusion.5), channel_id=1, source_target_pairs={{0,2},{2,4},{4,6},{6,0},{1,3},{3,5},{5,7},{7,1},{8,10},{10,12},{12... | collective-permute-start | bytes 786440 | tf_op jit(solution)/shard_map/ppermute | solution.py:23
  102.2 4.5 %collective-permute-start.11 = (bf16[2,256,256]{2,1,0:T(8,128)(2,1)S(1)}, bf16[2,256,256]{2,1,0:T(8,128)(2,1)S(1)}, u32[]{:S(2)}, u32[]{:S(2)}) collective-permute-start(bf16[2,256,256]{2,1,0:T(8,128)(2,1)S(1)} %pad_maximum_fusion.5), channel_id=1, source_target_pairs={{0,4},{2,6},{4,0},{6,2},{1,5},{3,7},{5,1},{7,3},{8,12},{10,14},{12... | collective-permute-start | bytes 786440 | tf_op jit(solution)/shard_map/ppermute | solution.py:23
  106.6 3.3 %collective-permute-start.12 = (bf16[2,256,256]{2,1,0:T(8,128)(2,1)S(1)}, bf16[2,256,256]{2,1,0:T(8,128)(2,1)S(1)}, u32[]{:S(2)}, u32[]{:S(2)}) collective-permute-start(bf16[2,256,256]{2,1,0:T(8,128)(2,1)S(1)} %pad_maximum_fusion.5), channel_id=1, source_target_pairs={{0,6},{2,0},{4,2},{6,4},{1,7},{3,1},{5,3},{7,5},{8,14},{10,8},{12,... | collective-permute-start | bytes 786440 | tf_op jit(solution)/shard_map/ppermute | solution.py:23
  110.9 2.9 %collective-permute-done.11 = bf16[2,256,256]{2,1,0:T(8,128)(2,1)S(1)} collective-permute-done((bf16[2,256,256]{2,1,0:T(8,128)(2,1)S(1)}, bf16[2,256,256]{2,1,0:T(8,128)(2,1)S(1)}, u32[]{:S(2)}, u32[]{:S(2)}) %collective-permute-start.11) | collective-permute-done | bytes 262176 | tf_op jit(solution)/shard_map/ppermute | solution.py:23
  114.5 2.3 %collective-permute-done.12 = bf16[2,256,256]{2,1,0:T(8,128)(2,1)S(1)} collective-permute-done((bf16[2,256,256]{2,1,0:T(8,128)(2,1)S(1)}, bf16[2,256,256]{2,1,0:T(8,128)(2,1)S(1)}, u32[]{:S(2)}, u32[]{:S(2)}) %collective-permute-start.12) | collective-permute-done | bytes 262176 | tf_op jit(solution)/shard_map/ppermute | solution.py:23
  118.8 15.5 %all-to-all-start.1 = ((bf16[64,4,896]{2,1,0:T(4,128)(2,1)}), bf16[64,4,896]{2,1,0:T(4,128)(2,1)S(1)}, u32[]{:S(2)}, u32[]{:S(2)}) async-start(bf16[64,4,896]{2,1,0:T(4,128)(2,1)} %reshape.23), calls=%async_computation.1 | async-start | bytes 917504 | tf_op jit(solution)/shard_map/all_to_all | solution.py:138
  134.7 25.8 %all-to-all-done.1 = bf16[64,4,896]{2,1,0:T(4,128)(2,1)S(1)} async-done(((bf16[64,4,896]{2,1,0:T(4,128)(2,1)}), bf16[64,4,896]{2,1,0:T(4,128)(2,1)S(1)}, u32[]{:S(2)}, u32[]{:S(2)}) %all-to-all-start.1) | async-done | bytes 458784 | tf_op jit(solution)/shard_map/all_to_all | solution.py:138
  161.1 7.1 %collective-permute-start.13 = (f32[448,128]{1,0:T(8,128)S(1)}, f32[448,128]{1,0:T(8,128)S(1)}, u32[]{:S(2)}, u32[]{:S(2)}) collective-permute-start(f32[448,128]{1,0:T(8,128)S(1)} %dynamic-slice_bitcast_fusion), channel_id=1, source_target_pairs={{0,1},{1,0},{2,3},{3,2},{4,5},{5,4},{6,7},{7,6},{8,9},{9,8},{10,11... | collective-permute-start | bytes 688136 | tf_op jit(solution)/shard_map/ppermute | solution.py:23
  (77 shorter events, 22.3 us)
Async XLA Ops:
  10.3 14.8 %copy-start.7 = (bf16[1,3584,128]{2,1,0:T(8,128)(2,1)S(1)}, bf16[1,3584,128]{2,1,0:T(8,128)(2,1)}, u32[]{:S(2)}) copy-start(bf16[1,3584,128]{2,1,0:T(8,128)(2,1)} %param.11) | copy-start | bytes 2752516
  11.9 59.3 %all-to-all-start = ((bf16[64,8,896]{2,1,0:T(8,128)(2,1)}), bf16[64,8,896]{2,1,0:T(8,128)(2,1)}, u32[]{:S(2)}, u32[]{:S(2)}) async-start(bf16[64,8,896]{2,1,0:T(8,128)(2,1)} %bitcast.4), calls=%async_computation | async-start | bytes 1835008 | tf_op jit(solution)/shard_map/all_to_all | solution.py:105
  25.1 1.2 copy-start.8
  28.6 19.9 %collective-permute-start.1 = (bf16[3,896,128]{1,2,0:T(8,128)(2,1)S(1)}, bf16[3,896,128]{1,2,0:T(8,128)(2,1)S(1)}, u32[]{:S(2)}, u32[]{:S(2)}) collective-permute-start(bf16[3,896,128]{1,2,0:T(8,128)(2,1)S(1)} %get-tuple-element.13), channel_id=1, source_target_pairs={{0,4},{2,6},{4,0},{6,2},{1,5},{3,7},{5,1},{7,3},{8,12},{10,14},{12... | collective-permute-start | bytes 2064392 | tf_op jit(solution)/shard_map/ppermute | solution.py:23
  33.4 30.8 %collective-permute-start.4 = (bf16[3,896,128]{1,2,0:T(8,128)(2,1)S(1)}, bf16[3,896,128]{1,2,0:T(8,128)(2,1)S(1)}, u32[]{:S(2)}, u32[]{:S(2)}) collective-permute-start(bf16[3,896,128]{1,2,0:T(8,128)(2,1)S(1)} %get-tuple-element.15), channel_id=1, source_target_pairs={{0,2},{2,4},{4,6},{6,0},{1,3},{3,5},{5,7},{7,1},{8,10},{10,12},{12... | collective-permute-start | bytes 2064392 | tf_op jit(solution)/shard_map/ppermute | solution.py:23
  35.7 30.8 %collective-permute-start.7 = (bf16[3,896,128]{1,2,0:T(8,128)(2,1)S(1)}, bf16[3,896,128]{1,2,0:T(8,128)(2,1)S(1)}, u32[]{:S(2)}, u32[]{:S(2)}) collective-permute-start(bf16[3,896,128]{1,2,0:T(8,128)(2,1)S(1)} %get-tuple-element.14), channel_id=1, source_target_pairs={{0,6},{2,0},{4,2},{6,4},{1,7},{3,1},{5,3},{7,5},{8,14},{10,8},{12,... | collective-permute-start | bytes 2064392 | tf_op jit(solution)/shard_map/ppermute | solution.py:23
  39.9 49.0 %collective-permute-start = (bf16[3,896,128]{1,2,0:T(8,128)(2,1)S(1)}, bf16[3,896,128]{1,2,0:T(8,128)(2,1)S(1)}, u32[]{:S(2)}, u32[]{:S(2)}) collective-permute-start(bf16[3,896,128]{1,2,0:T(8,128)(2,1)S(1)} %get-tuple-element.16), channel_id=1, source_target_pairs={{0,1},{1,0},{2,3},{3,2},{4,5},{5,4},{6,7},{7,6},{8,9},{9,8},{10,11... | collective-permute-start | bytes 2064392 | tf_op jit(solution)/shard_map/ppermute | solution.py:23
  48.4 20.3 %collective-permute-start.2 = (bf16[3,896,128]{1,2,0:T(8,128)(2,1)S(1)}, bf16[3,896,128]{1,2,0:T(8,128)(2,1)S(1)}, u32[]{:S(2)}, u32[]{:S(2)}) collective-permute-start(bf16[3,896,128]{1,2,0:T(8,128)(2,1)S(1)} %collective-permute-done.1), channel_id=1, source_target_pairs={{0,1},{1,0},{2,3},{3,2},{4,5},{5,4},{6,7},{7,6},{8,9},{9,8},{10,11... | collective-permute-start | bytes 2064392 | tf_op jit(solution)/shard_map/ppermute | solution.py:23
  64.2 4.7 %collective-permute-start.5 = (bf16[3,896,128]{1,2,0:T(8,128)(2,1)S(1)}, bf16[3,896,128]{1,2,0:T(8,128)(2,1)S(1)}, u32[]{:S(2)}, u32[]{:S(2)}) collective-permute-start(bf16[3,896,128]{1,2,0:T(8,128)(2,1)S(1)} %collective-permute-done.4), channel_id=1, source_target_pairs={{0,1},{1,0},{2,3},{3,2},{4,5},{5,4},{6,7},{7,6},{8,9},{9,8},{10,11... | collective-permute-start | bytes 2064392 | tf_op jit(solution)/shard_map/ppermute | solution.py:23
  66.5 4.0 %collective-permute-start.8 = (bf16[3,896,128]{1,2,0:T(8,128)(2,1)S(1)}, bf16[3,896,128]{1,2,0:T(8,128)(2,1)S(1)}, u32[]{:S(2)}, u32[]{:S(2)}) collective-permute-start(bf16[3,896,128]{1,2,0:T(8,128)(2,1)S(1)} %collective-permute-done.7), channel_id=1, source_target_pairs={{0,1},{1,0},{2,3},{3,2},{4,5},{5,4},{6,7},{7,6},{8,9},{9,8},{10,11... | collective-permute-start | bytes 2064392 | tf_op jit(solution)/shard_map/ppermute | solution.py:23
  68.9 1.7 copy-start.5
  69.0 1.2 copy-start.3
  71.3 1.9 %copy-start.6 = (bf16[3,896,256]{1,2,0:T(8,128)(2,1)S(1)}, bf16[3,896,256]{1,2,0:T(8,128)(2,1)}, u32[]{:S(2)}) copy-start(bf16[3,896,256]{1,2,0:T(8,128)(2,1)} %copy-done.5) | copy-start | bytes 4128772
  73.2 1.3 copy-start.4
  77.7 12.3 %collective-permute-start.3 = (bf16[3,256,256]{2,1,0:T(8,128)(2,1)S(1)}, bf16[3,256,256]{2,1,0:T(8,128)(2,1)S(1)}, u32[]{:S(2)}, u32[]{:S(2)}) collective-permute-start(bf16[3,256,256]{2,1,0:T(8,128)(2,1)S(1)} %pad_maximum_fusion.2), channel_id=1, source_target_pairs={{0,4},{2,6},{4,0},{6,2},{1,5},{3,7},{5,1},{7,3},{8,12},{10,14},{12... | collective-permute-start | bytes 1179656 | tf_op jit(solution)/shard_map/ppermute | solution.py:23
  82.6 15.3 %collective-permute-start.6 = (bf16[3,256,256]{2,1,0:T(8,128)(2,1)S(1)}, bf16[3,256,256]{2,1,0:T(8,128)(2,1)S(1)}, u32[]{:S(2)}, u32[]{:S(2)}) collective-permute-start(bf16[3,256,256]{2,1,0:T(8,128)(2,1)S(1)} %pad_maximum_fusion.3), channel_id=1, source_target_pairs={{0,6},{2,0},{4,2},{6,4},{1,7},{3,1},{5,3},{7,5},{8,14},{10,8},{12,... | collective-permute-start | bytes 1179656 | tf_op jit(solution)/shard_map/ppermute | solution.py:23
  86.4 11.5 %collective-permute-start.9 = (bf16[3,256,256]{2,1,0:T(8,128)(2,1)S(1)}, bf16[3,256,256]{2,1,0:T(8,128)(2,1)S(1)}, u32[]{:S(2)}, u32[]{:S(2)}) collective-permute-start(bf16[3,256,256]{2,1,0:T(8,128)(2,1)S(1)} %pad_maximum_fusion.4), channel_id=1, source_target_pairs={{0,2},{2,4},{4,6},{6,0},{1,3},{3,5},{5,7},{7,1},{8,10},{10,12},{12... | collective-permute-start | bytes 1179656 | tf_op jit(solution)/shard_map/ppermute | solution.py:23
  98.2 12.1 %collective-permute-start.10 = (bf16[2,256,256]{2,1,0:T(8,128)(2,1)S(1)}, bf16[2,256,256]{2,1,0:T(8,128)(2,1)S(1)}, u32[]{:S(2)}, u32[]{:S(2)}) collective-permute-start(bf16[2,256,256]{2,1,0:T(8,128)(2,1)S(1)} %pad_maximum_fusion.5), channel_id=1, source_target_pairs={{0,2},{2,4},{4,6},{6,0},{1,3},{3,5},{5,7},{7,1},{8,10},{10,12},{12... | collective-permute-start | bytes 786440 | tf_op jit(solution)/shard_map/ppermute | solution.py:23
  102.2 11.7 %collective-permute-start.11 = (bf16[2,256,256]{2,1,0:T(8,128)(2,1)S(1)}, bf16[2,256,256]{2,1,0:T(8,128)(2,1)S(1)}, u32[]{:S(2)}, u32[]{:S(2)}) collective-permute-start(bf16[2,256,256]{2,1,0:T(8,128)(2,1)S(1)} %pad_maximum_fusion.5), channel_id=1, source_target_pairs={{0,4},{2,6},{4,0},{6,2},{1,5},{3,7},{5,1},{7,3},{8,12},{10,14},{12... | collective-permute-start | bytes 786440 | tf_op jit(solution)/shard_map/ppermute | solution.py:23
  106.6 10.2 %collective-permute-start.12 = (bf16[2,256,256]{2,1,0:T(8,128)(2,1)S(1)}, bf16[2,256,256]{2,1,0:T(8,128)(2,1)S(1)}, u32[]{:S(2)}, u32[]{:S(2)}) collective-permute-start(bf16[2,256,256]{2,1,0:T(8,128)(2,1)S(1)} %pad_maximum_fusion.5), channel_id=1, source_target_pairs={{0,6},{2,0},{4,2},{6,4},{1,7},{3,1},{5,3},{7,5},{8,14},{10,8},{12,... | collective-permute-start | bytes 786440 | tf_op jit(solution)/shard_map/ppermute | solution.py:23
  117.9 16.4 %copy-start.1 = (s32[128,2]{0,1:T(2,128)S(1)}, s32[128,2]{0,1:T(2,128)}, u32[]{:S(2)}) copy-start(s32[128,2]{0,1:T(2,128)} %param.9) | copy-start | bytes 3076
  117.9 16.4 %copy-start.2 = (f32[128,2]{0,1:T(2,128)S(1)}, f32[128,2]{0,1:T(2,128)}, u32[]{:S(2)}) copy-start(f32[128,2]{0,1:T(2,128)} %param.10) | copy-start | bytes 3076
  118.8 41.7 %all-to-all-start.1 = ((bf16[64,4,896]{2,1,0:T(4,128)(2,1)}), bf16[64,4,896]{2,1,0:T(4,128)(2,1)S(1)}, u32[]{:S(2)}, u32[]{:S(2)}) async-start(bf16[64,4,896]{2,1,0:T(4,128)(2,1)} %reshape.23), calls=%async_computation.1 | async-start | bytes 917504 | tf_op jit(solution)/shard_map/all_to_all | solution.py:138
  161.1 8.2 %collective-permute-start.13 = (f32[448,128]{1,0:T(8,128)S(1)}, f32[448,128]{1,0:T(8,128)S(1)}, u32[]{:S(2)}, u32[]{:S(2)}) collective-permute-start(f32[448,128]{1,0:T(8,128)S(1)} %dynamic-slice_bitcast_fusion), channel_id=1, source_target_pairs={{0,1},{1,0},{2,3},{3,2},{4,5},{5,4},{6,7},{7,6},{8,9},{9,8},{10,11... | collective-permute-start | bytes 688136 | tf_op jit(solution)/shard_map/ppermute | solution.py:23
  (1 other events, 0.7 us)

commit v3 on v2

--- a/solution.py
+++ b/solution.py
@@ -73,16 +73,70 @@
     weight_ref[...] = jnp.concatenate(parts, axis=1)
 
 
-def call(kernel, shape, arrays, flops):
-    whole = pl.BlockSpec(memory_space=pltpu.VMEM)
-    return pl.pallas_call(
+def activations(rows_in, rows_grad, own_ref, other_ref, part_ref):
+    for m, left in enumerate((rows_in, rows_in, rows_grad)):
+        right = jnp.concatenate([own_ref[m], other_ref[m]], axis=1)
+        part_ref[m] = dot(left, right, 1, 0).astype(part_ref.dtype)
+
+
+def first_kernel(recv_ref, own_ref, other_ref, in_ref, grad_ref, part_ref):
+    recv = recv_ref[...]
+    rows_in = recv[:, :SLOTS, :].reshape(in_ref.shape)
+    rows_grad = recv[:, SLOTS:, :].reshape(grad_ref.shape)
+    in_ref[...] = rows_in
+    grad_ref[...] = rows_grad
+    activations(rows_in, rows_grad, own_ref, other_ref, part_ref)
+
+
+def next_kernel(in_ref, grad_ref, own_ref, other_ref, part_ref):
+    activations(in_ref[...], grad_ref[...], own_ref, other_ref, part_ref)
+
+
+def hidden_kernel(first_ref, *refs):
+    *others, grads_ref = refs
+    gate_act, up_act, hidden_grad = (
+        first_ref[m] + sum(other[m].astype(F32) for other in others) for m in range(3)
+    )
+    sigmoid_gate = jax.nn.sigmoid(gate_act)
+    gate_grad = hidden_grad * up_act * sigmoid_gate * (1.0 + gate_act * (1.0 - sigmoid_gate))
+    up_grad = hidden_grad * gate_act * sigmoid_gate
+    for y in range(N_Y):
+        grads_ref[y, 0] = gate_grad.astype(BF16)
+        grads_ref[y, 1] = up_grad.astype(BF16)
+
+
+def back_kernel(here_ref, grads_ref, *refs):
+    weights, out_ref = refs[:-1], refs[-1]
+    total = None
+    for d in range(N_Y):
+        own, other = weights[2 * d], weights[2 * d + 1]
+        origin = lax.rem(here_ref[0] + N_Y - d, N_Y)
+        for m in range(2):
+            right = jnp.concatenate([own[m], other[m]], axis=1)
+            term = dot(grads_ref[origin, m], right, 1, 1)
+            total = term if total is None else total + term
+    out_ref[...] = total.reshape(out_ref.shape).astype(BF16)
+
+
+def call(kernel, shapes, arrays, flops, kind=BF16):
+    def place(array):
+        return pltpu.SMEM if array.shape == (1,) else pltpu.VMEM
+
+    size = 0
+    for shape in shapes:
+        length = 2
+        for dim in shape:
+            length *= dim
+        size += length
+    out = pl.pallas_call(
         kernel,
-        out_shape=jax.ShapeDtypeStruct(shape, BF16),
-        in_specs=[pl.BlockSpec(memory_space=pltpu.SMEM)] + [whole] * (len(arrays) - 1),
-        out_specs=whole,
+        out_shape=[jax.ShapeDtypeStruct(shape, kind) for shape in shapes],
+        in_specs=[pl.BlockSpec(memory_space=place(array)) for array in arrays],
+        out_specs=[pl.BlockSpec(memory_space=pltpu.VMEM)] * len(shapes),
         compiler_params=pltpu.CompilerParams(vmem_limit_bytes=24 * 1024 * 1024),
-        cost_estimate=pl.CostEstimate(flops=flops, bytes_accessed=2 * shape[0] * shape[1], transcendentals=0),
+        cost_estimate=pl.CostEstimate(flops=flops, bytes_accessed=size, transcendentals=0),
     )(*arrays)
+    return out if len(shapes) > 1 else out[0]
 
 
 def shards(layer_input, out_grad, expert_ids, gate_probs, w_gate, w_up, w_down):
@@ -97,12 +151,12 @@
     own = jnp.concatenate([layer_input.T, out_grad.T], axis=1)
     both = lax.all_gather(own, "c", axis=0, tiled=True)
     send = call(
-        dispatch_kernel, (2 * rows, chip), (core_ref, expert_ids.T, both), 4 * rows * chip * tokens
+        dispatch_kernel, [(2 * rows, chip)], (core_ref, expert_ids.T, both), 4 * rows * chip * tokens
     ).reshape(groups, 2 * SLOTS, chip)
-    weights = call(weight_kernel, (rows, 2 * tokens), (core_ref, expert_ids.T, gate_probs.T), rows * tokens * 256)
+    weights = call(weight_kernel, [(rows, 2 * tokens)], (core_ref, expert_ids.T, gate_probs.T), rows * tokens * 256)
 
     send, w_gate, w_up, w_down = lax.optimization_barrier((send, w_gate, w_up, w_down))
-    recv = lax.all_to_all(send, GROUP, split_axis=0, concat_axis=0, tiled=True).reshape(2 * rows, chip)
+    recv = lax.all_to_all(send, GROUP, split_axis=0, concat_axis=0, tiled=True)
 
     mats = jnp.stack([w_gate[0], w_up[0], w_down[0].T])
 
@@ -110,34 +164,26 @@
         return lax.dynamic_slice_in_dim(mats, chip * ((here + step) % N_Y), chip, axis=1)
 
     blocks = [part(0)] + [shift(part(d), "y", d, N_Y) for d in range(1, N_Y)]
-    full = [jnp.concatenate([block, shift(block, "c", 1, N_C)], axis=2) for block in blocks]
-
-    source = 2 * SLOTS * (iota(rows, 2 * rows, 0) // SLOTS) + iota(rows, 2 * rows, 0) % SLOTS
-    place = iota(rows, 2 * rows, 1)
-    rows_in = dot(ones_where(place == source), recv, 1, 0).astype(BF16)
-    rows_grad = dot(ones_where(place == source + SLOTS), recv, 1, 0).astype(BF16)
-
-    def partial(d):
-        return jnp.stack(
-            [dot(rows_in, full[d][0], 1, 0), dot(rows_in, full[d][1], 1, 0), dot(rows_grad, full[d][2], 1, 0)]
-        )
-
-    sums = partial(0)
-    for d in (2, 1, 3):
-        sums = sums + shift(partial(d).astype(BF16), "y", -d, N_Y).astype(F32)
-    gate_act, up_act, hidden_grad = sums[0], sums[1], sums[2]
-    sigmoid_gate = jax.nn.sigmoid(gate_act)
-    gate_grad = hidden_grad * up_act * sigmoid_gate * (1.0 + gate_act * (1.0 - sigmoid_gate))
-    up_grad = hidden_grad * gate_act * sigmoid_gate
-    grads = jnp.stack([gate_grad.astype(BF16), up_grad.astype(BF16)])
-    back = jnp.zeros((rows, chip), F32)
-    for d in range(N_Y):
-        theirs = shift(grads, "y", d, N_Y) if d else grads
-        back = back + dot(theirs[0], full[d][0], 1, 1) + dot(theirs[1], full[d][1], 1, 1)
-
-    returned = lax.all_to_all(
-        back.astype(BF16).reshape(groups, SLOTS, chip), GROUP, split_axis=0, concat_axis=0, tiled=True
-    ).reshape(rows, chip)
+    pieces = []
+    for block in blocks:
+        pieces += [block, shift(block, "c", 1, N_C)]
+
+    here_ref = here.astype(jnp.int32).reshape(1)
+    units = N_C * w_gate.shape[2]
+    product = 2 * rows * chip * units * N_Y
+    shape = (3, rows, units)
+    rows_in, rows_grad, part = call(
+        first_kernel, [(rows, chip), (rows, chip), shape], [recv] + pieces[4:6], 3 * product // N_Y
+    )
+    parts = [shift(part, "y", -2, N_Y)]
+    for d in (1, 3):
+        part = call(next_kernel, [shape], [rows_in, rows_grad] + pieces[2 * d : 2 * d + 2], 3 * product // N_Y)
+        parts.append(shift(part, "y", -d, N_Y))
+    part = call(next_kernel, [shape], [rows_in, rows_grad] + pieces[:2], 3 * product // N_Y, F32)
+    grads = call(hidden_kernel, [(N_Y, 2, rows, units)], [part] + parts, 40 * rows * units)
+    grads = lax.all_to_all(grads, "y", split_axis=0, concat_axis=0, tiled=True)
+    back = call(back_kernel, [(groups, SLOTS, chip)], [here_ref, grads] + pieces, 2 * product)
+    returned = lax.all_to_all(back, GROUP, split_axis=0, concat_axis=0, tiled=True).reshape(rows, chip)
     mixed = dot(returned, weights, 0, 0)
     mixed = (mixed[:, :tokens] + mixed[:, tokens:]).reshape(N_C, width, tokens)
     mine = lax.dynamic_index_in_dim(mixed, core, 0, keepdims=False)

time: 173 us -> 171 us (0.988); the launches traced: 170 us -> 170 us
  blocking collectives: 8.64 us -> 22.5 us
  matrix products: 10.6 us -> 0.34 us
  Pallas kernels: 1.97 us -> 11.9 us
  starting transfers between devices: 81.1 us -> 74.7 us
  waiting for transfers between devices: 57.5 us -> 53.1 us
  local copies, waits for them, and re-layouts: 5.92 us -> 3.57 us
    all_to_all x0 -> x1, blocking collectives: none -> 13.9 us  [shards(): grads = lax.all_to_all(grads, 'y', split_axis=0, concat_axis=0, tiled=True)]
    ppermute x14 -> x11, starting transfers between devices: 52.5 us -> 40.4 us  [shift(): lax.ppermute(value, axis, [(i, (i + step) % size) for i in range(size)])]
    dot_general x23 -> x1, matrix products: 10.6 us -> 0.34 us  [dot(): lax.dot_general(left, right, (((left_dim,), (right_dim,)), ((), ())), pre...]
    pallas_call x2 -> x8, Pallas kernels: 1.97 us -> 11.9 us  [call(): pl.pallas_call(kernel, out_shape=[jax.ShapeDtypeStruct(shape, kind) for s...]
    all_to_all x2, starting transfers between devices: 28.6 us -> 34.4 us  [the longest x1 21.4 us: shards(): lax.all_to_all(back, GROUP, split_axis=0, concat_axis=0, tiled=True)]
    ppermute x14 -> x11, waiting for transfers between devices: 31 us -> 28.2 us  [shift(): lax.ppermute(value, axis, [(i, (i + step) % size) for i in range(size)])]
  transfers between devices with their start and end apart: 16 -> 13, of which waited for: 9 -> 7; matrix products, arithmetic and copies ran while one was open for 7% -> 2% of each run, Pallas kernels for 0% -> 4%
where the time goes in v3:
time: 171 us; the launch traced here: 170 us
  starting transfers between devices  74.7 us (44%)
  waiting for transfers between devices  53.1 us (31%)
  blocking collectives  22.5 us (13%)
  Pallas kernels  11.9 us (7%)
  local copies, waits for them, and re-layouts  3.57 us (2%)
  other arithmetic  3.53 us (2%)
    ppermute x11, starting transfers between devices, shift(): lax.ppermute(value, axis, [(i, (i + step) % size) for i in range(size)])  40.4 us
    ppermute x11, waiting for transfers between devices, shift(): lax.ppermute(value, axis, [(i, (i + step) % size) for i in range(size)])  28.2 us
    all_to_all x1, waiting for transfers between devices, shards(): lax.all_to_all(back, GROUP, split_axis=0, concat_axis=0, tiled=True)  24.7 us
    all_to_all x1, starting transfers between devices, shards(): lax.all_to_all(back, GROUP, split_axis=0, concat_axis=0, tiled=True)  21.4 us
    all_to_all x1, blocking collectives, shards(): grads = lax.all_to_all(grads, 'y', split_axis=0, concat_axis=0, tiled=True)  13.9 us
    all_to_all x1, starting transfers between devices, shards(): recv = lax.all_to_all(send, GROUP, split_axis=0, concat_axis=0, tiled=True)  12.9 us
    pallas_call x8, Pallas kernels, call(): pl.pallas_call(kernel, out_shape=[jax.ShapeDtypeStruct(shape, kind) for s...  11.9 us
    all_gather x1, blocking collectives, shards(): both = lax.all_gather(own, 'c', axis=0, tiled=True)  8.64 us
  transfers between devices with their start and end apart: 13, of which 7 were waited for; matrix products, arithmetic and copies ran while one was open for 2% of the time, Pallas kernels for 4%

profile of v3, /device:TPU:1, one launch (start us, length us, event | category | flops | bytes accessed | tf_op | source)
XLA Modules:
  0.0 170.0 jit_solution(8807740562266336366)
XLA Ops:
  1.1 8.6 %all_gather.3.both_ref = bf16[896,256]{1,0:T(8,128)(2,1)S(1)} all-gather(bf16[448,256]{1,0:T(8,128)(2,1)S(1)} %pad_maximum_fusion.1), channel_id=1, replica_groups=mesh['z'=16,'x'=4,'y'=4,'c'=2] {'c'}, dimensions={0}, use_global_device_ids=true | all-gather | bytes 688128 | tf_op jit(solution)/shard_map/all_gather | solution.py:152
  12.0 12.9 %all-to-all-start = ((bf16[64,8,896]{2,1,0:T(8,128)(2,1)}), bf16[64,8,896]{2,1,0:T(8,128)(2,1)S(1)}, u32[]{:S(2)}, u32[]{:S(2)}) async-start(bf16[64,8,896]{2,1,0:T(8,128)(2,1)} %bitcast.5), calls=%async_computation | async-start | bytes 1835008 | tf_op jit(solution)/shard_map/all_to_all | solution.py:159
  25.6 1.8 %pad_maximum_fusion = bf16[3,3584,128]{2,1,0:T(8,128)(2,1)S(1)} fusion(bf16[1,3584,128]{2,1,0:T(8,128)(2,1)S(1)} %bitcast.28, bf16[1,3584,128]{2,1,0:T(8,128)(2,1)} %param.12, bf16[1,3584,128]{2,1,0:T(8,128)(2,1)} %param.11), kind=kLoop, calls=%fused_computation | loop fusion | flops 2752512 | bytes 5505024 | tf_op jit(solution)/shard_map/stack | solution.py:161
  27.6 4.8 %collective-permute-start = (bf16[3,896,128]{2,1,0:T(8,128)(2,1)S(1)}, bf16[3,896,128]{2,1,0:T(8,128)(2,1)S(1)}, u32[]{:S(2)}, u32[]{:S(2)}) collective-permute-start(bf16[3,896,128]{2,1,0:T(8,128)(2,1)S(1)} %get-tuple-element.22), channel_id=1, source_target_pairs={{0,4},{2,6},{4,0},{6,2},{1,5},{3,7},{5,1},{7,3},{8,12},{10,14},{12... | collective-permute-start | bytes 2064392 | tf_op jit(solution)/shard_map/ppermute | solution.py:23
  32.4 2.7 %collective-permute-start.7 = (bf16[3,896,128]{2,1,0:T(8,128)(2,1)S(1)}, bf16[3,896,128]{2,1,0:T(8,128)(2,1)S(1)}, u32[]{:S(2)}, u32[]{:S(2)}) collective-permute-start(bf16[3,896,128]{2,1,0:T(8,128)(2,1)S(1)} %get-tuple-element.19), channel_id=1, source_target_pairs={{0,6},{2,0},{4,2},{6,4},{1,7},{3,1},{5,3},{7,5},{8,14},{10,8},{12,... | collective-permute-start | bytes 2064392 | tf_op jit(solution)/shard_map/ppermute | solution.py:23
  35.1 2.6 %collective-permute-start.4 = (bf16[3,896,128]{2,1,0:T(8,128)(2,1)S(1)}, bf16[3,896,128]{2,1,0:T(8,128)(2,1)}, u32[]{:S(2)}, u32[]{:S(2)}) collective-permute-start(bf16[3,896,128]{2,1,0:T(8,128)(2,1)S(1)} %get-tuple-element.20), channel_id=1, source_target_pairs={{0,2},{2,4},{4,6},{6,0},{1,3},{3,5},{5,7},{7,1},{8,10},{10,12},{12... | collective-permute-start | bytes 2064392 | tf_op jit(solution)/shard_map/ppermute | solution.py:23
  37.7 9.6 %collective-permute-done.own_ref.refs_4_ = bf16[3,896,128]{2,1,0:T(8,128)(2,1)S(1)} collective-permute-done((bf16[3,896,128]{2,1,0:T(8,128)(2,1)S(1)}, bf16[3,896,128]{2,1,0:T(8,128)(2,1)S(1)}, u32[]{:S(2)}, u32[]{:S(2)}) %collective-permute-start) | collective-permute-done | bytes 688160 | tf_op jit(solution)/shard_map/ppermute | solution.py:23
  47.4 4.5 %collective-permute-start.1 = (bf16[3,896,128]{2,1,0:T(8,128)(2,1)S(1)}, bf16[3,896,128]{2,1,0:T(8,128)(2,1)S(1)}, u32[]{:S(2)}, u32[]{:S(2)}) collective-permute-start(bf16[3,896,128]{2,1,0:T(8,128)(2,1)S(1)} %collective-permute-done.own_ref.refs_4_), channel_id=1, source_target_pairs={{0,1},{1,0},{2,3},{3,2},{4,5},{5,4},{6,7},{7,6},{8,9},{9,8},{10,11... | collective-permute-start | bytes 2064392 | tf_op jit(solution)/shard_map/ppermute | solution.py:23
  51.9 10.6 %collective-permute-done.7.own_ref.refs_6_ = bf16[3,896,128]{2,1,0:T(8,128)(2,1)S(1)} collective-permute-done((bf16[3,896,128]{2,1,0:T(8,128)(2,1)S(1)}, bf16[3,896,128]{2,1,0:T(8,128)(2,1)S(1)}, u32[]{:S(2)}, u32[]{:S(2)}) %collective-permute-start.7) | collective-permute-done | bytes 688160 | tf_op jit(solution)/shard_map/ppermute | solution.py:23
  62.6 3.3 %collective-permute-start.8 = (bf16[3,896,128]{2,1,0:T(8,128)(2,1)S(1)}, bf16[3,896,128]{2,1,0:T(8,128)(2,1)}, u32[]{:S(2)}, u32[]{:S(2)}) collective-permute-start(bf16[3,896,128]{2,1,0:T(8,128)(2,1)S(1)} %collective-permute-done.7.own_ref.refs_6_), channel_id=1, source_target_pairs={{0,1},{1,0},{2,3},{3,2},{4,5},{5,4},{6,7},{7,6},{8,9},{9,8},{10,11... | collective-permute-start | bytes 2064392 | tf_op jit(solution)/shard_map/ppermute | solution.py:23
  65.9 1.9 %collective-permute-start.5 = (bf16[3,896,128]{2,1,0:T(8,128)(2,1)}, bf16[3,896,128]{2,1,0:T(8,128)(2,1)}, u32[]{:S(2)}, u32[]{:S(2)}) collective-permute-start(bf16[3,896,128]{2,1,0:T(8,128)(2,1)} %collective-permute-done.4.own_ref.refs_2_), channel_id=1, source_target_pairs={{0,1},{1,0},{2,3},{3,2},{4,5},{5,4},{6,7},{7,6},{8,9},{9,8},{10,11... | collective-permute-start | bytes 2064392 | tf_op jit(solution)/shard_map/ppermute | solution.py:23
  67.8 2.4 %collective-permute-start.2 = (bf16[3,896,128]{2,1,0:T(8,128)(2,1)S(1)}, bf16[3,896,128]{2,1,0:T(8,128)(2,1)}, u32[]{:S(2)}, u32[]{:S(2)}) collective-permute-start(bf16[3,896,128]{2,1,0:T(8,128)(2,1)S(1)} %get-tuple-element.21.own_ref.refs_0_), channel_id=1, source_target_pairs={{0,1},{1,0},{2,3},{3,2},{4,5},{5,4},{6,7},{7,6},{8,9},{9,8},{10,11... | collective-permute-start | bytes 2064392 | tf_op jit(solution)/shard_map/ppermute | solution.py:23
  73.0 1.7 shard_map.77
  74.7 3.2 %collective-permute-start.9 = (bf16[3,256,256]{2,1,0:T(8,128)(2,1)S(1)}, bf16[3,256,256]{2,1,0:T(8,128)(2,1)S(1)}, u32[]{:S(2)}, u32[]{:S(2)}) collective-permute-start(bf16[3,256,256]{2,1,0:T(8,128)(2,1)S(1)} %shard_map.77), channel_id=1, source_target_pairs={{0,2},{2,4},{4,6},{6,0},{1,3},{3,5},{5,7},{7,1},{8,10},{10,12},{12... | collective-permute-start | bytes 1179656 | tf_op jit(solution)/shard_map/ppermute | solution.py:23
  78.0 1.9 %shard_map.76 = bf16[3,256,256]{2,1,0:T(8,128)(2,1)S(1)} custom-call(bf16[256,896]{1,0:T(8,128)(2,1)S(1)} %get-tuple-element.16.in_ref, bf16[256,896]{1,0:T(8,128)(2,1)S(1)} %get-tuple-element.17.grad_ref, bf16[3,896,128]{2,1,0:T(8,128)(2,1)} %collective-permute-done.4.own_ref.refs_2_, bf16[3,896,128]{2,1,0:T(8,128)(2,1)} %collective-permute-done.5.other_ref.refs_3_), custom_call_target="tpu_custom_call" | custom-call | flops 352321536 | bytes 393216 | tf_op jit(solution)/shard_map/pallas_call | solution.py:131
  79.8 3.4 %collective-permute-start.6 = (bf16[3,256,256]{2,1,0:T(8,128)(2,1)S(1)}, bf16[3,256,256]{2,1,0:T(8,128)(2,1)S(1)}, u32[]{:S(2)}, u32[]{:S(2)}) collective-permute-start(bf16[3,256,256]{2,1,0:T(8,128)(2,1)S(1)} %shard_map.76), channel_id=1, source_target_pairs={{0,6},{2,0},{4,2},{6,4},{1,7},{3,1},{5,3},{7,5},{8,14},{10,8},{12,... | collective-permute-start | bytes 1179656 | tf_op jit(solution)/shard_map/ppermute | solution.py:23
  83.2 3.5 %collective-permute-start.3 = (bf16[3,256,256]{2,1,0:T(8,128)(2,1)S(1)}, bf16[3,256,256]{2,1,0:T(8,128)(2,1)S(1)}, u32[]{:S(2)}, u32[]{:S(2)}) collective-permute-start(bf16[3,256,256]{2,1,0:T(8,128)(2,1)S(1)} %get-tuple-element.18), channel_id=1, source_target_pairs={{0,4},{2,6},{4,0},{6,2},{1,5},{3,7},{5,1},{7,3},{8,12},{10,14},{12... | collective-permute-start | bytes 1179656 | tf_op jit(solution)/shard_map/ppermute | solution.py:23
  86.8 1.7 shard_map.75.first_ref
  88.7 6.6 %collective-permute-done.3.refs_0_ = bf16[3,256,256]{2,1,0:T(8,128)(2,1)S(1)} collective-permute-done((bf16[3,256,256]{2,1,0:T(8,128)(2,1)S(1)}, bf16[3,256,256]{2,1,0:T(8,128)(2,1)S(1)}, u32[]{:S(2)}, u32[]{:S(2)}) %collective-permute-start.3) | collective-permute-done | bytes 393248 | tf_op jit(solution)/shard_map/ppermute | solution.py:23
  95.5 13.9 %all_to_all.15.grads_ref = bf16[4,2,256,256]{3,2,1,0:T(8,128)(2,1)S(1)} all-to-all(bf16[4,2,256,256]{3,2,1,0:T(8,128)(2,1)S(1)} %shard_map.78), channel_id=1, replica_groups=mesh['z'=16,'x'=4,'y'=4,'c'=2] {'y'}, dimensions={0} | all-to-all | bytes 2097152 | tf_op jit(solution)/shard_map/all_to_all | solution.py:184
  109.4 3.8 %shard_map.79 = bf16[64,4,896]{2,1,0:T(4,128)(2,1)} custom-call(s32[1]{0:T(128)} %bitcast.here_ref, bf16[4,2,256,256]{3,2,1,0:T(8,128)(2,1)S(1)} %all_to_all.15.grads_ref, bf16[3,896,128]{2,1,0:T(8,128)(2,1)S(1)} %get-tuple-element.21.own_ref.refs_0_, bf16[3,896,128]{2,1,0:T(8,128)(2,1)} %collective-permute-done.2.other_ref.refs_1_, ...), custom_call_target="tpu_custom_call" | custom-call | flops 939524096 | bytes 458752 | tf_op jit(solution)/shard_map/pallas_call | solution.py:131
  113.2 21.4 %all-to-all-start.2 = ((bf16[64,4,896]{2,1,0:T(4,128)(2,1)}), bf16[64,4,896]{2,1,0:T(4,128)(2,1)S(1)}, u32[]{:S(2)}, u32[]{:S(2)}) async-start(bf16[64,4,896]{2,1,0:T(4,128)(2,1)} %shard_map.79), calls=%async_computation.2 | async-start | bytes 917504 | tf_op jit(solution)/shard_map/all_to_all | solution.py:186
  135.1 24.7 %all-to-all-done.2 = bf16[64,4,896]{2,1,0:T(4,128)(2,1)S(1)} async-done(((bf16[64,4,896]{2,1,0:T(4,128)(2,1)}), bf16[64,4,896]{2,1,0:T(4,128)(2,1)S(1)}, u32[]{:S(2)}, u32[]{:S(2)}) %all-to-all-start.2) | async-done | bytes 458784 | tf_op jit(solution)/shard_map/all_to_all | solution.py:186
  160.3 8.0 %collective-permute-start.10 = (f32[448,128]{1,0:T(8,128)S(1)}, f32[448,128]{1,0:T(8,128)S(1)}, u32[]{:S(2)}, u32[]{:S(2)}) collective-permute-start(f32[448,128]{1,0:T(8,128)S(1)} %dynamic-slice_bitcast_fusion), channel_id=1, source_target_pairs={{0,1},{1,0},{2,3},{3,2},{4,5},{5,4},{6,7},{7,6},{8,9},{9,8},{10,11... | collective-permute-start | bytes 688136 | tf_op jit(solution)/shard_map/ppermute | solution.py:23
  (35 shorter events, 10.0 us)
Async XLA Ops:
  0.0 25.0 %copy-start.6 = (bf16[1,128,3584]{2,1,0:T(8,128)(2,1)S(1)}, bf16[1,128,3584]{2,1,0:T(8,128)(2,1)}, u32[]{:S(2)}) copy-start(bf16[1,128,3584]{2,1,0:T(8,128)(2,1)} %param.13) | copy-start | bytes 2752516
  9.7 0.7 copy-start.3
  12.0 59.3 %all-to-all-start = ((bf16[64,8,896]{2,1,0:T(8,128)(2,1)}), bf16[64,8,896]{2,1,0:T(8,128)(2,1)S(1)}, u32[]{:S(2)}, u32[]{:S(2)}) async-start(bf16[64,8,896]{2,1,0:T(8,128)(2,1)} %bitcast.5), calls=%async_computation | async-start | bytes 1835008 | tf_op jit(solution)/shard_map/all_to_all | solution.py:159
  27.6 19.8 %collective-permute-start = (bf16[3,896,128]{2,1,0:T(8,128)(2,1)S(1)}, bf16[3,896,128]{2,1,0:T(8,128)(2,1)S(1)}, u32[]{:S(2)}, u32[]{:S(2)}) collective-permute-start(bf16[3,896,128]{2,1,0:T(8,128)(2,1)S(1)} %get-tuple-element.22), channel_id=1, source_target_pairs={{0,4},{2,6},{4,0},{6,2},{1,5},{3,7},{5,1},{7,3},{8,12},{10,14},{12... | collective-permute-start | bytes 2064392 | tf_op jit(solution)/shard_map/ppermute | solution.py:23
  32.4 30.1 %collective-permute-start.7 = (bf16[3,896,128]{2,1,0:T(8,128)(2,1)S(1)}, bf16[3,896,128]{2,1,0:T(8,128)(2,1)S(1)}, u32[]{:S(2)}, u32[]{:S(2)}) collective-permute-start(bf16[3,896,128]{2,1,0:T(8,128)(2,1)S(1)} %get-tuple-element.19), channel_id=1, source_target_pairs={{0,6},{2,0},{4,2},{6,4},{1,7},{3,1},{5,3},{7,5},{8,14},{10,8},{12,... | collective-permute-start | bytes 2064392 | tf_op jit(solution)/shard_map/ppermute | solution.py:23
  35.1 30.8 %collective-permute-start.4 = (bf16[3,896,128]{2,1,0:T(8,128)(2,1)S(1)}, bf16[3,896,128]{2,1,0:T(8,128)(2,1)}, u32[]{:S(2)}, u32[]{:S(2)}) collective-permute-start(bf16[3,896,128]{2,1,0:T(8,128)(2,1)S(1)} %get-tuple-element.20), channel_id=1, source_target_pairs={{0,2},{2,4},{4,6},{6,0},{1,3},{3,5},{5,7},{7,1},{8,10},{10,12},{12... | collective-permute-start | bytes 2064392 | tf_op jit(solution)/shard_map/ppermute | solution.py:23
  47.4 22.9 %collective-permute-start.1 = (bf16[3,896,128]{2,1,0:T(8,128)(2,1)S(1)}, bf16[3,896,128]{2,1,0:T(8,128)(2,1)S(1)}, u32[]{:S(2)}, u32[]{:S(2)}) collective-permute-start(bf16[3,896,128]{2,1,0:T(8,128)(2,1)S(1)} %collective-permute-done.own_ref.refs_4_), channel_id=1, source_target_pairs={{0,1},{1,0},{2,3},{3,2},{4,5},{5,4},{6,7},{7,6},{8,9},{9,8},{10,11... | collective-permute-start | bytes 2064392 | tf_op jit(solution)/shard_map/ppermute | solution.py:23
  62.6 10.5 %collective-permute-start.8 = (bf16[3,896,128]{2,1,0:T(8,128)(2,1)S(1)}, bf16[3,896,128]{2,1,0:T(8,128)(2,1)}, u32[]{:S(2)}, u32[]{:S(2)}) collective-permute-start(bf16[3,896,128]{2,1,0:T(8,128)(2,1)S(1)} %collective-permute-done.7.own_ref.refs_6_), channel_id=1, source_target_pairs={{0,1},{1,0},{2,3},{3,2},{4,5},{5,4},{6,7},{7,6},{8,9},{9,8},{10,11... | collective-permute-start | bytes 2064392 | tf_op jit(solution)/shard_map/ppermute | solution.py:23
  65.9 12.0 %collective-permute-start.5 = (bf16[3,896,128]{2,1,0:T(8,128)(2,1)}, bf16[3,896,128]{2,1,0:T(8,128)(2,1)}, u32[]{:S(2)}, u32[]{:S(2)}) collective-permute-start(bf16[3,896,128]{2,1,0:T(8,128)(2,1)} %collective-permute-done.4.own_ref.refs_2_), channel_id=1, source_target_pairs={{0,1},{1,0},{2,3},{3,2},{4,5},{5,4},{6,7},{7,6},{8,9},{9,8},{10,11... | collective-permute-start | bytes 2064392 | tf_op jit(solution)/shard_map/ppermute | solution.py:23
  67.8 18.9 %collective-permute-start.2 = (bf16[3,896,128]{2,1,0:T(8,128)(2,1)S(1)}, bf16[3,896,128]{2,1,0:T(8,128)(2,1)}, u32[]{:S(2)}, u32[]{:S(2)}) collective-permute-start(bf16[3,896,128]{2,1,0:T(8,128)(2,1)S(1)} %get-tuple-element.21.own_ref.refs_0_), channel_id=1, source_target_pairs={{0,1},{1,0},{2,3},{3,2},{4,5},{5,4},{6,7},{7,6},{8,9},{9,8},{10,11... | collective-permute-start | bytes 2064392 | tf_op jit(solution)/shard_map/ppermute | solution.py:23
  70.3 0.8 copy-start
  71.3 1.1 copy-start.1
  74.7 13.7 %collective-permute-start.9 = (bf16[3,256,256]{2,1,0:T(8,128)(2,1)S(1)}, bf16[3,256,256]{2,1,0:T(8,128)(2,1)S(1)}, u32[]{:S(2)}, u32[]{:S(2)}) collective-permute-start(bf16[3,256,256]{2,1,0:T(8,128)(2,1)S(1)} %shard_map.77), channel_id=1, source_target_pairs={{0,2},{2,4},{4,6},{6,0},{1,3},{3,5},{5,7},{7,1},{8,10},{10,12},{12... | collective-permute-start | bytes 1179656 | tf_op jit(solution)/shard_map/ppermute | solution.py:23
  79.8 8.8 %collective-permute-start.6 = (bf16[3,256,256]{2,1,0:T(8,128)(2,1)S(1)}, bf16[3,256,256]{2,1,0:T(8,128)(2,1)S(1)}, u32[]{:S(2)}, u32[]{:S(2)}) collective-permute-start(bf16[3,256,256]{2,1,0:T(8,128)(2,1)S(1)} %shard_map.76), channel_id=1, source_target_pairs={{0,6},{2,0},{4,2},{6,4},{1,7},{3,1},{5,3},{7,5},{8,14},{10,8},{12,... | collective-permute-start | bytes 1179656 | tf_op jit(solution)/shard_map/ppermute | solution.py:23
  83.2 12.0 %collective-permute-start.3 = (bf16[3,256,256]{2,1,0:T(8,128)(2,1)S(1)}, bf16[3,256,256]{2,1,0:T(8,128)(2,1)S(1)}, u32[]{:S(2)}, u32[]{:S(2)}) collective-permute-start(bf16[3,256,256]{2,1,0:T(8,128)(2,1)S(1)} %get-tuple-element.18), channel_id=1, source_target_pairs={{0,4},{2,6},{4,0},{6,2},{1,5},{3,7},{5,1},{7,3},{8,12},{10,14},{12... | collective-permute-start | bytes 1179656 | tf_op jit(solution)/shard_map/ppermute | solution.py:23
  88.4 21.0 %copy-start.2 = (bf16[3,896,128]{2,1,0:T(8,128)(2,1)S(1)}, bf16[3,896,128]{2,1,0:T(8,128)(2,1)}, u32[]{:S(2)}) copy-start(bf16[3,896,128]{2,1,0:T(8,128)(2,1)} %copy-done) | copy-start | bytes 2064388
  109.4 25.3 %copy-start.4 = (s32[128,2]{0,1:T(2,128)S(1)}, s32[128,2]{0,1:T(2,128)}, u32[]{:S(2)}) copy-start(s32[128,2]{0,1:T(2,128)} %param.9) | copy-start | bytes 3076
  109.4 25.3 %copy-start.5 = (f32[128,2]{0,1:T(2,128)S(1)}, f32[128,2]{0,1:T(2,128)}, u32[]{:S(2)}) copy-start(f32[128,2]{0,1:T(2,128)} %param.10) | copy-start | bytes 3076
  113.2 46.5 %all-to-all-start.2 = ((bf16[64,4,896]{2,1,0:T(4,128)(2,1)}), bf16[64,4,896]{2,1,0:T(4,128)(2,1)S(1)}, u32[]{:S(2)}, u32[]{:S(2)}) async-start(bf16[64,4,896]{2,1,0:T(4,128)(2,1)} %shard_map.79), calls=%async_computation.2 | async-start | bytes 917504 | tf_op jit(solution)/shard_map/all_to_all | solution.py:186
  160.3 9.1 %collective-permute-start.10 = (f32[448,128]{1,0:T(8,128)S(1)}, f32[448,128]{1,0:T(8,128)S(1)}, u32[]{:S(2)}, u32[]{:S(2)}) collective-permute-start(f32[448,128]{1,0:T(8,128)S(1)} %dynamic-slice_bitcast_fusion), channel_id=1, source_target_pairs={{0,1},{1,0},{2,3},{3,2},{4,5},{5,4},{6,7},{7,6},{8,9},{9,8},{10,11... | collective-permute-start | bytes 688136 | tf_op jit(solution)/shard_map/ppermute | solution.py:23

commit v4 on v3

--- a/solution.py
+++ b/solution.py
@@ -73,29 +73,35 @@
     weight_ref[...] = jnp.concatenate(parts, axis=1)
 
 
-def activations(rows_in, rows_grad, own_ref, other_ref, part_ref):
-    for m, left in enumerate((rows_in, rows_in, rows_grad)):
-        right = jnp.concatenate([own_ref[m], other_ref[m]], axis=1)
-        part_ref[m] = dot(left, right, 1, 0).astype(part_ref.dtype)
-
-
-def first_kernel(recv_ref, own_ref, other_ref, in_ref, grad_ref, part_ref):
-    recv = recv_ref[...]
-    rows_in = recv[:, :SLOTS, :].reshape(in_ref.shape)
-    rows_grad = recv[:, SLOTS:, :].reshape(grad_ref.shape)
-    in_ref[...] = rows_in
-    grad_ref[...] = rows_grad
-    activations(rows_in, rows_grad, own_ref, other_ref, part_ref)
-
-
-def next_kernel(in_ref, grad_ref, own_ref, other_ref, part_ref):
-    activations(in_ref[...], grad_ref[...], own_ref, other_ref, part_ref)
-
-
-def hidden_kernel(first_ref, *refs):
-    *others, grads_ref = refs
+def middle_kernel(here_ref, recv_ref, *refs):
+    pieces, part_ref = refs[: N_Y * N_C], refs[N_Y * N_C]
+    recv_held, held, part_held, recv_sem, sems, part_sems = refs[N_Y * N_C + 1 :]
+    recv_copy = pltpu.make_async_copy(recv_ref, recv_held, recv_sem)
+    recv_copy.start()
+    copies = [pltpu.make_async_copy(piece, held.at[i], sems.at[i]) for i, piece in enumerate(pieces)]
+    for copy in copies:
+        copy.start()
+    recv_copy.wait()
+    recv = recv_held[...]
+    rows_in = recv[:, :SLOTS, :].reshape(-1, recv.shape[2])
+    rows_grad = recv[:, SLOTS:, :].reshape(-1, recv.shape[2])
+    outs = []
+    for d in range(N_Y):
+        for i in range(N_C * d, N_C * (d + 1)):
+            copies[i].wait()
+        for m, left in enumerate((rows_in, rows_in, rows_grad)):
+            right = jnp.concatenate([held[N_C * d + c, m] for c in range(N_C)], axis=1)
+            part_held[d, m] = dot(left, right, 1, 0).astype(BF16)
+        target = lax.rem(here_ref[0] + N_Y - d, N_Y)
+        outs.append(pltpu.make_async_copy(part_held.at[d], part_ref.at[target], part_sems.at[d]))
+        outs[-1].start()
+    for out in outs:
+        out.wait()
+
+
+def hidden_kernel(parts_ref, grads_ref):
     gate_act, up_act, hidden_grad = (
-        first_ref[m] + sum(other[m].astype(F32) for other in others) for m in range(3)
+        sum(parts_ref[y, m].astype(F32) for y in range(N_Y)) for m in range(3)
     )
     sigmoid_gate = jax.nn.sigmoid(gate_act)
     gate_grad = hidden_grad * up_act * sigmoid_gate * (1.0 + gate_act * (1.0 - sigmoid_gate))
@@ -118,25 +124,47 @@
     out_ref[...] = total.reshape(out_ref.shape).astype(BF16)
 
 
-def call(kernel, shapes, arrays, flops, kind=BF16):
+def call(kernel, shape, arrays, flops):
     def place(array):
         return pltpu.SMEM if array.shape == (1,) else pltpu.VMEM
 
-    size = 0
-    for shape in shapes:
-        length = 2
-        for dim in shape:
-            length *= dim
-        size += length
-    out = pl.pallas_call(
+    size = 2
+    for dim in shape:
+        size *= dim
+    return pl.pallas_call(
         kernel,
-        out_shape=[jax.ShapeDtypeStruct(shape, kind) for shape in shapes],
+        out_shape=jax.ShapeDtypeStruct(shape, BF16),
         in_specs=[pl.BlockSpec(memory_space=place(array)) for array in arrays],
-        out_specs=[pl.BlockSpec(memory_space=pltpu.VMEM)] * len(shapes),
+        out_specs=pl.BlockSpec(memory_space=pltpu.VMEM),
         compiler_params=pltpu.CompilerParams(vmem_limit_bytes=24 * 1024 * 1024),
         cost_estimate=pl.CostEstimate(flops=flops, bytes_accessed=size, transcendentals=0),
     )(*arrays)
-    return out if len(shapes) > 1 else out[0]
+
+
+def call_middle(here_ref, recv, pieces):
+    groups, chunk, chip = recv.shape
+    mats, _, lanes = pieces[0].shape
+    rows, units = groups * chunk // 2, N_C * lanes
+    parts = (N_Y, mats, rows, units)
+    size = 2 * (recv.size + len(pieces) * pieces[0].size + N_Y * mats * rows * units)
+    return pl.pallas_call(
+        middle_kernel,
+        out_shape=jax.ShapeDtypeStruct(parts, BF16),
+        in_specs=[pl.BlockSpec(memory_space=pltpu.SMEM)] + [pl.BlockSpec(memory_space=pl.ANY)] * (1 + len(pieces)),
+        out_specs=pl.BlockSpec(memory_space=pl.ANY),
+        scratch_shapes=[
+            pltpu.VMEM(recv.shape, BF16),
+            pltpu.VMEM((len(pieces), mats, chip, lanes), BF16),
+            pltpu.VMEM(parts, BF16),
+            pltpu.SemaphoreType.DMA,
+            pltpu.SemaphoreType.DMA((len(pieces),)),
+            pltpu.SemaphoreType.DMA((N_Y,)),
+        ],
+        compiler_params=pltpu.CompilerParams(vmem_limit_bytes=60 * 1024 * 1024),
+        cost_estimate=pl.CostEstimate(
+            flops=2 * rows * chip * units * N_Y * mats, bytes_accessed=size, transcendentals=0
+        ),
+    )(here_ref, recv, *pieces)
 
 
 def shards(layer_input, out_grad, expert_ids, gate_probs, w_gate, w_up, w_down):
@@ -151,9 +179,9 @@
     own = jnp.concatenate([layer_input.T, out_grad.T], axis=1)
     both = lax.all_gather(own, "c", axis=0, tiled=True)
     send = call(
-        dispatch_kernel, [(2 * rows, chip)], (core_ref, expert_ids.T, both), 4 * rows * chip * tokens
+        dispatch_kernel, (2 * rows, chip), (core_ref, expert_ids.T, both), 4 * rows * chip * tokens
     ).reshape(groups, 2 * SLOTS, chip)
-    weights = call(weight_kernel, [(rows, 2 * tokens)], (core_ref, expert_ids.T, gate_probs.T), rows * tokens * 256)
+    weights = call(weight_kernel, (rows, 2 * tokens), (core_ref, expert_ids.T, gate_probs.T), rows * tokens * 256)
 
     send, w_gate, w_up, w_down = lax.optimization_barrier((send, w_gate, w_up, w_down))
     recv = lax.all_to_all(send, GROUP, split_axis=0, concat_axis=0, tiled=True)
@@ -164,31 +192,26 @@
         return lax.dynamic_slice_in_dim(mats, chip * ((here + step) % N_Y), chip, axis=1)
 
     blocks = [part(0)] + [shift(part(d), "y", d, N_Y) for d in range(1, N_Y)]
-    pieces = []
-    for block in blocks:
-        pieces += [block, shift(block, "c", 1, N_C)]
+    others = [shift(blocks[0], "c", 1, N_C)]
+    others[0], blocks[2] = lax.optimization_barrier((others[0], blocks[2]))
+    others += [shift(block, "c", 1, N_C) for block in blocks[1:]]
+    pieces = [piece for pair in zip(blocks, others) for piece in pair]
 
     here_ref = here.astype(jnp.int32).reshape(1)
     units = N_C * w_gate.shape[2]
     product = 2 * rows * chip * units * N_Y
-    shape = (3, rows, units)
-    rows_in, rows_grad, part = call(
-        first_kernel, [(rows, chip), (rows, chip), shape], [recv] + pieces[4:6], 3 * product // N_Y
-    )
-    parts = [shift(part, "y", -2, N_Y)]
-    for d in (1, 3):
-        part = call(next_kernel, [shape], [rows_in, rows_grad] + pieces[2 * d : 2 * d + 2], 3 * product // N_Y)
-        parts.append(shift(part, "y", -d, N_Y))
-    part = call(next_kernel, [shape], [rows_in, rows_grad] + pieces[:2], 3 * product // N_Y, F32)
-    grads = call(hidden_kernel, [(N_Y, 2, rows, units)], [part] + parts, 40 * rows * units)
+    parts = call_middle(here_ref, recv, pieces)
+    parts = lax.all_to_all(parts, "y", split_axis=0, concat_axis=0, tiled=True)
+    grads = call(hidden_kernel, (N_Y, 2, rows, units), [parts], 40 * rows * units)
     grads = lax.all_to_all(grads, "y", split_axis=0, concat_axis=0, tiled=True)
-    back = call(back_kernel, [(groups, SLOTS, chip)], [here_ref, grads] + pieces, 2 * product)
+    back = call(back_kernel, (groups, SLOTS, chip), [here_ref, grads] + pieces, 2 * product)
     returned = lax.all_to_all(back, GROUP, split_axis=0, concat_axis=0, tiled=True).reshape(rows, chip)
     mixed = dot(returned, weights, 0, 0)
     mixed = (mixed[:, :tokens] + mixed[:, tokens:]).reshape(N_C, width, tokens)
     mine = lax.dynamic_index_in_dim(mixed, core, 0, keepdims=False)
     sibling = lax.dynamic_index_in_dim(mixed, 1 - core, 0, keepdims=False)
-    result = mine + shift(sibling, "c", 1, N_C)
+    sent = lax.all_gather(sibling, "c", axis=0)
+    result = mine + lax.dynamic_index_in_dim(sent, 1 - core, 0, keepdims=False)
     return result.astype(BF16).T
 
 

time: 171 us -> 173 us (1.012)
  blocking collectives: 22.5 us -> 50.8 us
  starting transfers between devices: 74.7 us -> 55.5 us
  waiting for transfers between devices: 53.1 us -> 46.7 us
    all_to_all x0 -> x1, blocking collectives: none -> 21.4 us  [shards(): parts = lax.all_to_all(parts, 'y', split_axis=0, concat_axis=0, tiled=True)]
    ppermute x11 -> x7, starting transfers between devices: 40.4 us -> 21.2 us  [shift(): lax.ppermute(value, axis, [(i, (i + step) % size) for i in range(size)])]
    all_gather x0 -> x1, blocking collectives: none -> 7.61 us  [shards(): sent = lax.all_gather(sibling, 'c', axis=0)]
    ppermute x11 -> x7, waiting for transfers between devices: 28.2 us -> 21.6 us  [shift(): lax.ppermute(value, axis, [(i, (i + step) % size) for i in range(size)])]
    pallas_call x8 -> x5, Pallas kernels: 11.9 us -> 11.9 us  [the longest x1 6.45 us: call_middle(): pl.pallas_call(middle_kernel, out_shape=jax.ShapeDtypeStruct(parts, BF16)...]
  transfers between devices with their start and end apart: 13 -> 9, of which waited for: 7 -> 4; matrix products, arithmetic and copies ran while one was open for 2% -> 1% of each run, Pallas kernels for 4% -> 0%
where the time goes in v4:
time: 173 us; the launch traced here: 172 us
  starting transfers between devices  55.5 us (32%)
  blocking collectives  50.8 us (29%)
  waiting for transfers between devices  46.7 us (27%)
  Pallas kernels  11.9 us (7%)
  local copies, waits for them, and re-layouts  3.42 us (2%)
  other arithmetic  3.26 us (2%)
    all_to_all x1, waiting for transfers between devices, shards(): lax.all_to_all(back, GROUP, split_axis=0, concat_axis=0, tiled=True)  25.1 us
    ppermute x7, waiting for transfers between devices, shift(): lax.ppermute(value, axis, [(i, (i + step) % size) for i in range(size)])  21.6 us
    all_to_all x1, blocking collectives, shards(): parts = lax.all_to_all(parts, 'y', split_axis=0, concat_axis=0, tiled=True)  21.4 us
    ppermute x7, starting transfers between devices, shift(): lax.ppermute(value, axis, [(i, (i + step) % size) for i in range(size)])  21.2 us
    all_to_all x1, starting transfers between devices, shards(): lax.all_to_all(back, GROUP, split_axis=0, concat_axis=0, tiled=True)  21.2 us
    all_to_all x1, blocking collectives, shards(): grads = lax.all_to_all(grads, 'y', split_axis=0, concat_axis=0, tiled=True)  13.2 us
    all_to_all x1, starting transfers between devices, shards(): recv = lax.all_to_all(send, GROUP, split_axis=0, concat_axis=0, tiled=True)  13.1 us
    all_gather x1, blocking collectives, shards(): both = lax.all_gather(own, 'c', axis=0, tiled=True)  8.64 us
  transfers between devices with their start and end apart: 9, of which 4 were waited for; matrix products, arithmetic and copies ran while one was open for 1% of the time, Pallas kernels for 0%

profile of v4, /device:TPU:1, one launch (start us, length us, event | category | flops | bytes accessed | tf_op | source)
XLA Modules:
  0.0 172.3 jit_solution(15128478018210326697)
XLA Ops:
  0.0 1.1 pad_maximum_fusion.1
  1.1 8.6 %all_gather.7.both_ref = bf16[896,256]{1,0:T(8,128)(2,1)S(1)} all-gather(bf16[448,256]{1,0:T(8,128)(2,1)S(1)} %pad_maximum_fusion.1), channel_id=1, replica_groups=mesh['z'=16,'x'=4,'y'=4,'c'=2] {'c'}, dimensions={0}, use_global_device_ids=true | all-gather | bytes 688128 | tf_op jit(solution)/shard_map/all_gather | solution.py:180
  9.7 0.7 copy-done.14
  10.4 1.6 shard_map.73
  12.0 13.1 %all-to-all-start = ((bf16[64,8,896]{2,1,0:T(8,128)(2,1)}), bf16[64,8,896]{2,1,0:T(8,128)(2,1)}, u32[]{:S(2)}, u32[]{:S(2)}) async-start(bf16[64,8,896]{2,1,0:T(8,128)(2,1)} %bitcast.5), calls=%async_computation | async-start | bytes 1835008 | tf_op jit(solution)/shard_map/all_to_all | solution.py:187
  25.9 1.5 pad_maximum_fusion
  27.6 2.6 %collective-permute-start = (bf16[3,896,128]{2,1,0:T(8,128)(2,1)S(1)}, bf16[3,896,128]{2,1,0:T(8,128)(2,1)S(1)}, u32[]{:S(2)}, u32[]{:S(2)}) collective-permute-start(bf16[3,896,128]{2,1,0:T(8,128)(2,1)S(1)} %get-tuple-element.20.refs_0_), channel_id=1, source_target_pairs={{0,1},{1,0},{2,3},{3,2},{4,5},{5,4},{6,7},{7,6},{8,9},{9,8},{10,11... | collective-permute-start | bytes 2064392 | tf_op jit(solution)/shard_map/ppermute | solution.py:23
  30.2 4.8 %collective-permute-start.1 = (bf16[3,896,128]{2,1,0:T(8,128)(2,1)S(1)}, bf16[3,896,128]{2,1,0:T(8,128)(2,1)S(1)}, u32[]{:S(2)}, u32[]{:S(2)}) collective-permute-start(bf16[3,896,128]{2,1,0:T(8,128)(2,1)S(1)} %get-tuple-element.19), channel_id=1, source_target_pairs={{0,4},{2,6},{4,0},{6,2},{1,5},{3,7},{5,1},{7,3},{8,12},{10,14},{12... | collective-permute-start | bytes 2064392 | tf_op jit(solution)/shard_map/ppermute | solution.py:23
  35.0 2.3 %collective-permute-start.2 = (bf16[3,896,128]{2,1,0:T(8,128)(2,1)S(1)}, bf16[3,896,128]{2,1,0:T(8,128)(2,1)S(1)}, u32[]{:S(2)}, u32[]{:S(2)}) collective-permute-start(bf16[3,896,128]{2,1,0:T(8,128)(2,1)S(1)} %get-tuple-element.18), channel_id=1, source_target_pairs={{0,2},{2,4},{4,6},{6,0},{1,3},{3,5},{5,7},{7,1},{8,10},{10,12},{12... | collective-permute-start | bytes 2064392 | tf_op jit(solution)/shard_map/ppermute | solution.py:23
  37.3 4.2 %collective-permute-start.5 = (bf16[3,896,128]{2,1,0:T(8,128)(2,1)S(1)}, bf16[3,896,128]{2,1,0:T(8,128)(2,1)S(1)}, u32[]{:S(2)}, u32[]{:S(2)}) collective-permute-start(bf16[3,896,128]{2,1,0:T(8,128)(2,1)S(1)} %get-tuple-element.17), channel_id=1, source_target_pairs={{0,6},{2,0},{4,2},{6,4},{1,7},{3,1},{5,3},{7,5},{8,14},{10,8},{12,... | collective-permute-start | bytes 2064392 | tf_op jit(solution)/shard_map/ppermute | solution.py:23
  41.5 9.2 %collective-permute-done.1.refs_4_ = bf16[3,896,128]{2,1,0:T(8,128)(2,1)S(1)} collective-permute-done((bf16[3,896,128]{2,1,0:T(8,128)(2,1)S(1)}, bf16[3,896,128]{2,1,0:T(8,128)(2,1)S(1)}, u32[]{:S(2)}, u32[]{:S(2)}) %collective-permute-start.1) | collective-permute-done | bytes 688160 | tf_op jit(solution)/shard_map/ppermute | solution.py:23
  50.8 3.0 %collective-permute-start.4 = (bf16[3,896,128]{2,1,0:T(8,128)(2,1)S(1)}, bf16[3,896,128]{2,1,0:T(8,128)(2,1)S(1)}, u32[]{:S(2)}, u32[]{:S(2)}) collective-permute-start(bf16[3,896,128]{2,1,0:T(8,128)(2,1)S(1)} %collective-permute-done.1.refs_4_), channel_id=1, source_target_pairs={{0,1},{1,0},{2,3},{3,2},{4,5},{5,4},{6,7},{7,6},{8,9},{9,8},{10,11... | collective-permute-start | bytes 2064392 | tf_op jit(solution)/shard_map/ppermute | solution.py:23
  53.8 12.0 %collective-permute-done.2.refs_2_ = bf16[3,896,128]{2,1,0:T(8,128)(2,1)S(1)} collective-permute-done((bf16[3,896,128]{2,1,0:T(8,128)(2,1)S(1)}, bf16[3,896,128]{2,1,0:T(8,128)(2,1)S(1)}, u32[]{:S(2)}, u32[]{:S(2)}) %collective-permute-start.2) | collective-permute-done | bytes 688160 | tf_op jit(solution)/shard_map/ppermute | solution.py:23
  65.8 2.3 %collective-permute-start.3 = (bf16[3,896,128]{2,1,0:T(8,128)(2,1)S(1)}, bf16[3,896,128]{2,1,0:T(8,128)(2,1)S(1)}, u32[]{:S(2)}, u32[]{:S(2)}) collective-permute-start(bf16[3,896,128]{2,1,0:T(8,128)(2,1)S(1)} %collective-permute-done.2.refs_2_), channel_id=1, source_target_pairs={{0,1},{1,0},{2,3},{3,2},{4,5},{5,4},{6,7},{7,6},{8,9},{9,8},{10,11... | collective-permute-start | bytes 2064392 | tf_op jit(solution)/shard_map/ppermute | solution.py:23
  68.1 2.1 %collective-permute-start.6 = (bf16[3,896,128]{2,1,0:T(8,128)(2,1)S(1)}, bf16[3,896,128]{2,1,0:T(8,128)(2,1)}, u32[]{:S(2)}, u32[]{:S(2)}) collective-permute-start(bf16[3,896,128]{2,1,0:T(8,128)(2,1)S(1)} %collective-permute-done.5.refs_6_), channel_id=1, source_target_pairs={{0,1},{1,0},{2,3},{3,2},{4,5},{5,4},{6,7},{7,6},{8,9},{9,8},{10,11... | collective-permute-start | bytes 2064392 | tf_op jit(solution)/shard_map/ppermute | solution.py:23
  70.2 0.8 copy-done.10
  71.0 0.9 copy-done.12
  72.3 6.4 %shard_map.74 = bf16[4,3,256,256]{3,2,1,0:T(8,128)(2,1)} custom-call(s32[1]{0:T(128)} %bitcast.here_ref, bf16[64,8,896]{2,1,0:T(8,128)(2,1)} %all-to-all-done.recv_ref, bf16[3,896,128]{2,1,0:T(8,128)(2,1)} %copy-done, bf16[3,896,128]{2,1,0:T(8,128)(2,1)} %copy-done.2, bf16[3,896,128]{2,1,0:T(8,128)(2,1)} %copy-done.6, bf16[3,896,128]{2,1,0:T(8,128)(2,1)} %copy-done.12, ...), custom_call_target="tpu_custom_call" | custom-call | flops 1409286144 | bytes 7995392 | tf_op jit(solution)/shard_map/pallas_call | solution.py:150
  78.8 21.4 %all_to_all.20.parts_ref = bf16[4,3,256,256]{3,2,1,0:T(8,128)(2,1)S(1)} all-to-all(bf16[4,3,256,256]{3,2,1,0:T(8,128)(2,1)} %shard_map.74), channel_id=1, replica_groups=mesh['z'=16,'x'=4,'y'=4,'c'=2] {'y'}, dimensions={0} | all-to-all | bytes 3145728 | tf_op jit(solution)/shard_map/all_to_all | solution.py:204
  100.5 13.2 %all_to_all.21.grads_ref = bf16[4,2,256,256]{3,2,1,0:T(8,128)(2,1)S(1)} all-to-all(bf16[4,2,256,256]{3,2,1,0:T(8,128)(2,1)S(1)} %shard_map.75), channel_id=1, replica_groups=mesh['z'=16,'x'=4,'y'=4,'c'=2] {'y'}, dimensions={0} | all-to-all | bytes 2097152 | tf_op jit(solution)/shard_map/all_to_all | solution.py:206
  113.7 3.2 %shard_map.76 = bf16[64,4,896]{2,1,0:T(4,128)(2,1)} custom-call(s32[1]{0:T(128)} %bitcast.here_ref, bf16[4,2,256,256]{3,2,1,0:T(8,128)(2,1)S(1)} %all_to_all.21.grads_ref, bf16[3,896,128]{2,1,0:T(8,128)(2,1)S(1)} %copy-done.1, bf16[3,896,128]{2,1,0:T(8,128)(2,1)S(1)} %copy-done.3, bf16[3,896,128]{2,1,0:T(8,128)(2,1)S(1)} %copy-done.7, ...), custom_call_target="tpu_custom_call" | custom-call | flops 939524096 | bytes 458752 | tf_op jit(solution)/shard_map/pallas_call | solution.py:134
  116.9 21.2 %all-to-all-start.3 = ((bf16[64,4,896]{2,1,0:T(4,128)(2,1)}), bf16[64,4,896]{2,1,0:T(4,128)(2,1)S(1)}, u32[]{:S(2)}, u32[]{:S(2)}) async-start(bf16[64,4,896]{2,1,0:T(4,128)(2,1)} %shard_map.76), calls=%async_computation.3 | async-start | bytes 917504 | tf_op jit(solution)/shard_map/all_to_all | solution.py:208
  138.4 25.1 %all-to-all-done.3 = bf16[64,4,896]{2,1,0:T(4,128)(2,1)S(1)} async-done(((bf16[64,4,896]{2,1,0:T(4,128)(2,1)}), bf16[64,4,896]{2,1,0:T(4,128)(2,1)S(1)}, u32[]{:S(2)}, u32[]{:S(2)}) %all-to-all-start.3) | async-done | bytes 458784 | tf_op jit(solution)/shard_map/all_to_all | solution.py:208
  164.0 7.6 %all_gather.8 = f32[2,448,128]{2,1,0:T(8,128)S(1)} all-gather(f32[1,448,128]{2,1,0:T(8,128)S(1)} %constant_dynamic-slice_fusion), channel_id=1, replica_groups=mesh['z'=16,'x'=4,'y'=4,'c'=2] {'c'}, dimensions={0}, use_global_device_ids=true | all-gather | bytes 688128 | tf_op jit(solution)/shard_map/all_gather | solution.py:213
  (50 shorter events, 3.1 us)
Async XLA Ops:
  0.0 25.2 %copy-start.17 = (bf16[1,128,3584]{2,1,0:T(8,128)(2,1)S(1)}, bf16[1,128,3584]{2,1,0:T(8,128)(2,1)}, u32[]{:S(2)}) copy-start(bf16[1,128,3584]{2,1,0:T(8,128)(2,1)} %param.13) | copy-start | bytes 2752516
  10.4 15.5 %copy-start.18 = (bf16[1,3584,128]{2,1,0:T(8,128)(2,1)S(1)}, bf16[1,3584,128]{2,1,0:T(8,128)(2,1)}, u32[]{:S(2)}) copy-start(bf16[1,3584,128]{2,1,0:T(8,128)(2,1)} %param.12) | copy-start | bytes 2752516
  12.0 60.2 %all-to-all-start = ((bf16[64,8,896]{2,1,0:T(8,128)(2,1)}), bf16[64,8,896]{2,1,0:T(8,128)(2,1)}, u32[]{:S(2)}, u32[]{:S(2)}) async-start(bf16[64,8,896]{2,1,0:T(8,128)(2,1)} %bitcast.5), calls=%async_computation | async-start | bytes 1835008 | tf_op jit(solution)/shard_map/all_to_all | solution.py:187
  27.6 44.7 %copy-start = (bf16[3,896,128]{2,1,0:T(8,128)(2,1)}, bf16[3,896,128]{2,1,0:T(8,128)(2,1)S(1)}, u32[]{:S(2)}) copy-start(bf16[3,896,128]{2,1,0:T(8,128)(2,1)S(1)} %get-tuple-element.20.refs_0_) | copy-start | bytes 2064388
  27.6 13.9 %collective-permute-start = (bf16[3,896,128]{2,1,0:T(8,128)(2,1)S(1)}, bf16[3,896,128]{2,1,0:T(8,128)(2,1)S(1)}, u32[]{:S(2)}, u32[]{:S(2)}) collective-permute-start(bf16[3,896,128]{2,1,0:T(8,128)(2,1)S(1)} %get-tuple-element.20.refs_0_), channel_id=1, source_target_pairs={{0,1},{1,0},{2,3},{3,2},{4,5},{5,4},{6,7},{7,6},{8,9},{9,8},{10,11... | collective-permute-start | bytes 2064392 | tf_op jit(solution)/shard_map/ppermute | solution.py:23
  30.2 20.6 %collective-permute-start.1 = (bf16[3,896,128]{2,1,0:T(8,128)(2,1)S(1)}, bf16[3,896,128]{2,1,0:T(8,128)(2,1)S(1)}, u32[]{:S(2)}, u32[]{:S(2)}) collective-permute-start(bf16[3,896,128]{2,1,0:T(8,128)(2,1)S(1)} %get-tuple-element.19), channel_id=1, source_target_pairs={{0,4},{2,6},{4,0},{6,2},{1,5},{3,7},{5,1},{7,3},{8,12},{10,14},{12... | collective-permute-start | bytes 2064392 | tf_op jit(solution)/shard_map/ppermute | solution.py:23
  35.0 30.8 %collective-permute-start.2 = (bf16[3,896,128]{2,1,0:T(8,128)(2,1)S(1)}, bf16[3,896,128]{2,1,0:T(8,128)(2,1)S(1)}, u32[]{:S(2)}, u32[]{:S(2)}) collective-permute-start(bf16[3,896,128]{2,1,0:T(8,128)(2,1)S(1)} %get-tuple-element.18), channel_id=1, source_target_pairs={{0,2},{2,4},{4,6},{6,0},{1,3},{3,5},{5,7},{7,1},{8,10},{10,12},{12... | collective-permute-start | bytes 2064392 | tf_op jit(solution)/shard_map/ppermute | solution.py:23
  37.3 30.8 %collective-permute-start.5 = (bf16[3,896,128]{2,1,0:T(8,128)(2,1)S(1)}, bf16[3,896,128]{2,1,0:T(8,128)(2,1)S(1)}, u32[]{:S(2)}, u32[]{:S(2)}) collective-permute-start(bf16[3,896,128]{2,1,0:T(8,128)(2,1)S(1)} %get-tuple-element.17), channel_id=1, source_target_pairs={{0,6},{2,0},{4,2},{6,4},{1,7},{3,1},{5,3},{7,5},{8,14},{10,8},{12,... | collective-permute-start | bytes 2064392 | tf_op jit(solution)/shard_map/ppermute | solution.py:23
  41.5 30.8 %copy-start.2 = (bf16[3,896,128]{2,1,0:T(8,128)(2,1)}, bf16[3,896,128]{2,1,0:T(8,128)(2,1)S(1)}, u32[]{:S(2)}) copy-start(bf16[3,896,128]{2,1,0:T(8,128)(2,1)S(1)} %collective-permute-done.refs_1_) | copy-start | bytes 2064388
  50.8 21.5 %copy-start.4 = (bf16[3,896,128]{2,1,0:T(8,128)(2,1)}, bf16[3,896,128]{2,1,0:T(8,128)(2,1)S(1)}, u32[]{:S(2)}) copy-start(bf16[3,896,128]{2,1,0:T(8,128)(2,1)S(1)} %collective-permute-done.1.refs_4_) | copy-start | bytes 2064388
  50.8 19.4 %collective-permute-start.4 = (bf16[3,896,128]{2,1,0:T(8,128)(2,1)S(1)}, bf16[3,896,128]{2,1,0:T(8,128)(2,1)S(1)}, u32[]{:S(2)}, u32[]{:S(2)}) collective-permute-start(bf16[3,896,128]{2,1,0:T(8,128)(2,1)S(1)} %collective-permute-done.1.refs_4_), channel_id=1, source_target_pairs={{0,1},{1,0},{2,3},{3,2},{4,5},{5,4},{6,7},{7,6},{8,9},{9,8},{10,11... | collective-permute-start | bytes 2064392 | tf_op jit(solution)/shard_map/ppermute | solution.py:23
  65.8 6.5 %copy-start.6 = (bf16[3,896,128]{2,1,0:T(8,128)(2,1)}, bf16[3,896,128]{2,1,0:T(8,128)(2,1)S(1)}, u32[]{:S(2)}) copy-start(bf16[3,896,128]{2,1,0:T(8,128)(2,1)S(1)} %collective-permute-done.2.refs_2_) | copy-start | bytes 2064388
  65.8 4.4 %collective-permute-start.3 = (bf16[3,896,128]{2,1,0:T(8,128)(2,1)S(1)}, bf16[3,896,128]{2,1,0:T(8,128)(2,1)S(1)}, u32[]{:S(2)}, u32[]{:S(2)}) collective-permute-start(bf16[3,896,128]{2,1,0:T(8,128)(2,1)S(1)} %collective-permute-done.2.refs_2_), channel_id=1, source_target_pairs={{0,1},{1,0},{2,3},{3,2},{4,5},{5,4},{6,7},{7,6},{8,9},{9,8},{10,11... | collective-permute-start | bytes 2064392 | tf_op jit(solution)/shard_map/ppermute | solution.py:23
  68.1 4.2 %collective-permute-start.6 = (bf16[3,896,128]{2,1,0:T(8,128)(2,1)S(1)}, bf16[3,896,128]{2,1,0:T(8,128)(2,1)}, u32[]{:S(2)}, u32[]{:S(2)}) collective-permute-start(bf16[3,896,128]{2,1,0:T(8,128)(2,1)S(1)} %collective-permute-done.5.refs_6_), channel_id=1, source_target_pairs={{0,1},{1,0},{2,3},{3,2},{4,5},{5,4},{6,7},{7,6},{8,9},{9,8},{10,11... | collective-permute-start | bytes 2064392 | tf_op jit(solution)/shard_map/ppermute | solution.py:23
  78.8 34.9 %copy-start.13 = (bf16[3,896,128]{2,1,0:T(8,128)(2,1)S(1)}, bf16[3,896,128]{2,1,0:T(8,128)(2,1)}, u32[]{:S(2)}) copy-start(bf16[3,896,128]{2,1,0:T(8,128)(2,1)} %copy-done.12) | copy-start | bytes 2064388
  100.1 13.5 %copy-start.1 = (bf16[3,896,128]{2,1,0:T(8,128)(2,1)S(1)}, bf16[3,896,128]{2,1,0:T(8,128)(2,1)}, u32[]{:S(2)}) copy-start(bf16[3,896,128]{2,1,0:T(8,128)(2,1)} %copy-done) | copy-start | bytes 2064388
  100.1 13.5 %copy-start.3 = (bf16[3,896,128]{2,1,0:T(8,128)(2,1)S(1)}, bf16[3,896,128]{2,1,0:T(8,128)(2,1)}, u32[]{:S(2)}) copy-start(bf16[3,896,128]{2,1,0:T(8,128)(2,1)} %copy-done.2) | copy-start | bytes 2064388
  100.1 13.5 %copy-start.5 = (bf16[3,896,128]{2,1,0:T(8,128)(2,1)S(1)}, bf16[3,896,128]{2,1,0:T(8,128)(2,1)}, u32[]{:S(2)}) copy-start(bf16[3,896,128]{2,1,0:T(8,128)(2,1)} %copy-done.4) | copy-start | bytes 2064388
  100.1 13.5 %copy-start.7 = (bf16[3,896,128]{2,1,0:T(8,128)(2,1)S(1)}, bf16[3,896,128]{2,1,0:T(8,128)(2,1)}, u32[]{:S(2)}) copy-start(bf16[3,896,128]{2,1,0:T(8,128)(2,1)} %copy-done.6) | copy-start | bytes 2064388
  100.1 13.5 %copy-start.9 = (bf16[3,896,128]{2,1,0:T(8,128)(2,1)S(1)}, bf16[3,896,128]{2,1,0:T(8,128)(2,1)}, u32[]{:S(2)}) copy-start(bf16[3,896,128]{2,1,0:T(8,128)(2,1)} %copy-done.8) | copy-start | bytes 2064388
  100.2 13.5 %copy-start.11 = (bf16[3,896,128]{2,1,0:T(8,128)(2,1)S(1)}, bf16[3,896,128]{2,1,0:T(8,128)(2,1)}, u32[]{:S(2)}) copy-start(bf16[3,896,128]{2,1,0:T(8,128)(2,1)} %copy-done.10) | copy-start | bytes 2064388
  113.7 24.4 %copy-start.15 = (s32[128,2]{0,1:T(2,128)S(1)}, s32[128,2]{0,1:T(2,128)}, u32[]{:S(2)}) copy-start(s32[128,2]{0,1:T(2,128)} %param.9) | copy-start | bytes 3076
  113.7 24.4 %copy-start.16 = (f32[128,2]{0,1:T(2,128)S(1)}, f32[128,2]{0,1:T(2,128)}, u32[]{:S(2)}) copy-start(f32[128,2]{0,1:T(2,128)} %param.10) | copy-start | bytes 3076
  116.9 46.6 %all-to-all-start.3 = ((bf16[64,4,896]{2,1,0:T(4,128)(2,1)}), bf16[64,4,896]{2,1,0:T(4,128)(2,1)S(1)}, u32[]{:S(2)}, u32[]{:S(2)}) async-start(bf16[64,4,896]{2,1,0:T(4,128)(2,1)} %shard_map.76), calls=%async_computation.3 | async-start | bytes 917504 | tf_op jit(solution)/shard_map/all_to_all | solution.py:208
  (4 other events, 6.6 us)

commit v5 on v3

--- a/solution.py
+++ b/solution.py
@@ -42,21 +42,30 @@
     return first, second, named, ranks.astype(BF16)
 
 
-def dispatch_kernel(core_ref, ids_ref, both_ref, send_ref):
+def select_kernel(core_ref, ids_ref, in_ref, grad_ref, own_ref, select_ref, ids_held, sems):
+    tokens = ids_ref.shape[1]
+    copies = [
+        pltpu.make_async_copy(ids_ref, ids_held, sems.at[0]),
+        pltpu.make_async_copy(in_ref, own_ref.at[:, pl.ds(0, tokens)], sems.at[1]),
+        pltpu.make_async_copy(grad_ref, own_ref.at[:, pl.ds(tokens, tokens)], sems.at[2]),
+    ]
+    for copy in copies:
+        copy.start()
     chunk = 2 * SLOTS
-    rows = send_ref.shape[0]
-    experts, tokens = rows // chunk, ids_ref.shape[1]
-    _, _, named, ranks = routing(ids_ref, experts)
+    rows = select_ref.shape[0]
+    experts = rows // chunk
+    copies[0].wait()
+    _, _, named, ranks = routing(ids_held, experts)
     spread = ones_where(iota(rows, experts, 0) // chunk == iota(rows, experts, 1))
     spread_named = dot(spread, named, 1, 0)
     spread_ranks = dot(spread, ranks, 1, 0)
     place = iota(rows, tokens, 0) % chunk
     wanted = (place % SLOTS + SLOTS * core_ref[0]).astype(F32)
     chosen = (spread_named > 0.5) & (spread_ranks == wanted)
-    select = jnp.concatenate(
-        [ones_where(chosen & (place < SLOTS)), ones_where(chosen & (place >= SLOTS))], axis=1
-    )
-    send_ref[...] = dot(select, both_ref[...], 1, 1).astype(BF16)
+    select_ref[:, :tokens] = ones_where(chosen & (place < SLOTS))
+    select_ref[:, tokens:] = ones_where(chosen & (place >= SLOTS))
+    copies[1].wait()
+    copies[2].wait()
 
 
 def weight_kernel(core_ref, ids_ref, probs_ref, weight_ref):
@@ -73,29 +82,34 @@
     weight_ref[...] = jnp.concatenate(parts, axis=1)
 
 
-def activations(rows_in, rows_grad, own_ref, other_ref, part_ref):
-    for m, left in enumerate((rows_in, rows_in, rows_grad)):
-        right = jnp.concatenate([own_ref[m], other_ref[m]], axis=1)
-        part_ref[m] = dot(left, right, 1, 0).astype(part_ref.dtype)
-
-
-def first_kernel(recv_ref, own_ref, other_ref, in_ref, grad_ref, part_ref):
+def units_of(block, other, m):
+    return jnp.concatenate([block[m], other[m]], axis=1)
+
+
+def first_kernel(recv_ref, block_ref, other_ref, in_ref, grad_ref, part_ref):
     recv = recv_ref[...]
     rows_in = recv[:, :SLOTS, :].reshape(in_ref.shape)
     rows_grad = recv[:, SLOTS:, :].reshape(grad_ref.shape)
     in_ref[...] = rows_in
     grad_ref[...] = rows_grad
-    activations(rows_in, rows_grad, own_ref, other_ref, part_ref)
-
-
-def next_kernel(in_ref, grad_ref, own_ref, other_ref, part_ref):
-    activations(in_ref[...], grad_ref[...], own_ref, other_ref, part_ref)
-
-
-def hidden_kernel(first_ref, *refs):
-    *others, grads_ref = refs
+    for m, left in enumerate((rows_in, rows_in, rows_grad)):
+        part_ref[m] = dot(left, units_of(block_ref, other_ref, m), 1, 0).astype(BF16)
+
+
+def next_kernel(in_ref, grad_ref, block_ref, other_ref, part_ref):
+    for m, left in enumerate((in_ref, in_ref, grad_ref)):
+        part_ref[m] = dot(left[...], units_of(block_ref, other_ref, m), 1, 0).astype(BF16)
+
+
+def own_kernel(in_ref, grad_ref, block_ref, other_ref, arrived_ref, part_ref):
+    for m, left in enumerate((in_ref, in_ref, grad_ref)):
+        part = dot(left[...], units_of(block_ref, other_ref, m), 1, 0)
+        part_ref[m] = part + arrived_ref[m].astype(F32)
+
+
+def hidden_kernel(own_ref, next_ref, last_ref, grads_ref):
     gate_act, up_act, hidden_grad = (
-        first_ref[m] + sum(other[m].astype(F32) for other in others) for m in range(3)
+        own_ref[m] + next_ref[m].astype(F32) + last_ref[m].astype(F32) for m in range(3)
     )
     sigmoid_gate = jax.nn.sigmoid(gate_act)
     gate_grad = hidden_grad * up_act * sigmoid_gate * (1.0 + gate_act * (1.0 - sigmoid_gate))
@@ -106,14 +120,12 @@
 
 
 def back_kernel(here_ref, grads_ref, *refs):
-    weights, out_ref = refs[:-1], refs[-1]
+    blocks, others, out_ref = refs[:N_Y], refs[N_Y:-1], refs[-1]
     total = None
     for d in range(N_Y):
-        own, other = weights[2 * d], weights[2 * d + 1]
         origin = lax.rem(here_ref[0] + N_Y - d, N_Y)
         for m in range(2):
-            right = jnp.concatenate([own[m], other[m]], axis=1)
-            term = dot(grads_ref[origin, m], right, 1, 1)
+            term = dot(grads_ref[origin, m], units_of(blocks[d], others[d], m), 1, 1)
             total = term if total is None else total + term
     out_ref[...] = total.reshape(out_ref.shape).astype(BF16)
 
@@ -139,6 +151,24 @@
     return out if len(shapes) > 1 else out[0]
 
 
+def call_select(core_ref, ids, layer_input, out_grad, rows):
+    width, tokens = layer_input.shape
+    return pl.pallas_call(
+        select_kernel,
+        out_shape=[
+            jax.ShapeDtypeStruct((width, 2 * tokens), BF16),
+            jax.ShapeDtypeStruct((rows, 2 * tokens), BF16),
+        ],
+        in_specs=[pl.BlockSpec(memory_space=pltpu.SMEM)] + [pl.BlockSpec(memory_space=pl.ANY)] * 3,
+        out_specs=[pl.BlockSpec(memory_space=pltpu.VMEM)] * 2,
+        scratch_shapes=[pltpu.VMEM(ids.shape, jnp.int32), pltpu.SemaphoreType.DMA((3,))],
+        compiler_params=pltpu.CompilerParams(vmem_limit_bytes=60 * 1024 * 1024),
+        cost_estimate=pl.CostEstimate(
+            flops=rows * tokens * 300, bytes_accessed=4 * tokens * (2 * width + rows), transcendentals=0
+        ),
+    )(core_ref, ids, layer_input, out_grad)
+
+
 def shards(layer_input, out_grad, expert_ids, gate_probs, w_gate, w_up, w_down):
     groups = N_Z * N_X
     tokens, width = layer_input.shape
@@ -148,11 +178,9 @@
     here = lax.axis_index("y")
     core_ref = core.astype(jnp.int32).reshape(1)
 
-    own = jnp.concatenate([layer_input.T, out_grad.T], axis=1)
+    own, select = call_select(core_ref, expert_ids.T, layer_input.T, out_grad.T, 2 * rows)
     both = lax.all_gather(own, "c", axis=0, tiled=True)
-    send = call(
-        dispatch_kernel, [(2 * rows, chip)], (core_ref, expert_ids.T, both), 4 * rows * chip * tokens
-    ).reshape(groups, 2 * SLOTS, chip)
+    send = dot(select, both, 1, 1).astype(BF16).reshape(groups, 2 * SLOTS, chip)
     weights = call(weight_kernel, [(rows, 2 * tokens)], (core_ref, expert_ids.T, gate_probs.T), rows * tokens * 256)
 
     send, w_gate, w_up, w_down = lax.optimization_barrier((send, w_gate, w_up, w_down))
@@ -164,31 +192,33 @@
         return lax.dynamic_slice_in_dim(mats, chip * ((here + step) % N_Y), chip, axis=1)
 
     blocks = [part(0)] + [shift(part(d), "y", d, N_Y) for d in range(1, N_Y)]
-    pieces = []
-    for block in blocks:
-        pieces += [block, shift(block, "c", 1, N_C)]
+    other_0, other_1, other_2, other_3 = (shift(block, "c", 1, N_C) for block in blocks)
 
     here_ref = here.astype(jnp.int32).reshape(1)
     units = N_C * w_gate.shape[2]
-    product = 2 * rows * chip * units * N_Y
     shape = (3, rows, units)
-    rows_in, rows_grad, part = call(
-        first_kernel, [(rows, chip), (rows, chip), shape], [recv] + pieces[4:6], 3 * product // N_Y
-    )
-    parts = [shift(part, "y", -2, N_Y)]
-    for d in (1, 3):
-        part = call(next_kernel, [shape], [rows_in, rows_grad] + pieces[2 * d : 2 * d + 2], 3 * product // N_Y)
-        parts.append(shift(part, "y", -d, N_Y))
-    part = call(next_kernel, [shape], [rows_in, rows_grad] + pieces[:2], 3 * product // N_Y, F32)
-    grads = call(hidden_kernel, [(N_Y, 2, rows, units)], [part] + parts, 40 * rows * units)
+    product = 2 * rows * chip * units
+    rows_in, rows_grad, part_2 = call(
+        first_kernel, [(rows, chip), (rows, chip), shape], [recv, blocks[2], other_2], 3 * product
+    )
+    arrived = shift(part_2, "y", -2, N_Y)
+    part_1 = call(next_kernel, [shape], [rows_in, rows_grad, blocks[1], other_1], 3 * product)
+    part_1 = shift(part_1, "y", -1, N_Y)
+    part_3 = call(next_kernel, [shape], [rows_in, rows_grad, blocks[3], other_3], 3 * product)
+    part_3 = shift(part_3, "y", -3, N_Y)
+    part_0 = call(own_kernel, [shape], [rows_in, rows_grad, blocks[0], other_0, arrived], 3 * product, F32)
+    grads = call(hidden_kernel, [(N_Y, 2, rows, units)], [part_0, part_1, part_3], 40 * rows * units)
     grads = lax.all_to_all(grads, "y", split_axis=0, concat_axis=0, tiled=True)
-    back = call(back_kernel, [(groups, SLOTS, chip)], [here_ref, grads] + pieces, 2 * product)
+    back = call(
+        back_kernel, [(groups, SLOTS, chip)], [here_ref, grads, *blocks, other_0, other_1, other_2, other_3], 8 * product
+    )
     returned = lax.all_to_all(back, GROUP, split_axis=0, concat_axis=0, tiled=True).reshape(rows, chip)
     mixed = dot(returned, weights, 0, 0)
     mixed = (mixed[:, :tokens] + mixed[:, tokens:]).reshape(N_C, width, tokens)
     mine = lax.dynamic_index_in_dim(mixed, core, 0, keepdims=False)
     sibling = lax.dynamic_index_in_dim(mixed, 1 - core, 0, keepdims=False)
-    result = mine + shift(sibling, "c", 1, N_C)
+    sent = lax.all_gather(sibling, "c", axis=0)
+    result = mine + lax.dynamic_index_in_dim(sent, 1 - core, 0, keepdims=False)
     return result.astype(BF16).T
 
 

time: 171 us -> 167 us (0.977)
  starting transfers between devices: 74.7 us -> 66.1 us
  blocking collectives: 22.5 us -> 29.5 us
  waiting for transfers between devices: 53.1 us -> 50.5 us
  matrix products: 0.34 us -> 2.7 us
    all_gather x0 -> x1, blocking collectives: none -> 7.65 us  [shards(): sent = lax.all_gather(sibling, 'c', axis=0)]
    ppermute x11 -> x10, starting transfers between devices: 40.4 us -> 32.8 us  [shift(): lax.ppermute(value, axis, [(i, (i + step) % size) for i in range(size)])]
    ppermute x11 -> x10, waiting for transfers between devices: 28.2 us -> 25 us  [shift(): lax.ppermute(value, axis, [(i, (i + step) % size) for i in range(size)])]
    dot_general x1 -> x2, matrix products: 0.34 us -> 2.7 us  [dot(): lax.dot_general(left, right, (((left_dim,), (right_dim,)), ((), ())), pre...]
    pallas_call x0 -> x1, Pallas kernels: none -> 1.93 us  [call_select(): pl.pallas_call(select_kernel, out_shape=[jax.ShapeDtypeStruct((width, 2 *...]
    pallas_call x8 -> x7, Pallas kernels: 11.9 us -> 10.2 us  [call(): pl.pallas_call(kernel, out_shape=[jax.ShapeDtypeStruct(shape, kind) for s...]
  transfers between devices with their start and end apart: 13 -> 12, of which waited for: 7 -> 6; matrix products, arithmetic and copies ran while one was open for 2% -> 2% of each run, Pallas kernels for 4% -> 4%
where the time goes in v5:
time: 167 us
  starting transfers between devices  66.1 us (40%)
  waiting for transfers between devices  50.5 us (30%)
  blocking collectives  29.5 us (18%)
  Pallas kernels  12.1 us (7%)
  local copies, waits for them, and re-layouts  2.89 us (2%)
  matrix products  2.7 us (2%)
  other arithmetic  2.47 us (1%)
    ppermute x10, starting transfers between devices, shift(): lax.ppermute(value, axis, [(i, (i + step) % size) for i in range(size)])  32.8 us
    ppermute x10, waiting for transfers between devices, shift(): lax.ppermute(value, axis, [(i, (i + step) % size) for i in range(size)])  25 us
    all_to_all x1, waiting for transfers between devices, shards(): lax.all_to_all(back, GROUP, split_axis=0, concat_axis=0, tiled=True)  25 us
    all_to_all x1, starting transfers between devices, shards(): lax.all_to_all(back, GROUP, split_axis=0, concat_axis=0, tiled=True)  20.5 us
    all_to_all x1, blocking collectives, shards(): grads = lax.all_to_all(grads, 'y', split_axis=0, concat_axis=0, tiled=True)  12.9 us
    all_to_all x1, starting transfers between devices, shards(): recv = lax.all_to_all(send, GROUP, split_axis=0, concat_axis=0, tiled=True)  12.9 us
    pallas_call x7, Pallas kernels, call(): pl.pallas_call(kernel, out_shape=[jax.ShapeDtypeStruct(shape, kind) for s...  10.2 us
    all_gather x1, blocking collectives, shards(): both = lax.all_gather(own, 'c', axis=0, tiled=True)  8.85 us
  transfers between devices with their start and end apart: 12, of which 6 were waited for; matrix products, arithmetic and copies ran while one was open for 2% of the time, Pallas kernels for 4%

profile of v5, /device:TPU:1, one launch (start us, length us, event | category | flops | bytes accessed | tf_op | source)
XLA Modules:
  0.0 166.6 jit_solution(9382477966190138548)
XLA Ops:
  0.0 1.9 %shard_map.73 = (bf16[448,256]{1,0:T(8,128)(2,1)}, bf16[512,256]{1,0:T(8,128)(2,1)}) custom-call(s32[1]{0:T(128)} %bitcast.1.core_ref, s32[2,128]{1,0:T(2,128)} %bitcast.22, bf16[448,128]{1,0:T(8,128)(2,1)} %bitcast.28, bf16[448,128]{1,0:T(8,128)(2,1)} %bitcast.29), custom_call_target="tpu_custom_call" | custom-call | flops 19660800 | bytes 720896 | tf_op jit(solution)/shard_map/pallas_call | solution.py:156
  1.9 8.8 %all_gather.7 = bf16[896,256]{1,0:T(8,128)(2,1)S(1)} all-gather(bf16[448,256]{1,0:T(8,128)(2,1)} %get-tuple-element.15), channel_id=1, replica_groups=mesh['z'=16,'x'=4,'y'=4,'c'=2] {'c'}, dimensions={0}, use_global_device_ids=true | all-gather | bytes 688128 | tf_op jit(solution)/shard_map/all_gather | solution.py:182
  10.8 2.4 %fusion = bf16[64,8,896]{2,1,0:T(8,128)(2,1)} fusion(bf16[512,256]{1,0:T(8,128)(2,1)} %get-tuple-element.14, bf16[896,256]{1,0:T(8,128)(2,1)S(1)} %all_gather.7), kind=kOutput, calls=%fused_computation.2 | convolution fusion | flops 235339776 | bytes 1638400 | tf_op jit(solution)/shard_map/dot_general | solution.py:17
  13.2 12.9 %all-to-all-start = ((bf16[64,8,896]{2,1,0:T(8,128)(2,1)}), bf16[64,8,896]{2,1,0:T(8,128)(2,1)S(1)}, u32[]{:S(2)}, u32[]{:S(2)}) async-start(bf16[64,8,896]{2,1,0:T(8,128)(2,1)} %fusion), calls=%async_computation | async-start | bytes 1835008 | tf_op jit(solution)/shard_map/all_to_all | solution.py:187
  26.8 1.8 %pad_maximum_fusion = bf16[3,3584,128]{2,1,0:T(8,128)(2,1)S(1)} fusion(bf16[1,3584,128]{2,1,0:T(8,128)(2,1)S(1)} %bitcast.25, bf16[1,3584,128]{2,1,0:T(8,128)(2,1)} %param.12, bf16[1,3584,128]{2,1,0:T(8,128)(2,1)} %param.11), kind=kLoop, calls=%fused_computation | loop fusion | flops 2752512 | bytes 5505024 | tf_op jit(solution)/shard_map/stack | solution.py:189
  28.7 4.8 %collective-permute-start = (bf16[3,896,128]{2,1,0:T(8,128)(2,1)S(1)}, bf16[3,896,128]{2,1,0:T(8,128)(2,1)S(1)}, u32[]{:S(2)}, u32[]{:S(2)}) collective-permute-start(bf16[3,896,128]{2,1,0:T(8,128)(2,1)S(1)} %get-tuple-element.26), channel_id=1, source_target_pairs={{0,4},{2,6},{4,0},{6,2},{1,5},{3,7},{5,1},{7,3},{8,12},{10,14},{12... | collective-permute-start | bytes 2064392 | tf_op jit(solution)/shard_map/ppermute | solution.py:23
  33.6 2.3 %collective-permute-start.4 = (bf16[3,896,128]{2,1,0:T(8,128)(2,1)S(1)}, bf16[3,896,128]{2,1,0:T(8,128)(2,1)S(1)}, u32[]{:S(2)}, u32[]{:S(2)}) collective-permute-start(bf16[3,896,128]{2,1,0:T(8,128)(2,1)S(1)} %get-tuple-element.24), channel_id=1, source_target_pairs={{0,2},{2,4},{4,6},{6,0},{1,3},{3,5},{5,7},{7,1},{8,10},{10,12},{12... | collective-permute-start | bytes 2064392 | tf_op jit(solution)/shard_map/ppermute | solution.py:23
  35.9 4.2 %collective-permute-start.7 = (bf16[3,896,128]{2,1,0:T(8,128)(2,1)S(1)}, bf16[3,896,128]{2,1,0:T(8,128)(2,1)}, u32[]{:S(2)}, u32[]{:S(2)}) collective-permute-start(bf16[3,896,128]{2,1,0:T(8,128)(2,1)S(1)} %get-tuple-element.23), channel_id=1, source_target_pairs={{0,6},{2,0},{4,2},{6,4},{1,7},{3,1},{5,3},{7,5},{8,14},{10,8},{12,... | collective-permute-start | bytes 2064392 | tf_op jit(solution)/shard_map/ppermute | solution.py:23
  40.1 8.4 %collective-permute-done.block_ref.refs_2_ = bf16[3,896,128]{2,1,0:T(8,128)(2,1)S(1)} collective-permute-done((bf16[3,896,128]{2,1,0:T(8,128)(2,1)S(1)}, bf16[3,896,128]{2,1,0:T(8,128)(2,1)S(1)}, u32[]{:S(2)}, u32[]{:S(2)}) %collective-permute-start) | collective-permute-done | bytes 688160 | tf_op jit(solution)/shard_map/ppermute | solution.py:23
  48.5 4.6 %collective-permute-start.1 = (bf16[3,896,128]{2,1,0:T(8,128)(2,1)S(1)}, bf16[3,896,128]{2,1,0:T(8,128)(2,1)S(1)}, u32[]{:S(2)}, u32[]{:S(2)}) collective-permute-start(bf16[3,896,128]{2,1,0:T(8,128)(2,1)S(1)} %collective-permute-done.block_ref.refs_2_), channel_id=1, source_target_pairs={{0,1},{1,0},{2,3},{3,2},{4,5},{5,4},{6,7},{7,6},{8,9},{9,8},{10,11... | collective-permute-start | bytes 2064392 | tf_op jit(solution)/shard_map/ppermute | solution.py:23
  53.1 11.2 %collective-permute-done.4.block_ref.refs_1_ = bf16[3,896,128]{2,1,0:T(8,128)(2,1)S(1)} collective-permute-done((bf16[3,896,128]{2,1,0:T(8,128)(2,1)S(1)}, bf16[3,896,128]{2,1,0:T(8,128)(2,1)S(1)}, u32[]{:S(2)}, u32[]{:S(2)}) %collective-permute-start.4) | collective-permute-done | bytes 688160 | tf_op jit(solution)/shard_map/ppermute | solution.py:23
  64.2 2.4 %collective-permute-start.5 = (bf16[3,896,128]{2,1,0:T(8,128)(2,1)S(1)}, bf16[3,896,128]{2,1,0:T(8,128)(2,1)}, u32[]{:S(2)}, u32[]{:S(2)}) collective-permute-start(bf16[3,896,128]{2,1,0:T(8,128)(2,1)S(1)} %collective-permute-done.4.block_ref.refs_1_), channel_id=1, source_target_pairs={{0,1},{1,0},{2,3},{3,2},{4,5},{5,4},{6,7},{7,6},{8,9},{9,8},{10,11... | collective-permute-start | bytes 2064392 | tf_op jit(solution)/shard_map/ppermute | solution.py:23
  66.7 1.9 %collective-permute-start.8 = (bf16[3,896,128]{2,1,0:T(8,128)(2,1)}, bf16[3,896,128]{2,1,0:T(8,128)(2,1)}, u32[]{:S(2)}, u32[]{:S(2)}) collective-permute-start(bf16[3,896,128]{2,1,0:T(8,128)(2,1)} %collective-permute-done.7.block_ref.refs_3_), channel_id=1, source_target_pairs={{0,1},{1,0},{2,3},{3,2},{4,5},{5,4},{6,7},{7,6},{8,9},{9,8},{10,11... | collective-permute-start | bytes 2064392 | tf_op jit(solution)/shard_map/ppermute | solution.py:23
  68.6 2.4 %collective-permute-start.2 = (bf16[3,896,128]{2,1,0:T(8,128)(2,1)S(1)}, bf16[3,896,128]{2,1,0:T(8,128)(2,1)}, u32[]{:S(2)}, u32[]{:S(2)}) collective-permute-start(bf16[3,896,128]{2,1,0:T(8,128)(2,1)S(1)} %get-tuple-element.25.block_ref.refs_0_), channel_id=1, source_target_pairs={{0,1},{1,0},{2,3},{3,2},{4,5},{5,4},{6,7},{7,6},{8,9},{9,8},{10,11... | collective-permute-start | bytes 2064392 | tf_op jit(solution)/shard_map/ppermute | solution.py:23
  74.1 4.9 %collective-permute-start.3 = (bf16[3,256,256]{2,1,0:T(8,128)(2,1)S(1)}, bf16[3,256,256]{2,1,0:T(8,128)(2,1)S(1)}, u32[]{:S(2)}, u32[]{:S(2)}) collective-permute-start(bf16[3,256,256]{2,1,0:T(8,128)(2,1)S(1)} %get-tuple-element.22), channel_id=1, source_target_pairs={{0,4},{2,6},{4,0},{6,2},{1,5},{3,7},{5,1},{7,3},{8,12},{10,14},{12... | collective-permute-start | bytes 1179656 | tf_op jit(solution)/shard_map/ppermute | solution.py:23
  80.7 2.7 %collective-permute-start.6 = (bf16[3,256,256]{2,1,0:T(8,128)(2,1)S(1)}, bf16[3,256,256]{2,1,0:T(8,128)(2,1)S(1)}, u32[]{:S(2)}, u32[]{:S(2)}) collective-permute-start(bf16[3,256,256]{2,1,0:T(8,128)(2,1)S(1)} %shard_map.76), channel_id=1, source_target_pairs={{0,6},{2,0},{4,2},{6,4},{1,7},{3,1},{5,3},{7,5},{8,14},{10,8},{12,... | collective-permute-start | bytes 1179656 | tf_op jit(solution)/shard_map/ppermute | solution.py:23
  83.4 1.9 %shard_map.77 = bf16[3,256,256]{2,1,0:T(8,128)(2,1)S(1)} custom-call(bf16[256,896]{1,0:T(8,128)(2,1)S(1)} %get-tuple-element.20.in_ref, bf16[256,896]{1,0:T(8,128)(2,1)S(1)} %get-tuple-element.21.grad_ref, bf16[3,896,128]{2,1,0:T(8,128)(2,1)} %collective-permute-done.7.block_ref.refs_3_, bf16[3,896,128]{2,1,0:T(8,128)(2,1)} %collective-permute-done.8.other_ref.refs_7_), custom_call_target="tpu_custom_call" | custom-call | flops 352321536 | bytes 393216 | tf_op jit(solution)/shard_map/pallas_call | solution.py:143
  85.3 2.6 %collective-permute-start.9 = (bf16[3,256,256]{2,1,0:T(8,128)(2,1)S(1)}, bf16[3,256,256]{2,1,0:T(8,128)(2,1)S(1)}, u32[]{:S(2)}, u32[]{:S(2)}) collective-permute-start(bf16[3,256,256]{2,1,0:T(8,128)(2,1)S(1)} %shard_map.77), channel_id=1, source_target_pairs={{0,2},{2,4},{4,6},{6,0},{1,3},{3,5},{5,7},{7,1},{8,10},{10,12},{12... | collective-permute-start | bytes 1179656 | tf_op jit(solution)/shard_map/ppermute | solution.py:23
  89.6 4.0 %collective-permute-done.6.next_ref = bf16[3,256,256]{2,1,0:T(8,128)(2,1)S(1)} collective-permute-done((bf16[3,256,256]{2,1,0:T(8,128)(2,1)S(1)}, bf16[3,256,256]{2,1,0:T(8,128)(2,1)S(1)}, u32[]{:S(2)}, u32[]{:S(2)}) %collective-permute-start.6) | collective-permute-done | bytes 393248 | tf_op jit(solution)/shard_map/ppermute | solution.py:23
  95.2 12.9 %all_to_all.15.grads_ref = bf16[4,2,256,256]{3,2,1,0:T(8,128)(2,1)S(1)} all-to-all(bf16[4,2,256,256]{3,2,1,0:T(8,128)(2,1)S(1)} %shard_map.78), channel_id=1, replica_groups=mesh['z'=16,'x'=4,'y'=4,'c'=2] {'y'}, dimensions={0} | all-to-all | bytes 2097152 | tf_op jit(solution)/shard_map/all_to_all | solution.py:211
  108.2 3.8 %shard_map.79 = bf16[64,4,896]{2,1,0:T(4,128)(2,1)} custom-call(s32[1]{0:T(128)} %bitcast.here_ref, bf16[4,2,256,256]{3,2,1,0:T(8,128)(2,1)S(1)} %all_to_all.15.grads_ref, bf16[3,896,128]{2,1,0:T(8,128)(2,1)S(1)} %get-tuple-element.25.block_ref.refs_0_, bf16[3,896,128]{2,1,0:T(8,128)(2,1)S(1)} %collective-permute-done.4.block_ref.refs_1_, ...), custom_call_target="tpu_custom_call" | custom-call | flops 939524096 | bytes 458752 | tf_op jit(solution)/shard_map/pallas_call | solution.py:143
  112.0 20.5 %all-to-all-start.2 = ((bf16[64,4,896]{2,1,0:T(4,128)(2,1)}), bf16[64,4,896]{2,1,0:T(4,128)(2,1)S(1)}, u32[]{:S(2)}, u32[]{:S(2)}) async-start(bf16[64,4,896]{2,1,0:T(4,128)(2,1)} %shard_map.79), calls=%async_computation.2 | async-start | bytes 917504 | tf_op jit(solution)/shard_map/all_to_all | solution.py:215
  132.8 25.0 %all-to-all-done.2 = bf16[64,4,896]{2,1,0:T(4,128)(2,1)S(1)} async-done(((bf16[64,4,896]{2,1,0:T(4,128)(2,1)}), bf16[64,4,896]{2,1,0:T(4,128)(2,1)S(1)}, u32[]{:S(2)}, u32[]{:S(2)}) %all-to-all-start.2) | async-done | bytes 458784 | tf_op jit(solution)/shard_map/all_to_all | solution.py:215
  158.3 7.7 %all_gather.8 = f32[2,448,128]{2,1,0:T(8,128)S(1)} all-gather(f32[1,448,128]{2,1,0:T(8,128)S(1)} %constant_dynamic-slice_fusion), channel_id=1, replica_groups=mesh['z'=16,'x'=4,'y'=4,'c'=2] {'c'}, dimensions={0}, use_global_device_ids=true | all-gather | bytes 688128 | tf_op jit(solution)/shard_map/all_gather | solution.py:220
  (32 shorter events, 10.5 us)
Async XLA Ops:
  0.0 26.1 %copy-start.5 = (bf16[1,128,3584]{2,1,0:T(8,128)(2,1)S(1)}, bf16[1,128,3584]{2,1,0:T(8,128)(2,1)}, u32[]{:S(2)}) copy-start(bf16[1,128,3584]{2,1,0:T(8,128)(2,1)} %param.13) | copy-start | bytes 2752516
  13.2 59.2 %all-to-all-start = ((bf16[64,8,896]{2,1,0:T(8,128)(2,1)}), bf16[64,8,896]{2,1,0:T(8,128)(2,1)S(1)}, u32[]{:S(2)}, u32[]{:S(2)}) async-start(bf16[64,8,896]{2,1,0:T(8,128)(2,1)} %fusion), calls=%async_computation | async-start | bytes 1835008 | tf_op jit(solution)/shard_map/all_to_all | solution.py:187
  28.7 19.8 %collective-permute-start = (bf16[3,896,128]{2,1,0:T(8,128)(2,1)S(1)}, bf16[3,896,128]{2,1,0:T(8,128)(2,1)S(1)}, u32[]{:S(2)}, u32[]{:S(2)}) collective-permute-start(bf16[3,896,128]{2,1,0:T(8,128)(2,1)S(1)} %get-tuple-element.26), channel_id=1, source_target_pairs={{0,4},{2,6},{4,0},{6,2},{1,5},{3,7},{5,1},{7,3},{8,12},{10,14},{12... | collective-permute-start | bytes 2064392 | tf_op jit(solution)/shard_map/ppermute | solution.py:23
  33.6 30.7 %collective-permute-start.4 = (bf16[3,896,128]{2,1,0:T(8,128)(2,1)S(1)}, bf16[3,896,128]{2,1,0:T(8,128)(2,1)S(1)}, u32[]{:S(2)}, u32[]{:S(2)}) collective-permute-start(bf16[3,896,128]{2,1,0:T(8,128)(2,1)S(1)} %get-tuple-element.24), channel_id=1, source_target_pairs={{0,2},{2,4},{4,6},{6,0},{1,3},{3,5},{5,7},{7,1},{8,10},{10,12},{12... | collective-permute-start | bytes 2064392 | tf_op jit(solution)/shard_map/ppermute | solution.py:23
  35.9 30.8 %collective-permute-start.7 = (bf16[3,896,128]{2,1,0:T(8,128)(2,1)S(1)}, bf16[3,896,128]{2,1,0:T(8,128)(2,1)}, u32[]{:S(2)}, u32[]{:S(2)}) collective-permute-start(bf16[3,896,128]{2,1,0:T(8,128)(2,1)S(1)} %get-tuple-element.23), channel_id=1, source_target_pairs={{0,6},{2,0},{4,2},{6,4},{1,7},{3,1},{5,3},{7,5},{8,14},{10,8},{12,... | collective-permute-start | bytes 2064392 | tf_op jit(solution)/shard_map/ppermute | solution.py:23
  48.5 22.5 %collective-permute-start.1 = (bf16[3,896,128]{2,1,0:T(8,128)(2,1)S(1)}, bf16[3,896,128]{2,1,0:T(8,128)(2,1)S(1)}, u32[]{:S(2)}, u32[]{:S(2)}) collective-permute-start(bf16[3,896,128]{2,1,0:T(8,128)(2,1)S(1)} %collective-permute-done.block_ref.refs_2_), channel_id=1, source_target_pairs={{0,1},{1,0},{2,3},{3,2},{4,5},{5,4},{6,7},{7,6},{8,9},{9,8},{10,11... | collective-permute-start | bytes 2064392 | tf_op jit(solution)/shard_map/ppermute | solution.py:23
  64.2 14.7 %collective-permute-start.5 = (bf16[3,896,128]{2,1,0:T(8,128)(2,1)S(1)}, bf16[3,896,128]{2,1,0:T(8,128)(2,1)}, u32[]{:S(2)}, u32[]{:S(2)}) collective-permute-start(bf16[3,896,128]{2,1,0:T(8,128)(2,1)S(1)} %collective-permute-done.4.block_ref.refs_1_), channel_id=1, source_target_pairs={{0,1},{1,0},{2,3},{3,2},{4,5},{5,4},{6,7},{7,6},{8,9},{9,8},{10,11... | collective-permute-start | bytes 2064392 | tf_op jit(solution)/shard_map/ppermute | solution.py:23
  66.7 16.7 %collective-permute-start.8 = (bf16[3,896,128]{2,1,0:T(8,128)(2,1)}, bf16[3,896,128]{2,1,0:T(8,128)(2,1)}, u32[]{:S(2)}, u32[]{:S(2)}) collective-permute-start(bf16[3,896,128]{2,1,0:T(8,128)(2,1)} %collective-permute-done.7.block_ref.refs_3_), channel_id=1, source_target_pairs={{0,1},{1,0},{2,3},{3,2},{4,5},{5,4},{6,7},{7,6},{8,9},{9,8},{10,11... | collective-permute-start | bytes 2064392 | tf_op jit(solution)/shard_map/ppermute | solution.py:23
  68.6 19.3 %collective-permute-start.2 = (bf16[3,896,128]{2,1,0:T(8,128)(2,1)S(1)}, bf16[3,896,128]{2,1,0:T(8,128)(2,1)}, u32[]{:S(2)}, u32[]{:S(2)}) collective-permute-start(bf16[3,896,128]{2,1,0:T(8,128)(2,1)S(1)} %get-tuple-element.25.block_ref.refs_0_), channel_id=1, source_target_pairs={{0,1},{1,0},{2,3},{3,2},{4,5},{5,4},{6,7},{7,6},{8,9},{9,8},{10,11... | collective-permute-start | bytes 2064392 | tf_op jit(solution)/shard_map/ppermute | solution.py:23
  71.0 0.8 copy-start
  72.4 1.1 copy-start.1
  74.1 13.8 %collective-permute-start.3 = (bf16[3,256,256]{2,1,0:T(8,128)(2,1)S(1)}, bf16[3,256,256]{2,1,0:T(8,128)(2,1)S(1)}, u32[]{:S(2)}, u32[]{:S(2)}) collective-permute-start(bf16[3,256,256]{2,1,0:T(8,128)(2,1)S(1)} %get-tuple-element.22), channel_id=1, source_target_pairs={{0,4},{2,6},{4,0},{6,2},{1,5},{3,7},{5,1},{7,3},{8,12},{10,14},{12... | collective-permute-start | bytes 1179656 | tf_op jit(solution)/shard_map/ppermute | solution.py:23
  80.7 12.9 %collective-permute-start.6 = (bf16[3,256,256]{2,1,0:T(8,128)(2,1)S(1)}, bf16[3,256,256]{2,1,0:T(8,128)(2,1)S(1)}, u32[]{:S(2)}, u32[]{:S(2)}) collective-permute-start(bf16[3,256,256]{2,1,0:T(8,128)(2,1)S(1)} %shard_map.76), channel_id=1, source_target_pairs={{0,6},{2,0},{4,2},{6,4},{1,7},{3,1},{5,3},{7,5},{8,14},{10,8},{12,... | collective-permute-start | bytes 1179656 | tf_op jit(solution)/shard_map/ppermute | solution.py:23
  85.3 9.7 %collective-permute-start.9 = (bf16[3,256,256]{2,1,0:T(8,128)(2,1)S(1)}, bf16[3,256,256]{2,1,0:T(8,128)(2,1)S(1)}, u32[]{:S(2)}, u32[]{:S(2)}) collective-permute-start(bf16[3,256,256]{2,1,0:T(8,128)(2,1)S(1)} %shard_map.77), channel_id=1, source_target_pairs={{0,2},{2,4},{4,6},{6,0},{1,3},{3,5},{5,7},{7,1},{8,10},{10,12},{12... | collective-permute-start | bytes 1179656 | tf_op jit(solution)/shard_map/ppermute | solution.py:23
  89.6 18.6 %copy-start.2 = (bf16[3,896,128]{2,1,0:T(8,128)(2,1)S(1)}, bf16[3,896,128]{2,1,0:T(8,128)(2,1)}, u32[]{:S(2)}) copy-start(bf16[3,896,128]{2,1,0:T(8,128)(2,1)} %copy-done) | copy-start | bytes 2064388
  108.2 24.3 %copy-start.3 = (s32[128,2]{0,1:T(2,128)S(1)}, s32[128,2]{0,1:T(2,128)}, u32[]{:S(2)}) copy-start(s32[128,2]{0,1:T(2,128)} %param.9) | copy-start | bytes 3076
  108.2 24.3 %copy-start.4 = (f32[128,2]{0,1:T(2,128)S(1)}, f32[128,2]{0,1:T(2,128)}, u32[]{:S(2)}) copy-start(f32[128,2]{0,1:T(2,128)} %param.10) | copy-start | bytes 3076
  112.0 45.8 %all-to-all-start.2 = ((bf16[64,4,896]{2,1,0:T(4,128)(2,1)}), bf16[64,4,896]{2,1,0:T(4,128)(2,1)S(1)}, u32[]{:S(2)}, u32[]{:S(2)}) async-start(bf16[64,4,896]{2,1,0:T(4,128)(2,1)} %shard_map.79), calls=%async_computation.2 | async-start | bytes 917504 | tf_op jit(solution)/shard_map/all_to_all | solution.py:215

commit v6 on v5

--- a/solution.py
+++ b/solution.py
@@ -9,6 +9,7 @@
 GROUP = ("z", "x")
 LOCAL = ("y", "c")
 SLOTS = 4
+PAD = 16
 BF16 = jnp.bfloat16
 F32 = jnp.float32
 
@@ -31,47 +32,57 @@
     return jnp.where(condition, 1.0, 0.0).astype(BF16)
 
 
-def routing(ids_ref, experts):
-    tokens = ids_ref.shape[1]
-    expert = iota(experts, tokens, 0)
-    first = ids_ref[0:1, :] == expert
-    second = ids_ref[1:2, :] == expert
+def routing(ids, experts):
+    tokens = ids.shape[1]
+    expert = iota(experts, tokens, 0).astype(ids.dtype)
+    first = ids[0:1, :] == expert
+    second = ids[1:2, :] == expert
     named = ones_where(first | second)
     earlier = ones_where(iota(tokens, tokens, 0) < iota(tokens, tokens, 1))
     ranks = dot(named, earlier, 1, 0)
     return first, second, named, ranks.astype(BF16)
 
 
-def select_kernel(core_ref, ids_ref, in_ref, grad_ref, own_ref, select_ref, ids_held, sems):
-    tokens = ids_ref.shape[1]
+def pack_kernel(ids_ref, in_ref, grad_ref, own_ref, ids_held, sems):
+    width, tokens = in_ref.shape
     copies = [
         pltpu.make_async_copy(ids_ref, ids_held, sems.at[0]),
-        pltpu.make_async_copy(in_ref, own_ref.at[:, pl.ds(0, tokens)], sems.at[1]),
-        pltpu.make_async_copy(grad_ref, own_ref.at[:, pl.ds(tokens, tokens)], sems.at[2]),
+        pltpu.make_async_copy(in_ref, own_ref.at[pl.ds(0, width), pl.ds(0, tokens)], sems.at[1]),
+        pltpu.make_async_copy(grad_ref, own_ref.at[pl.ds(0, width), pl.ds(tokens, tokens)], sems.at[2]),
     ]
     for copy in copies:
         copy.start()
-    chunk = 2 * SLOTS
-    rows = select_ref.shape[0]
-    experts = rows // chunk
     copies[0].wait()
-    _, _, named, ranks = routing(ids_held, experts)
-    spread = ones_where(iota(rows, experts, 0) // chunk == iota(rows, experts, 1))
+    ids = ids_held[...].astype(F32)
+    row = iota(PAD, tokens, 0)
+    under = jnp.where(row == 0, ids[0:1, :], jnp.where(row == 1, ids[1:2, :], 0.0)).astype(BF16)
+    own_ref[width : width + PAD, :tokens] = under
+    own_ref[width : width + PAD, tokens:] = jnp.zeros_like(under)
+    copies[1].wait()
+    copies[2].wait()
+
+
+def dispatch_kernel(core_ref, both_ref, send_ref):
+    groups, chunk, chip = send_ref.shape
+    rows, width, tokens = groups * chunk, chip // N_C, both_ref.shape[1] // 2
+    _, _, named, ranks = routing(both_ref[width : width + PAD, :tokens].astype(F32), groups)
+    spread = ones_where(iota(rows, groups, 0) // chunk == iota(rows, groups, 1))
     spread_named = dot(spread, named, 1, 0)
     spread_ranks = dot(spread, ranks, 1, 0)
     place = iota(rows, tokens, 0) % chunk
     wanted = (place % SLOTS + SLOTS * core_ref[0]).astype(F32)
     chosen = (spread_named > 0.5) & (spread_ranks == wanted)
-    select_ref[:, :tokens] = ones_where(chosen & (place < SLOTS))
-    select_ref[:, tokens:] = ones_where(chosen & (place >= SLOTS))
-    copies[1].wait()
-    copies[2].wait()
+    select = jnp.concatenate(
+        [ones_where(chosen & (place < SLOTS)), ones_where(chosen & (place >= SLOTS))], axis=1
+    )
+    both = jnp.concatenate([both_ref[c * (width + PAD) : c * (width + PAD) + width] for c in range(N_C)], axis=0)
+    send_ref[...] = dot(select, both, 1, 1).reshape(send_ref.shape).astype(BF16)
 
 
 def weight_kernel(core_ref, ids_ref, probs_ref, weight_ref):
     rows = weight_ref.shape[0]
     experts, tokens = rows // SLOTS, ids_ref.shape[1]
-    first, second, named, ranks = routing(ids_ref, experts)
+    first, second, named, ranks = routing(ids_ref[...], experts)
     probs = jnp.where(first, probs_ref[0:1, :], 0.0) + jnp.where(second, probs_ref[1:2, :], 0.0)
     high = probs.astype(BF16)
     low = (probs - high.astype(F32)).astype(BF16)
@@ -121,12 +132,10 @@
 
 def back_kernel(here_ref, grads_ref, *refs):
     blocks, others, out_ref = refs[:N_Y], refs[N_Y:-1], refs[-1]
-    total = None
-    for d in range(N_Y):
-        origin = lax.rem(here_ref[0] + N_Y - d, N_Y)
-        for m in range(2):
-            term = dot(grads_ref[origin, m], units_of(blocks[d], others[d], m), 1, 1)
-            total = term if total is None else total + term
+    origins = [lax.rem(here_ref[0] + N_Y - d, N_Y) for d in range(N_Y)]
+    left = jnp.concatenate([grads_ref[origins[d], m] for d in range(N_Y) for m in range(2)], axis=1)
+    right = jnp.concatenate([units_of(blocks[d], others[d], m) for d in range(N_Y) for m in range(2)], axis=1)
+    total = dot(left, right, 1, 1)
     out_ref[...] = total.reshape(out_ref.shape).astype(BF16)
 
 
@@ -151,22 +160,17 @@
     return out if len(shapes) > 1 else out[0]
 
 
-def call_select(core_ref, ids, layer_input, out_grad, rows):
+def call_pack(ids, layer_input, out_grad):
     width, tokens = layer_input.shape
     return pl.pallas_call(
-        select_kernel,
-        out_shape=[
-            jax.ShapeDtypeStruct((width, 2 * tokens), BF16),
-            jax.ShapeDtypeStruct((rows, 2 * tokens), BF16),
-        ],
-        in_specs=[pl.BlockSpec(memory_space=pltpu.SMEM)] + [pl.BlockSpec(memory_space=pl.ANY)] * 3,
-        out_specs=[pl.BlockSpec(memory_space=pltpu.VMEM)] * 2,
+        pack_kernel,
+        out_shape=jax.ShapeDtypeStruct((width + PAD, 2 * tokens), BF16),
+        in_specs=[pl.BlockSpec(memory_space=pl.ANY)] * 3,
+        out_specs=pl.BlockSpec(memory_space=pltpu.VMEM),
         scratch_shapes=[pltpu.VMEM(ids.shape, jnp.int32), pltpu.SemaphoreType.DMA((3,))],
         compiler_params=pltpu.CompilerParams(vmem_limit_bytes=60 * 1024 * 1024),
-        cost_estimate=pl.CostEstimate(
-            flops=rows * tokens * 300, bytes_accessed=4 * tokens * (2 * width + rows), transcendentals=0
-        ),
-    )(core_ref, ids, layer_input, out_grad)
+        cost_estimate=pl.CostEstimate(flops=0, bytes_accessed=8 * tokens * width, transcendentals=0),
+    )(ids, layer_input, out_grad)
 
 
 def shards(layer_input, out_grad, expert_ids, gate_probs, w_gate, w_up, w_down):
@@ -178,9 +182,8 @@
     here = lax.axis_index("y")
     core_ref = core.astype(jnp.int32).reshape(1)
 
-    own, select = call_select(core_ref, expert_ids.T, layer_input.T, out_grad.T, 2 * rows)
-    both = lax.all_gather(own, "c", axis=0, tiled=True)
-    send = dot(select, both, 1, 1).astype(BF16).reshape(groups, 2 * SLOTS, chip)
+    both = lax.all_gather(call_pack(expert_ids.T, layer_input.T, out_grad.T), "c", axis=0, tiled=True)
+    send = call(dispatch_kernel, [(groups, 2 * SLOTS, chip)], [core_ref, both], 8 * rows * chip * tokens)
     weights = call(weight_kernel, [(rows, 2 * tokens)], (core_ref, expert_ids.T, gate_probs.T), rows * tokens * 256)
 
     send, w_gate, w_up, w_down = lax.optimization_barrier((send, w_gate, w_up, w_down))

time: 167 us -> 167 us (level)
  matrix products: 2.7 us -> 0.34 us
    dot_general x2 -> x1, matrix products: 2.7 us -> 0.34 us  [dot(): lax.dot_general(left, right, (((left_dim,), (right_dim,)), ((), ())), pre...]
    pallas_call x7 -> x8, Pallas kernels: 10.2 us -> 11.8 us  [call(): pl.pallas_call(kernel, out_shape=[jax.ShapeDtypeStruct(shape, kind) for s...]
where the time goes in v6:
time: 167 us; the launch traced here: 166 us
  starting transfers between devices  66 us (40%)
  waiting for transfers between devices  50.6 us (30%)
  blocking collectives  29.5 us (18%)
  Pallas kernels  13.6 us (8%)
  local copies, waits for them, and re-layouts  2.9 us (2%)
  other arithmetic  2.47 us (1%)
    ppermute x10, starting transfers between devices, shift(): lax.ppermute(value, axis, [(i, (i + step) % size) for i in range(size)])  32.7 us
    ppermute x10, waiting for transfers between devices, shift(): lax.ppermute(value, axis, [(i, (i + step) % size) for i in range(size)])  25 us
    all_to_all x1, waiting for transfers between devices, shards(): lax.all_to_all(back, GROUP, split_axis=0, concat_axis=0, tiled=True)  25 us
    all_to_all x1, starting transfers between devices, shards(): lax.all_to_all(back, GROUP, split_axis=0, concat_axis=0, tiled=True)  20.4 us
    all_to_all x1, blocking collectives, shards(): grads = lax.all_to_all(grads, 'y', split_axis=0, concat_axis=0, tiled=True)  13 us
    all_to_all x1, starting transfers between devices, shards(): recv = lax.all_to_all(send, GROUP, split_axis=0, concat_axis=0, tiled=True)  12.9 us
    pallas_call x8, Pallas kernels, call(): pl.pallas_call(kernel, out_shape=[jax.ShapeDtypeStruct(shape, kind) for s...  11.8 us
    all_gather x1, blocking collectives, shards(): lax.all_gather(call_pack(expert_ids.T, layer_input.T, out_grad.T), 'c', a...  8.86 us
  transfers between devices with their start and end apart: 12, of which 6 were waited for; matrix products, arithmetic and copies ran while one was open for 2% of the time, Pallas kernels for 4%

profile of v6, /device:TPU:1, one launch (start us, length us, event | category | flops | bytes accessed | tf_op | source)
XLA Modules:
  0.0 165.8 jit_solution(5657840915557977901)
XLA Ops:
  0.0 1.8 %shard_map.73 = bf16[464,256]{1,0:T(8,128)(2,1)} custom-call(s32[2,128]{1,0:T(2,128)} %bitcast.18, bf16[448,128]{1,0:T(8,128)(2,1)} %bitcast.24, bf16[448,128]{1,0:T(8,128)(2,1)} %bitcast.25), custom_call_target="tpu_custom_call" | custom-call | bytes 458752 | tf_op jit(solution)/shard_map/pallas_call | solution.py:165
  1.8 8.9 %all_gather.7.both_ref = bf16[928,256]{1,0:T(8,128)(2,1)S(1)} all-gather(bf16[464,256]{1,0:T(8,128)(2,1)} %shard_map.73), channel_id=1, replica_groups=mesh['z'=16,'x'=4,'y'=4,'c'=2] {'c'}, dimensions={0}, use_global_device_ids=true | all-gather | bytes 712704 | tf_op jit(solution)/shard_map/all_gather | solution.py:185
  12.3 12.9 %all-to-all-start = ((bf16[64,8,896]{2,1,0:T(8,128)(2,1)}), bf16[64,8,896]{2,1,0:T(8,128)(2,1)S(1)}, u32[]{:S(2)}, u32[]{:S(2)}) async-start(bf16[64,8,896]{2,1,0:T(8,128)(2,1)} %shard_map.74), calls=%async_computation | async-start | bytes 1835008 | tf_op jit(solution)/shard_map/all_to_all | solution.py:190
  25.9 1.8 %pad_maximum_fusion = bf16[3,3584,128]{2,1,0:T(8,128)(2,1)S(1)} fusion(bf16[1,3584,128]{2,1,0:T(8,128)(2,1)S(1)} %bitcast.21, bf16[1,3584,128]{2,1,0:T(8,128)(2,1)} %param.12, bf16[1,3584,128]{2,1,0:T(8,128)(2,1)} %param.11), kind=kLoop, calls=%fused_computation | loop fusion | flops 2752512 | bytes 5505024 | tf_op jit(solution)/shard_map/stack | solution.py:192
  27.9 4.8 %collective-permute-start = (bf16[3,896,128]{2,1,0:T(8,128)(2,1)S(1)}, bf16[3,896,128]{2,1,0:T(8,128)(2,1)S(1)}, u32[]{:S(2)}, u32[]{:S(2)}) collective-permute-start(bf16[3,896,128]{2,1,0:T(8,128)(2,1)S(1)} %get-tuple-element.22), channel_id=1, source_target_pairs={{0,4},{2,6},{4,0},{6,2},{1,5},{3,7},{5,1},{7,3},{8,12},{10,14},{12... | collective-permute-start | bytes 2064392 | tf_op jit(solution)/shard_map/ppermute | solution.py:24
  32.7 2.3 %collective-permute-start.4 = (bf16[3,896,128]{2,1,0:T(8,128)(2,1)S(1)}, bf16[3,896,128]{2,1,0:T(8,128)(2,1)S(1)}, u32[]{:S(2)}, u32[]{:S(2)}) collective-permute-start(bf16[3,896,128]{2,1,0:T(8,128)(2,1)S(1)} %get-tuple-element.20), channel_id=1, source_target_pairs={{0,2},{2,4},{4,6},{6,0},{1,3},{3,5},{5,7},{7,1},{8,10},{10,12},{12... | collective-permute-start | bytes 2064392 | tf_op jit(solution)/shard_map/ppermute | solution.py:24
  35.0 4.2 %collective-permute-start.7 = (bf16[3,896,128]{2,1,0:T(8,128)(2,1)S(1)}, bf16[3,896,128]{2,1,0:T(8,128)(2,1)}, u32[]{:S(2)}, u32[]{:S(2)}) collective-permute-start(bf16[3,896,128]{2,1,0:T(8,128)(2,1)S(1)} %get-tuple-element.19), channel_id=1, source_target_pairs={{0,6},{2,0},{4,2},{6,4},{1,7},{3,1},{5,3},{7,5},{8,14},{10,8},{12,... | collective-permute-start | bytes 2064392 | tf_op jit(solution)/shard_map/ppermute | solution.py:24
  39.2 8.4 %collective-permute-done.block_ref.refs_2_ = bf16[3,896,128]{2,1,0:T(8,128)(2,1)S(1)} collective-permute-done((bf16[3,896,128]{2,1,0:T(8,128)(2,1)S(1)}, bf16[3,896,128]{2,1,0:T(8,128)(2,1)S(1)}, u32[]{:S(2)}, u32[]{:S(2)}) %collective-permute-start) | collective-permute-done | bytes 688160 | tf_op jit(solution)/shard_map/ppermute | solution.py:24
  47.6 4.5 %collective-permute-start.1 = (bf16[3,896,128]{2,1,0:T(8,128)(2,1)S(1)}, bf16[3,896,128]{2,1,0:T(8,128)(2,1)S(1)}, u32[]{:S(2)}, u32[]{:S(2)}) collective-permute-start(bf16[3,896,128]{2,1,0:T(8,128)(2,1)S(1)} %collective-permute-done.block_ref.refs_2_), channel_id=1, source_target_pairs={{0,1},{1,0},{2,3},{3,2},{4,5},{5,4},{6,7},{7,6},{8,9},{9,8},{10,11... | collective-permute-start | bytes 2064392 | tf_op jit(solution)/shard_map/ppermute | solution.py:24
  52.2 11.2 %collective-permute-done.4.block_ref.refs_1_ = bf16[3,896,128]{2,1,0:T(8,128)(2,1)S(1)} collective-permute-done((bf16[3,896,128]{2,1,0:T(8,128)(2,1)S(1)}, bf16[3,896,128]{2,1,0:T(8,128)(2,1)S(1)}, u32[]{:S(2)}, u32[]{:S(2)}) %collective-permute-start.4) | collective-permute-done | bytes 688160 | tf_op jit(solution)/shard_map/ppermute | solution.py:24
  63.4 2.4 %collective-permute-start.5 = (bf16[3,896,128]{2,1,0:T(8,128)(2,1)S(1)}, bf16[3,896,128]{2,1,0:T(8,128)(2,1)}, u32[]{:S(2)}, u32[]{:S(2)}) collective-permute-start(bf16[3,896,128]{2,1,0:T(8,128)(2,1)S(1)} %collective-permute-done.4.block_ref.refs_1_), channel_id=1, source_target_pairs={{0,1},{1,0},{2,3},{3,2},{4,5},{5,4},{6,7},{7,6},{8,9},{9,8},{10,11... | collective-permute-start | bytes 2064392 | tf_op jit(solution)/shard_map/ppermute | solution.py:24
  65.8 1.9 %collective-permute-start.8 = (bf16[3,896,128]{2,1,0:T(8,128)(2,1)}, bf16[3,896,128]{2,1,0:T(8,128)(2,1)}, u32[]{:S(2)}, u32[]{:S(2)}) collective-permute-start(bf16[3,896,128]{2,1,0:T(8,128)(2,1)} %collective-permute-done.7.block_ref.refs_3_), channel_id=1, source_target_pairs={{0,1},{1,0},{2,3},{3,2},{4,5},{5,4},{6,7},{7,6},{8,9},{9,8},{10,11... | collective-permute-start | bytes 2064392 | tf_op jit(solution)/shard_map/ppermute | solution.py:24
  67.7 2.4 %collective-permute-start.2 = (bf16[3,896,128]{2,1,0:T(8,128)(2,1)S(1)}, bf16[3,896,128]{2,1,0:T(8,128)(2,1)}, u32[]{:S(2)}, u32[]{:S(2)}) collective-permute-start(bf16[3,896,128]{2,1,0:T(8,128)(2,1)S(1)} %get-tuple-element.21.block_ref.refs_0_), channel_id=1, source_target_pairs={{0,1},{1,0},{2,3},{3,2},{4,5},{5,4},{6,7},{7,6},{8,9},{9,8},{10,11... | collective-permute-start | bytes 2064392 | tf_op jit(solution)/shard_map/ppermute | solution.py:24
  73.3 4.8 %collective-permute-start.3 = (bf16[3,256,256]{2,1,0:T(8,128)(2,1)S(1)}, bf16[3,256,256]{2,1,0:T(8,128)(2,1)S(1)}, u32[]{:S(2)}, u32[]{:S(2)}) collective-permute-start(bf16[3,256,256]{2,1,0:T(8,128)(2,1)S(1)} %get-tuple-element.18), channel_id=1, source_target_pairs={{0,4},{2,6},{4,0},{6,2},{1,5},{3,7},{5,1},{7,3},{8,12},{10,14},{12... | collective-permute-start | bytes 1179656 | tf_op jit(solution)/shard_map/ppermute | solution.py:24
  78.1 1.7 %shard_map.77 = bf16[3,256,256]{2,1,0:T(8,128)(2,1)S(1)} custom-call(bf16[256,896]{1,0:T(8,128)(2,1)S(1)} %get-tuple-element.16.in_ref, bf16[256,896]{1,0:T(8,128)(2,1)S(1)} %get-tuple-element.17.grad_ref, bf16[3,896,128]{2,1,0:T(8,128)(2,1)S(1)} %collective-permute-done.4.block_ref.refs_1_, bf16[3,896,128]{2,1,0:T(8,128)(2,1)} %collective-permute-done.5.other_ref.refs_5_), custom_call_target="tpu_custom_call" | custom-call | flops 352321536 | bytes 393216 | tf_op jit(solution)/shard_map/pallas_call | solution.py:152
  79.8 2.7 %collective-permute-start.6 = (bf16[3,256,256]{2,1,0:T(8,128)(2,1)S(1)}, bf16[3,256,256]{2,1,0:T(8,128)(2,1)S(1)}, u32[]{:S(2)}, u32[]{:S(2)}) collective-permute-start(bf16[3,256,256]{2,1,0:T(8,128)(2,1)S(1)} %shard_map.77), channel_id=1, source_target_pairs={{0,6},{2,0},{4,2},{6,4},{1,7},{3,1},{5,3},{7,5},{8,14},{10,8},{12,... | collective-permute-start | bytes 1179656 | tf_op jit(solution)/shard_map/ppermute | solution.py:24
  82.5 1.9 %shard_map.78 = bf16[3,256,256]{2,1,0:T(8,128)(2,1)S(1)} custom-call(bf16[256,896]{1,0:T(8,128)(2,1)S(1)} %get-tuple-element.16.in_ref, bf16[256,896]{1,0:T(8,128)(2,1)S(1)} %get-tuple-element.17.grad_ref, bf16[3,896,128]{2,1,0:T(8,128)(2,1)} %collective-permute-done.7.block_ref.refs_3_, bf16[3,896,128]{2,1,0:T(8,128)(2,1)} %collective-permute-done.8.other_ref.refs_7_), custom_call_target="tpu_custom_call" | custom-call | flops 352321536 | bytes 393216 | tf_op jit(solution)/shard_map/pallas_call | solution.py:152
  84.4 2.6 %collective-permute-start.9 = (bf16[3,256,256]{2,1,0:T(8,128)(2,1)S(1)}, bf16[3,256,256]{2,1,0:T(8,128)(2,1)S(1)}, u32[]{:S(2)}, u32[]{:S(2)}) collective-permute-start(bf16[3,256,256]{2,1,0:T(8,128)(2,1)S(1)} %shard_map.78), channel_id=1, source_target_pairs={{0,2},{2,4},{4,6},{6,0},{1,3},{3,5},{5,7},{7,1},{8,10},{10,12},{12... | collective-permute-start | bytes 1179656 | tf_op jit(solution)/shard_map/ppermute | solution.py:24
  88.7 4.0 %collective-permute-done.6.next_ref = bf16[3,256,256]{2,1,0:T(8,128)(2,1)S(1)} collective-permute-done((bf16[3,256,256]{2,1,0:T(8,128)(2,1)S(1)}, bf16[3,256,256]{2,1,0:T(8,128)(2,1)S(1)}, u32[]{:S(2)}, u32[]{:S(2)}) %collective-permute-start.6) | collective-permute-done | bytes 393248 | tf_op jit(solution)/shard_map/ppermute | solution.py:24
  94.4 13.0 %all_to_all.15.grads_ref = bf16[4,2,256,256]{3,2,1,0:T(8,128)(2,1)S(1)} all-to-all(bf16[4,2,256,256]{3,2,1,0:T(8,128)(2,1)S(1)} %shard_map.79), channel_id=1, replica_groups=mesh['z'=16,'x'=4,'y'=4,'c'=2] {'y'}, dimensions={0} | all-to-all | bytes 2097152 | tf_op jit(solution)/shard_map/all_to_all | solution.py:214
  107.3 3.8 %shard_map.80 = bf16[64,4,896]{2,1,0:T(4,128)(2,1)} custom-call(s32[1]{0:T(128)} %bitcast.here_ref, bf16[4,2,256,256]{3,2,1,0:T(8,128)(2,1)S(1)} %all_to_all.15.grads_ref, bf16[3,896,128]{2,1,0:T(8,128)(2,1)S(1)} %get-tuple-element.21.block_ref.refs_0_, bf16[3,896,128]{2,1,0:T(8,128)(2,1)S(1)} %collective-permute-done.4.block_ref.refs_1_, ...), custom_call_target="tpu_custom_call" | custom-call | flops 939524096 | bytes 458752 | tf_op jit(solution)/shard_map/pallas_call | solution.py:152
  111.1 20.4 %all-to-all-start.2 = ((bf16[64,4,896]{2,1,0:T(4,128)(2,1)}), bf16[64,4,896]{2,1,0:T(4,128)(2,1)S(1)}, u32[]{:S(2)}, u32[]{:S(2)}) async-start(bf16[64,4,896]{2,1,0:T(4,128)(2,1)} %shard_map.80), calls=%async_computation.2 | async-start | bytes 917504 | tf_op jit(solution)/shard_map/all_to_all | solution.py:218
  131.9 25.0 %all-to-all-done.2 = bf16[64,4,896]{2,1,0:T(4,128)(2,1)S(1)} async-done(((bf16[64,4,896]{2,1,0:T(4,128)(2,1)}), bf16[64,4,896]{2,1,0:T(4,128)(2,1)S(1)}, u32[]{:S(2)}, u32[]{:S(2)}) %all-to-all-start.2) | async-done | bytes 458784 | tf_op jit(solution)/shard_map/all_to_all | solution.py:218
  157.4 7.7 %all_gather.8 = f32[2,448,128]{2,1,0:T(8,128)S(1)} all-gather(f32[1,448,128]{2,1,0:T(8,128)S(1)} %constant_dynamic-slice_fusion), channel_id=1, replica_groups=mesh['z'=16,'x'=4,'y'=4,'c'=2] {'c'}, dimensions={0}, use_global_device_ids=true | all-gather | bytes 688128 | tf_op jit(solution)/shard_map/all_gather | solution.py:223
  (32 shorter events, 10.5 us)
Async XLA Ops:
  0.0 25.2 %copy-start.5 = (bf16[1,128,3584]{2,1,0:T(8,128)(2,1)S(1)}, bf16[1,128,3584]{2,1,0:T(8,128)(2,1)}, u32[]{:S(2)}) copy-start(bf16[1,128,3584]{2,1,0:T(8,128)(2,1)} %param.13) | copy-start | bytes 2752516
  12.3 59.3 %all-to-all-start = ((bf16[64,8,896]{2,1,0:T(8,128)(2,1)}), bf16[64,8,896]{2,1,0:T(8,128)(2,1)S(1)}, u32[]{:S(2)}, u32[]{:S(2)}) async-start(bf16[64,8,896]{2,1,0:T(8,128)(2,1)} %shard_map.74), calls=%async_computation | async-start | bytes 1835008 | tf_op jit(solution)/shard_map/all_to_all | solution.py:190
  27.9 19.8 %collective-permute-start = (bf16[3,896,128]{2,1,0:T(8,128)(2,1)S(1)}, bf16[3,896,128]{2,1,0:T(8,128)(2,1)S(1)}, u32[]{:S(2)}, u32[]{:S(2)}) collective-permute-start(bf16[3,896,128]{2,1,0:T(8,128)(2,1)S(1)} %get-tuple-element.22), channel_id=1, source_target_pairs={{0,4},{2,6},{4,0},{6,2},{1,5},{3,7},{5,1},{7,3},{8,12},{10,14},{12... | collective-permute-start | bytes 2064392 | tf_op jit(solution)/shard_map/ppermute | solution.py:24
  32.7 30.7 %collective-permute-start.4 = (bf16[3,896,128]{2,1,0:T(8,128)(2,1)S(1)}, bf16[3,896,128]{2,1,0:T(8,128)(2,1)S(1)}, u32[]{:S(2)}, u32[]{:S(2)}) collective-permute-start(bf16[3,896,128]{2,1,0:T(8,128)(2,1)S(1)} %get-tuple-element.20), channel_id=1, source_target_pairs={{0,2},{2,4},{4,6},{6,0},{1,3},{3,5},{5,7},{7,1},{8,10},{10,12},{12... | collective-permute-start | bytes 2064392 | tf_op jit(solution)/shard_map/ppermute | solution.py:24
  35.0 30.8 %collective-permute-start.7 = (bf16[3,896,128]{2,1,0:T(8,128)(2,1)S(1)}, bf16[3,896,128]{2,1,0:T(8,128)(2,1)}, u32[]{:S(2)}, u32[]{:S(2)}) collective-permute-start(bf16[3,896,128]{2,1,0:T(8,128)(2,1)S(1)} %get-tuple-element.19), channel_id=1, source_target_pairs={{0,6},{2,0},{4,2},{6,4},{1,7},{3,1},{5,3},{7,5},{8,14},{10,8},{12,... | collective-permute-start | bytes 2064392 | tf_op jit(solution)/shard_map/ppermute | solution.py:24
  47.6 22.5 %collective-permute-start.1 = (bf16[3,896,128]{2,1,0:T(8,128)(2,1)S(1)}, bf16[3,896,128]{2,1,0:T(8,128)(2,1)S(1)}, u32[]{:S(2)}, u32[]{:S(2)}) collective-permute-start(bf16[3,896,128]{2,1,0:T(8,128)(2,1)S(1)} %collective-permute-done.block_ref.refs_2_), channel_id=1, source_target_pairs={{0,1},{1,0},{2,3},{3,2},{4,5},{5,4},{6,7},{7,6},{8,9},{9,8},{10,11... | collective-permute-start | bytes 2064392 | tf_op jit(solution)/shard_map/ppermute | solution.py:24
  63.4 14.8 %collective-permute-start.5 = (bf16[3,896,128]{2,1,0:T(8,128)(2,1)S(1)}, bf16[3,896,128]{2,1,0:T(8,128)(2,1)}, u32[]{:S(2)}, u32[]{:S(2)}) collective-permute-start(bf16[3,896,128]{2,1,0:T(8,128)(2,1)S(1)} %collective-permute-done.4.block_ref.refs_1_), channel_id=1, source_target_pairs={{0,1},{1,0},{2,3},{3,2},{4,5},{5,4},{6,7},{7,6},{8,9},{9,8},{10,11... | collective-permute-start | bytes 2064392 | tf_op jit(solution)/shard_map/ppermute | solution.py:24
  65.8 16.7 %collective-permute-start.8 = (bf16[3,896,128]{2,1,0:T(8,128)(2,1)}, bf16[3,896,128]{2,1,0:T(8,128)(2,1)}, u32[]{:S(2)}, u32[]{:S(2)}) collective-permute-start(bf16[3,896,128]{2,1,0:T(8,128)(2,1)} %collective-permute-done.7.block_ref.refs_3_), channel_id=1, source_target_pairs={{0,1},{1,0},{2,3},{3,2},{4,5},{5,4},{6,7},{7,6},{8,9},{9,8},{10,11... | collective-permute-start | bytes 2064392 | tf_op jit(solution)/shard_map/ppermute | solution.py:24
  67.7 19.3 %collective-permute-start.2 = (bf16[3,896,128]{2,1,0:T(8,128)(2,1)S(1)}, bf16[3,896,128]{2,1,0:T(8,128)(2,1)}, u32[]{:S(2)}, u32[]{:S(2)}) collective-permute-start(bf16[3,896,128]{2,1,0:T(8,128)(2,1)S(1)} %get-tuple-element.21.block_ref.refs_0_), channel_id=1, source_target_pairs={{0,1},{1,0},{2,3},{3,2},{4,5},{5,4},{6,7},{7,6},{8,9},{9,8},{10,11... | collective-permute-start | bytes 2064392 | tf_op jit(solution)/shard_map/ppermute | solution.py:24
  70.1 0.9 copy-start
  71.6 1.1 copy-start.1
  73.3 13.7 %collective-permute-start.3 = (bf16[3,256,256]{2,1,0:T(8,128)(2,1)S(1)}, bf16[3,256,256]{2,1,0:T(8,128)(2,1)S(1)}, u32[]{:S(2)}, u32[]{:S(2)}) collective-permute-start(bf16[3,256,256]{2,1,0:T(8,128)(2,1)S(1)} %get-tuple-element.18), channel_id=1, source_target_pairs={{0,4},{2,6},{4,0},{6,2},{1,5},{3,7},{5,1},{7,3},{8,12},{10,14},{12... | collective-permute-start | bytes 1179656 | tf_op jit(solution)/shard_map/ppermute | solution.py:24
  79.8 12.9 %collective-permute-start.6 = (bf16[3,256,256]{2,1,0:T(8,128)(2,1)S(1)}, bf16[3,256,256]{2,1,0:T(8,128)(2,1)S(1)}, u32[]{:S(2)}, u32[]{:S(2)}) collective-permute-start(bf16[3,256,256]{2,1,0:T(8,128)(2,1)S(1)} %shard_map.77), channel_id=1, source_target_pairs={{0,6},{2,0},{4,2},{6,4},{1,7},{3,1},{5,3},{7,5},{8,14},{10,8},{12,... | collective-permute-start | bytes 1179656 | tf_op jit(solution)/shard_map/ppermute | solution.py:24
  84.4 9.7 %collective-permute-start.9 = (bf16[3,256,256]{2,1,0:T(8,128)(2,1)S(1)}, bf16[3,256,256]{2,1,0:T(8,128)(2,1)S(1)}, u32[]{:S(2)}, u32[]{:S(2)}) collective-permute-start(bf16[3,256,256]{2,1,0:T(8,128)(2,1)S(1)} %shard_map.78), channel_id=1, source_target_pairs={{0,2},{2,4},{4,6},{6,0},{1,3},{3,5},{5,7},{7,1},{8,10},{10,12},{12... | collective-permute-start | bytes 1179656 | tf_op jit(solution)/shard_map/ppermute | solution.py:24
  88.7 18.6 %copy-start.2 = (bf16[3,896,128]{2,1,0:T(8,128)(2,1)S(1)}, bf16[3,896,128]{2,1,0:T(8,128)(2,1)}, u32[]{:S(2)}) copy-start(bf16[3,896,128]{2,1,0:T(8,128)(2,1)} %copy-done) | copy-start | bytes 2064388
  107.3 24.2 %copy-start.3 = (s32[128,2]{0,1:T(2,128)S(1)}, s32[128,2]{0,1:T(2,128)}, u32[]{:S(2)}) copy-start(s32[128,2]{0,1:T(2,128)} %param.9) | copy-start | bytes 3076
  107.3 24.2 %copy-start.4 = (f32[128,2]{0,1:T(2,128)S(1)}, f32[128,2]{0,1:T(2,128)}, u32[]{:S(2)}) copy-start(f32[128,2]{0,1:T(2,128)} %param.10) | copy-start | bytes 3076
  111.1 45.7 %all-to-all-start.2 = ((bf16[64,4,896]{2,1,0:T(4,128)(2,1)}), bf16[64,4,896]{2,1,0:T(4,128)(2,1)S(1)}, u32[]{:S(2)}, u32[]{:S(2)}) async-start(bf16[64,4,896]{2,1,0:T(4,128)(2,1)} %shard_map.80), calls=%async_computation.2 | async-start | bytes 917504 | tf_op jit(solution)/shard_map/all_to_all | solution.py:218

commit v7 on v6

--- a/solution.py
+++ b/solution.py
@@ -8,6 +8,7 @@
 N_Z, N_X, N_Y, N_C = 16, 4, 4, 2
 GROUP = ("z", "x")
 LOCAL = ("y", "c")
+ORDER = ("x", "z")
 SLOTS = 4
 PAD = 16
 BF16 = jnp.bfloat16
@@ -34,7 +35,8 @@
 
 def routing(ids, experts):
     tokens = ids.shape[1]
-    expert = iota(experts, tokens, 0).astype(ids.dtype)
+    place = iota(experts, tokens, 0)
+    expert = (place % N_Z * N_X + place // N_Z).astype(ids.dtype)
     first = ids[0:1, :] == expert
     second = ids[1:2, :] == expert
     named = ones_where(first | second)
@@ -187,7 +189,7 @@
     weights = call(weight_kernel, [(rows, 2 * tokens)], (core_ref, expert_ids.T, gate_probs.T), rows * tokens * 256)
 
     send, w_gate, w_up, w_down = lax.optimization_barrier((send, w_gate, w_up, w_down))
-    recv = lax.all_to_all(send, GROUP, split_axis=0, concat_axis=0, tiled=True)
+    recv = lax.all_to_all(send, ORDER, split_axis=0, concat_axis=0, tiled=True)
 
     mats = jnp.stack([w_gate[0], w_up[0], w_down[0].T])
 
@@ -215,7 +217,7 @@
     back = call(
         back_kernel, [(groups, SLOTS, chip)], [here_ref, grads, *blocks, other_0, other_1, other_2, other_3], 8 * product
     )
-    returned = lax.all_to_all(back, GROUP, split_axis=0, concat_axis=0, tiled=True).reshape(rows, chip)
+    returned = lax.all_to_all(back, ORDER, split_axis=0, concat_axis=0, tiled=True).reshape(rows, chip)
     mixed = dot(returned, weights, 0, 0)
     mixed = (mixed[:, :tokens] + mixed[:, tokens:]).reshape(N_C, width, tokens)
     mine = lax.dynamic_index_in_dim(mixed, core, 0, keepdims=False)

time: 167 us -> 165 us (0.988)
    all_to_all x1, blocking collectives: 13 us -> 14.7 us  [shards(): grads = lax.all_to_all(grads, 'y', split_axis=0, concat_axis=0, tiled=True)]
  transfers between devices with their start and end apart: 12 -> 12, of which waited for: 6 -> 5; matrix products, arithmetic and copies ran while one was open for 2% -> 2% of each run, Pallas kernels for 4% -> 4%
where the time goes in v7:
time: 165 us
  starting transfers between devices  64.8 us (39%)
  waiting for transfers between devices  49.8 us (30%)
  blocking collectives  30.2 us (18%)
  Pallas kernels  13.6 us (8%)
  local copies, waits for them, and re-layouts  2.9 us (2%)
  other arithmetic  2.47 us (1%)
    ppermute x10, starting transfers between devices, shift(): lax.ppermute(value, axis, [(i, (i + step) % size) for i in range(size)])  32.7 us
    ppermute x10, waiting for transfers between devices, shift(): lax.ppermute(value, axis, [(i, (i + step) % size) for i in range(size)])  25.2 us
    all_to_all x1, waiting for transfers between devices, shards(): lax.all_to_all(back, ORDER, split_axis=0, concat_axis=0, tiled=True)  24.6 us
    all_to_all x1, starting transfers between devices, shards(): lax.all_to_all(back, ORDER, split_axis=0, concat_axis=0, tiled=True)  19.2 us
    all_to_all x1, blocking collectives, shards(): grads = lax.all_to_all(grads, 'y', split_axis=0, concat_axis=0, tiled=True)  14.7 us
    all_to_all x1, starting transfers between devices, shards(): recv = lax.all_to_all(send, ORDER, split_axis=0, concat_axis=0, tiled=True)  12.9 us
    pallas_call x8, Pallas kernels, call(): pl.pallas_call(kernel, out_shape=[jax.ShapeDtypeStruct(shape, kind) for s...  11.8 us
    all_gather x1, blocking collectives, shards(): lax.all_gather(call_pack(expert_ids.T, layer_input.T, out_grad.T), 'c', a...  8.86 us
  transfers between devices with their start and end apart: 12, of which 5 were waited for; matrix products, arithmetic and copies ran while one was open for 2% of the time, Pallas kernels for 4%

profile of v7, /device:TPU:1, one launch (start us, length us, event | category | flops | bytes accessed | tf_op | source)
XLA Modules:
  0.0 164.5 jit_solution(6558694691292395347)
XLA Ops:
  0.0 1.8 %shard_map.73 = bf16[464,256]{1,0:T(8,128)(2,1)} custom-call(s32[2,128]{1,0:T(2,128)} %bitcast.18, bf16[448,128]{1,0:T(8,128)(2,1)} %bitcast.24, bf16[448,128]{1,0:T(8,128)(2,1)} %bitcast.25), custom_call_target="tpu_custom_call" | custom-call | bytes 458752 | tf_op jit(solution)/shard_map/pallas_call | solution.py:167
  1.8 8.9 %all_gather.7.both_ref = bf16[928,256]{1,0:T(8,128)(2,1)S(1)} all-gather(bf16[464,256]{1,0:T(8,128)(2,1)} %shard_map.73), channel_id=1, replica_groups=mesh['z'=16,'x'=4,'y'=4,'c'=2] {'c'}, dimensions={0}, use_global_device_ids=true | all-gather | bytes 712704 | tf_op jit(solution)/shard_map/all_gather | solution.py:187
  12.3 12.9 %all-to-all-start = ((bf16[64,8,896]{2,1,0:T(8,128)(2,1)}), bf16[64,8,896]{2,1,0:T(8,128)(2,1)S(1)}, u32[]{:S(2)}, u32[]{:S(2)}) async-start(bf16[64,8,896]{2,1,0:T(8,128)(2,1)} %shard_map.74), calls=%async_computation | async-start | bytes 1835008 | tf_op jit(solution)/shard_map/all_to_all | solution.py:192
  25.9 1.8 %pad_maximum_fusion = bf16[3,3584,128]{2,1,0:T(8,128)(2,1)S(1)} fusion(bf16[1,3584,128]{2,1,0:T(8,128)(2,1)S(1)} %bitcast.21, bf16[1,3584,128]{2,1,0:T(8,128)(2,1)} %param.12, bf16[1,3584,128]{2,1,0:T(8,128)(2,1)} %param.11), kind=kLoop, calls=%fused_computation | loop fusion | flops 2752512 | bytes 5505024 | tf_op jit(solution)/shard_map/stack | solution.py:194
  27.9 4.8 %collective-permute-start = (bf16[3,896,128]{2,1,0:T(8,128)(2,1)S(1)}, bf16[3,896,128]{2,1,0:T(8,128)(2,1)S(1)}, u32[]{:S(2)}, u32[]{:S(2)}) collective-permute-start(bf16[3,896,128]{2,1,0:T(8,128)(2,1)S(1)} %get-tuple-element.22), channel_id=1, source_target_pairs={{0,4},{2,6},{4,0},{6,2},{1,5},{3,7},{5,1},{7,3},{8,12},{10,14},{12... | collective-permute-start | bytes 2064392 | tf_op jit(solution)/shard_map/ppermute | solution.py:25
  32.7 2.3 %collective-permute-start.4 = (bf16[3,896,128]{2,1,0:T(8,128)(2,1)S(1)}, bf16[3,896,128]{2,1,0:T(8,128)(2,1)S(1)}, u32[]{:S(2)}, u32[]{:S(2)}) collective-permute-start(bf16[3,896,128]{2,1,0:T(8,128)(2,1)S(1)} %get-tuple-element.20), channel_id=1, source_target_pairs={{0,2},{2,4},{4,6},{6,0},{1,3},{3,5},{5,7},{7,1},{8,10},{10,12},{12... | collective-permute-start | bytes 2064392 | tf_op jit(solution)/shard_map/ppermute | solution.py:25
  35.0 4.2 %collective-permute-start.7 = (bf16[3,896,128]{2,1,0:T(8,128)(2,1)S(1)}, bf16[3,896,128]{2,1,0:T(8,128)(2,1)}, u32[]{:S(2)}, u32[]{:S(2)}) collective-permute-start(bf16[3,896,128]{2,1,0:T(8,128)(2,1)S(1)} %get-tuple-element.19), channel_id=1, source_target_pairs={{0,6},{2,0},{4,2},{6,4},{1,7},{3,1},{5,3},{7,5},{8,14},{10,8},{12,... | collective-permute-start | bytes 2064392 | tf_op jit(solution)/shard_map/ppermute | solution.py:25
  39.2 8.4 %collective-permute-done.block_ref.refs_2_ = bf16[3,896,128]{2,1,0:T(8,128)(2,1)S(1)} collective-permute-done((bf16[3,896,128]{2,1,0:T(8,128)(2,1)S(1)}, bf16[3,896,128]{2,1,0:T(8,128)(2,1)S(1)}, u32[]{:S(2)}, u32[]{:S(2)}) %collective-permute-start) | collective-permute-done | bytes 688160 | tf_op jit(solution)/shard_map/ppermute | solution.py:25
  47.6 4.6 %collective-permute-start.1 = (bf16[3,896,128]{2,1,0:T(8,128)(2,1)S(1)}, bf16[3,896,128]{2,1,0:T(8,128)(2,1)S(1)}, u32[]{:S(2)}, u32[]{:S(2)}) collective-permute-start(bf16[3,896,128]{2,1,0:T(8,128)(2,1)S(1)} %collective-permute-done.block_ref.refs_2_), channel_id=1, source_target_pairs={{0,1},{1,0},{2,3},{3,2},{4,5},{5,4},{6,7},{7,6},{8,9},{9,8},{10,11... | collective-permute-start | bytes 2064392 | tf_op jit(solution)/shard_map/ppermute | solution.py:25
  52.2 11.2 %collective-permute-done.4.block_ref.refs_1_ = bf16[3,896,128]{2,1,0:T(8,128)(2,1)S(1)} collective-permute-done((bf16[3,896,128]{2,1,0:T(8,128)(2,1)S(1)}, bf16[3,896,128]{2,1,0:T(8,128)(2,1)S(1)}, u32[]{:S(2)}, u32[]{:S(2)}) %collective-permute-start.4) | collective-permute-done | bytes 688160 | tf_op jit(solution)/shard_map/ppermute | solution.py:25
  63.4 2.4 %collective-permute-start.5 = (bf16[3,896,128]{2,1,0:T(8,128)(2,1)S(1)}, bf16[3,896,128]{2,1,0:T(8,128)(2,1)}, u32[]{:S(2)}, u32[]{:S(2)}) collective-permute-start(bf16[3,896,128]{2,1,0:T(8,128)(2,1)S(1)} %collective-permute-done.4.block_ref.refs_1_), channel_id=1, source_target_pairs={{0,1},{1,0},{2,3},{3,2},{4,5},{5,4},{6,7},{7,6},{8,9},{9,8},{10,11... | collective-permute-start | bytes 2064392 | tf_op jit(solution)/shard_map/ppermute | solution.py:25
  65.8 1.9 %collective-permute-start.8 = (bf16[3,896,128]{2,1,0:T(8,128)(2,1)}, bf16[3,896,128]{2,1,0:T(8,128)(2,1)}, u32[]{:S(2)}, u32[]{:S(2)}) collective-permute-start(bf16[3,896,128]{2,1,0:T(8,128)(2,1)} %collective-permute-done.7.block_ref.refs_3_), channel_id=1, source_target_pairs={{0,1},{1,0},{2,3},{3,2},{4,5},{5,4},{6,7},{7,6},{8,9},{9,8},{10,11... | collective-permute-start | bytes 2064392 | tf_op jit(solution)/shard_map/ppermute | solution.py:25
  67.7 2.4 %collective-permute-start.2 = (bf16[3,896,128]{2,1,0:T(8,128)(2,1)S(1)}, bf16[3,896,128]{2,1,0:T(8,128)(2,1)}, u32[]{:S(2)}, u32[]{:S(2)}) collective-permute-start(bf16[3,896,128]{2,1,0:T(8,128)(2,1)S(1)} %get-tuple-element.21.block_ref.refs_0_), channel_id=1, source_target_pairs={{0,1},{1,0},{2,3},{3,2},{4,5},{5,4},{6,7},{7,6},{8,9},{9,8},{10,11... | collective-permute-start | bytes 2064392 | tf_op jit(solution)/shard_map/ppermute | solution.py:25
  72.7 4.8 %collective-permute-start.3 = (bf16[3,256,256]{2,1,0:T(8,128)(2,1)S(1)}, bf16[3,256,256]{2,1,0:T(8,128)(2,1)S(1)}, u32[]{:S(2)}, u32[]{:S(2)}) collective-permute-start(bf16[3,256,256]{2,1,0:T(8,128)(2,1)S(1)} %get-tuple-element.18), channel_id=1, source_target_pairs={{0,4},{2,6},{4,0},{6,2},{1,5},{3,7},{5,1},{7,3},{8,12},{10,14},{12... | collective-permute-start | bytes 1179656 | tf_op jit(solution)/shard_map/ppermute | solution.py:25
  79.2 2.8 %collective-permute-start.6 = (bf16[3,256,256]{2,1,0:T(8,128)(2,1)S(1)}, bf16[3,256,256]{2,1,0:T(8,128)(2,1)S(1)}, u32[]{:S(2)}, u32[]{:S(2)}) collective-permute-start(bf16[3,256,256]{2,1,0:T(8,128)(2,1)S(1)} %shard_map.77), channel_id=1, source_target_pairs={{0,6},{2,0},{4,2},{6,4},{1,7},{3,1},{5,3},{7,5},{8,14},{10,8},{12,... | collective-permute-start | bytes 1179656 | tf_op jit(solution)/shard_map/ppermute | solution.py:25
  82.1 1.9 %shard_map.78 = bf16[3,256,256]{2,1,0:T(8,128)(2,1)S(1)} custom-call(bf16[256,896]{1,0:T(8,128)(2,1)S(1)} %get-tuple-element.16.in_ref, bf16[256,896]{1,0:T(8,128)(2,1)S(1)} %get-tuple-element.17.grad_ref, bf16[3,896,128]{2,1,0:T(8,128)(2,1)} %collective-permute-done.7.block_ref.refs_3_, bf16[3,896,128]{2,1,0:T(8,128)(2,1)} %collective-permute-done.8.other_ref.refs_7_), custom_call_target="tpu_custom_call" | custom-call | flops 352321536 | bytes 393216 | tf_op jit(solution)/shard_map/pallas_call | solution.py:154
  84.0 2.4 %collective-permute-start.9 = (bf16[3,256,256]{2,1,0:T(8,128)(2,1)S(1)}, bf16[3,256,256]{2,1,0:T(8,128)(2,1)S(1)}, u32[]{:S(2)}, u32[]{:S(2)}) collective-permute-start(bf16[3,256,256]{2,1,0:T(8,128)(2,1)S(1)} %shard_map.78), channel_id=1, source_target_pairs={{0,2},{2,4},{4,6},{6,0},{1,3},{3,5},{5,7},{7,1},{8,10},{10,12},{12... | collective-permute-start | bytes 1179656 | tf_op jit(solution)/shard_map/ppermute | solution.py:25
  86.4 1.7 %shard_map.76.own_ref = f32[3,256,256]{2,1,0:T(8,128)S(1)} custom-call(bf16[256,896]{1,0:T(8,128)(2,1)S(1)} %get-tuple-element.16.in_ref, bf16[256,896]{1,0:T(8,128)(2,1)S(1)} %get-tuple-element.17.grad_ref, bf16[3,896,128]{2,1,0:T(8,128)(2,1)S(1)} %get-tuple-element.21.block_ref.refs_0_, bf16[3,896,128]{2,1,0:T(8,128)(2,1)} %collective-permute-done.2.other_ref.refs_4_, ...), custom_call_target="tpu_custom_call" | custom-call | flops 352321536 | bytes 393216 | tf_op jit(solution)/shard_map/pallas_call | solution.py:154
  88.1 4.6 %collective-permute-done.6.next_ref = bf16[3,256,256]{2,1,0:T(8,128)(2,1)S(1)} collective-permute-done((bf16[3,256,256]{2,1,0:T(8,128)(2,1)S(1)}, bf16[3,256,256]{2,1,0:T(8,128)(2,1)S(1)}, u32[]{:S(2)}, u32[]{:S(2)}) %collective-permute-start.6) | collective-permute-done | bytes 393248 | tf_op jit(solution)/shard_map/ppermute | solution.py:25
  93.9 14.7 %all_to_all.15.grads_ref = bf16[4,2,256,256]{3,2,1,0:T(8,128)(2,1)S(1)} all-to-all(bf16[4,2,256,256]{3,2,1,0:T(8,128)(2,1)S(1)} %shard_map.79), channel_id=1, replica_groups=mesh['z'=16,'x'=4,'y'=4,'c'=2] {'y'}, dimensions={0} | all-to-all | bytes 2097152 | tf_op jit(solution)/shard_map/all_to_all | solution.py:216
  108.6 3.8 %shard_map.80 = bf16[64,4,896]{2,1,0:T(4,128)(2,1)} custom-call(s32[1]{0:T(128)} %bitcast.here_ref, bf16[4,2,256,256]{3,2,1,0:T(8,128)(2,1)S(1)} %all_to_all.15.grads_ref, bf16[3,896,128]{2,1,0:T(8,128)(2,1)S(1)} %get-tuple-element.21.block_ref.refs_0_, bf16[3,896,128]{2,1,0:T(8,128)(2,1)S(1)} %collective-permute-done.4.block_ref.refs_1_, ...), custom_call_target="tpu_custom_call" | custom-call | flops 939524096 | bytes 458752 | tf_op jit(solution)/shard_map/pallas_call | solution.py:154
  112.4 19.2 %all-to-all-start.2 = ((bf16[64,4,896]{2,1,0:T(4,128)(2,1)}), bf16[64,4,896]{2,1,0:T(4,128)(2,1)S(1)}, u32[]{:S(2)}, u32[]{:S(2)}) async-start(bf16[64,4,896]{2,1,0:T(4,128)(2,1)} %shard_map.80), calls=%async_computation.2 | async-start | bytes 917504 | tf_op jit(solution)/shard_map/all_to_all | solution.py:220
  132.0 24.6 %all-to-all-done.2 = bf16[64,4,896]{2,1,0:T(4,128)(2,1)S(1)} async-done(((bf16[64,4,896]{2,1,0:T(4,128)(2,1)}), bf16[64,4,896]{2,1,0:T(4,128)(2,1)S(1)}, u32[]{:S(2)}, u32[]{:S(2)}) %all-to-all-start.2) | async-done | bytes 458784 | tf_op jit(solution)/shard_map/all_to_all | solution.py:220
  157.2 6.7 %all_gather.8 = f32[2,448,128]{2,1,0:T(8,128)S(1)} all-gather(f32[1,448,128]{2,1,0:T(8,128)S(1)} %constant_dynamic-slice_fusion), channel_id=1, replica_groups=mesh['z'=16,'x'=4,'y'=4,'c'=2] {'c'}, dimensions={0}, use_global_device_ids=true | all-gather | bytes 688128 | tf_op jit(solution)/shard_map/all_gather | solution.py:225
  (32 shorter events, 9.4 us)
Async XLA Ops:
  0.0 25.2 %copy-start.5 = (bf16[1,128,3584]{2,1,0:T(8,128)(2,1)S(1)}, bf16[1,128,3584]{2,1,0:T(8,128)(2,1)}, u32[]{:S(2)}) copy-start(bf16[1,128,3584]{2,1,0:T(8,128)(2,1)} %param.13) | copy-start | bytes 2752516
  12.3 58.7 %all-to-all-start = ((bf16[64,8,896]{2,1,0:T(8,128)(2,1)}), bf16[64,8,896]{2,1,0:T(8,128)(2,1)S(1)}, u32[]{:S(2)}, u32[]{:S(2)}) async-start(bf16[64,8,896]{2,1,0:T(8,128)(2,1)} %shard_map.74), calls=%async_computation | async-start | bytes 1835008 | tf_op jit(solution)/shard_map/all_to_all | solution.py:192
  27.9 19.8 %collective-permute-start = (bf16[3,896,128]{2,1,0:T(8,128)(2,1)S(1)}, bf16[3,896,128]{2,1,0:T(8,128)(2,1)S(1)}, u32[]{:S(2)}, u32[]{:S(2)}) collective-permute-start(bf16[3,896,128]{2,1,0:T(8,128)(2,1)S(1)} %get-tuple-element.22), channel_id=1, source_target_pairs={{0,4},{2,6},{4,0},{6,2},{1,5},{3,7},{5,1},{7,3},{8,12},{10,14},{12... | collective-permute-start | bytes 2064392 | tf_op jit(solution)/shard_map/ppermute | solution.py:25
  32.7 30.7 %collective-permute-start.4 = (bf16[3,896,128]{2,1,0:T(8,128)(2,1)S(1)}, bf16[3,896,128]{2,1,0:T(8,128)(2,1)S(1)}, u32[]{:S(2)}, u32[]{:S(2)}) collective-permute-start(bf16[3,896,128]{2,1,0:T(8,128)(2,1)S(1)} %get-tuple-element.20), channel_id=1, source_target_pairs={{0,2},{2,4},{4,6},{6,0},{1,3},{3,5},{5,7},{7,1},{8,10},{10,12},{12... | collective-permute-start | bytes 2064392 | tf_op jit(solution)/shard_map/ppermute | solution.py:25
  35.0 30.8 %collective-permute-start.7 = (bf16[3,896,128]{2,1,0:T(8,128)(2,1)S(1)}, bf16[3,896,128]{2,1,0:T(8,128)(2,1)}, u32[]{:S(2)}, u32[]{:S(2)}) collective-permute-start(bf16[3,896,128]{2,1,0:T(8,128)(2,1)S(1)} %get-tuple-element.19), channel_id=1, source_target_pairs={{0,6},{2,0},{4,2},{6,4},{1,7},{3,1},{5,3},{7,5},{8,14},{10,8},{12,... | collective-permute-start | bytes 2064392 | tf_op jit(solution)/shard_map/ppermute | solution.py:25
  47.6 22.5 %collective-permute-start.1 = (bf16[3,896,128]{2,1,0:T(8,128)(2,1)S(1)}, bf16[3,896,128]{2,1,0:T(8,128)(2,1)S(1)}, u32[]{:S(2)}, u32[]{:S(2)}) collective-permute-start(bf16[3,896,128]{2,1,0:T(8,128)(2,1)S(1)} %collective-permute-done.block_ref.refs_2_), channel_id=1, source_target_pairs={{0,1},{1,0},{2,3},{3,2},{4,5},{5,4},{6,7},{7,6},{8,9},{9,8},{10,11... | collective-permute-start | bytes 2064392 | tf_op jit(solution)/shard_map/ppermute | solution.py:25
  63.4 14.2 %collective-permute-start.5 = (bf16[3,896,128]{2,1,0:T(8,128)(2,1)S(1)}, bf16[3,896,128]{2,1,0:T(8,128)(2,1)}, u32[]{:S(2)}, u32[]{:S(2)}) collective-permute-start(bf16[3,896,128]{2,1,0:T(8,128)(2,1)S(1)} %collective-permute-done.4.block_ref.refs_1_), channel_id=1, source_target_pairs={{0,1},{1,0},{2,3},{3,2},{4,5},{5,4},{6,7},{7,6},{8,9},{9,8},{10,11... | collective-permute-start | bytes 2064392 | tf_op jit(solution)/shard_map/ppermute | solution.py:25
  65.8 16.3 %collective-permute-start.8 = (bf16[3,896,128]{2,1,0:T(8,128)(2,1)}, bf16[3,896,128]{2,1,0:T(8,128)(2,1)}, u32[]{:S(2)}, u32[]{:S(2)}) collective-permute-start(bf16[3,896,128]{2,1,0:T(8,128)(2,1)} %collective-permute-done.7.block_ref.refs_3_), channel_id=1, source_target_pairs={{0,1},{1,0},{2,3},{3,2},{4,5},{5,4},{6,7},{7,6},{8,9},{9,8},{10,11... | collective-permute-start | bytes 2064392 | tf_op jit(solution)/shard_map/ppermute | solution.py:25
  67.7 18.7 %collective-permute-start.2 = (bf16[3,896,128]{2,1,0:T(8,128)(2,1)S(1)}, bf16[3,896,128]{2,1,0:T(8,128)(2,1)}, u32[]{:S(2)}, u32[]{:S(2)}) collective-permute-start(bf16[3,896,128]{2,1,0:T(8,128)(2,1)S(1)} %get-tuple-element.21.block_ref.refs_0_), channel_id=1, source_target_pairs={{0,1},{1,0},{2,3},{3,2},{4,5},{5,4},{6,7},{7,6},{8,9},{9,8},{10,11... | collective-permute-start | bytes 2064392 | tf_op jit(solution)/shard_map/ppermute | solution.py:25
  70.1 0.9 copy-start
  71.0 1.1 copy-start.1
  72.7 13.7 %collective-permute-start.3 = (bf16[3,256,256]{2,1,0:T(8,128)(2,1)S(1)}, bf16[3,256,256]{2,1,0:T(8,128)(2,1)S(1)}, u32[]{:S(2)}, u32[]{:S(2)}) collective-permute-start(bf16[3,256,256]{2,1,0:T(8,128)(2,1)S(1)} %get-tuple-element.18), channel_id=1, source_target_pairs={{0,4},{2,6},{4,0},{6,2},{1,5},{3,7},{5,1},{7,3},{8,12},{10,14},{12... | collective-permute-start | bytes 1179656 | tf_op jit(solution)/shard_map/ppermute | solution.py:25
  79.2 13.5 %collective-permute-start.6 = (bf16[3,256,256]{2,1,0:T(8,128)(2,1)S(1)}, bf16[3,256,256]{2,1,0:T(8,128)(2,1)S(1)}, u32[]{:S(2)}, u32[]{:S(2)}) collective-permute-start(bf16[3,256,256]{2,1,0:T(8,128)(2,1)S(1)} %shard_map.77), channel_id=1, source_target_pairs={{0,6},{2,0},{4,2},{6,4},{1,7},{3,1},{5,3},{7,5},{8,14},{10,8},{12,... | collective-permute-start | bytes 1179656 | tf_op jit(solution)/shard_map/ppermute | solution.py:25
  84.0 9.7 %collective-permute-start.9 = (bf16[3,256,256]{2,1,0:T(8,128)(2,1)S(1)}, bf16[3,256,256]{2,1,0:T(8,128)(2,1)S(1)}, u32[]{:S(2)}, u32[]{:S(2)}) collective-permute-start(bf16[3,256,256]{2,1,0:T(8,128)(2,1)S(1)} %shard_map.78), channel_id=1, source_target_pairs={{0,2},{2,4},{4,6},{6,0},{1,3},{3,5},{5,7},{7,1},{8,10},{10,12},{12... | collective-permute-start | bytes 1179656 | tf_op jit(solution)/shard_map/ppermute | solution.py:25
  88.1 20.5 %copy-start.2 = (bf16[3,896,128]{2,1,0:T(8,128)(2,1)S(1)}, bf16[3,896,128]{2,1,0:T(8,128)(2,1)}, u32[]{:S(2)}) copy-start(bf16[3,896,128]{2,1,0:T(8,128)(2,1)} %copy-done) | copy-start | bytes 2064388
  108.6 23.0 %copy-start.3 = (s32[128,2]{0,1:T(2,128)S(1)}, s32[128,2]{0,1:T(2,128)}, u32[]{:S(2)}) copy-start(s32[128,2]{0,1:T(2,128)} %param.9) | copy-start | bytes 3076
  108.6 23.0 %copy-start.4 = (f32[128,2]{0,1:T(2,128)S(1)}, f32[128,2]{0,1:T(2,128)}, u32[]{:S(2)}) copy-start(f32[128,2]{0,1:T(2,128)} %param.10) | copy-start | bytes 3076
  112.4 44.2 %all-to-all-start.2 = ((bf16[64,4,896]{2,1,0:T(4,128)(2,1)}), bf16[64,4,896]{2,1,0:T(4,128)(2,1)S(1)}, u32[]{:S(2)}, u32[]{:S(2)}) async-start(bf16[64,4,896]{2,1,0:T(4,128)(2,1)} %shard_map.80), calls=%async_computation.2 | async-start | bytes 917504 | tf_op jit(solution)/shard_map/all_to_all | solution.py:220

commit v8 on v7

--- a/solution.py
+++ b/solution.py
@@ -127,17 +127,23 @@
     sigmoid_gate = jax.nn.sigmoid(gate_act)
     gate_grad = hidden_grad * up_act * sigmoid_gate * (1.0 + gate_act * (1.0 - sigmoid_gate))
     up_grad = hidden_grad * gate_act * sigmoid_gate
-    for y in range(N_Y):
-        grads_ref[y, 0] = gate_grad.astype(BF16)
-        grads_ref[y, 1] = up_grad.astype(BF16)
-
-
-def back_kernel(here_ref, grads_ref, *refs):
-    blocks, others, out_ref = refs[:N_Y], refs[N_Y:-1], refs[-1]
-    origins = [lax.rem(here_ref[0] + N_Y - d, N_Y) for d in range(N_Y)]
-    left = jnp.concatenate([grads_ref[origins[d], m] for d in range(N_Y) for m in range(2)], axis=1)
-    right = jnp.concatenate([units_of(blocks[d], others[d], m) for d in range(N_Y) for m in range(2)], axis=1)
-    total = dot(left, right, 1, 1)
+    grads_ref[0] = gate_grad.astype(BF16)
+    grads_ref[1] = up_grad.astype(BF16)
+
+
+def product_back(grads, blocks, others):
+    left = jnp.concatenate([grad[m] for grad in grads for m in range(2)], axis=1)
+    right = jnp.concatenate([units_of(b, o, m) for b, o in zip(blocks, others) for m in range(2)], axis=1)
+    return dot(left, right, 1, 1)
+
+
+def early_kernel(own_ref, arrived_ref, block_ref, far_ref, other_ref, far_other_ref, total_ref):
+    total_ref[...] = product_back((own_ref, arrived_ref), (block_ref, far_ref), (other_ref, far_other_ref))
+
+
+def back_kernel(total_ref, *refs):
+    grads, blocks, others, out_ref = refs[:2], refs[2:4], refs[4:6], refs[6]
+    total = total_ref[...] + product_back(grads, blocks, others)
     out_ref[...] = total.reshape(out_ref.shape).astype(BF16)
 
 
@@ -199,7 +205,6 @@
     blocks = [part(0)] + [shift(part(d), "y", d, N_Y) for d in range(1, N_Y)]
     other_0, other_1, other_2, other_3 = (shift(block, "c", 1, N_C) for block in blocks)
 
-    here_ref = here.astype(jnp.int32).reshape(1)
     units = N_C * w_gate.shape[2]
     shape = (3, rows, units)
     product = 2 * rows * chip * units
@@ -212,10 +217,16 @@
     part_3 = call(next_kernel, [shape], [rows_in, rows_grad, blocks[3], other_3], 3 * product)
     part_3 = shift(part_3, "y", -3, N_Y)
     part_0 = call(own_kernel, [shape], [rows_in, rows_grad, blocks[0], other_0, arrived], 3 * product, F32)
-    grads = call(hidden_kernel, [(N_Y, 2, rows, units)], [part_0, part_1, part_3], 40 * rows * units)
-    grads = lax.all_to_all(grads, "y", split_axis=0, concat_axis=0, tiled=True)
+    grads = call(hidden_kernel, [(2, rows, units)], [part_0, part_1, part_3], 40 * rows * units)
+    grads_2, grads_1, grads_3 = (shift(grads, "y", d, N_Y) for d in (2, 1, 3))
+    total = call(
+        early_kernel, [(rows, chip)], [grads, grads_2, blocks[0], blocks[2], other_0, other_2], 4 * product, F32
+    )
     back = call(
-        back_kernel, [(groups, SLOTS, chip)], [here_ref, grads, *blocks, other_0, other_1, other_2, other_3], 8 * product
+        back_kernel,
+        [(groups, SLOTS, chip)],
+        [total, grads_1, grads_3, blocks[1], blocks[3], other_1, other_3],
+        4 * product,
     )
     returned = lax.all_to_all(back, ORDER, split_axis=0, concat_axis=0, tiled=True).reshape(rows, chip)
     mixed = dot(returned, weights, 0, 0)

time: 165 us -> 167 us (1.012)
  blocking collectives: 30.2 us -> 13.8 us
  starting transfers between devices: 64.8 us -> 75.7 us
  waiting for transfers between devices: 49.8 us -> 54 us
  local copies, waits for them, and re-layouts: 2.9 us -> 4.86 us
    all_to_all x1 -> x0, blocking collectives: 14.7 us -> none  [shards(): grads = lax.all_to_all(grads, 'y', split_axis=0, concat_axis=0, tiled=True)]
    ppermute x10 -> x13, starting transfers between devices: 32.7 us -> 42.5 us  [shift(): lax.ppermute(value, axis, [(i, (i + step) % size) for i in range(size)])]
    ppermute x10 -> x13, waiting for transfers between devices: 25.2 us -> 27.5 us  [shift(): lax.ppermute(value, axis, [(i, (i + step) % size) for i in range(size)])]
    unnamed x12 -> x18, local copies, waits for them, and re-layouts: 1.96 us -> 3.92 us
    all_to_all x1, waiting for transfers between devices: 24.6 us -> 26.5 us  [shards(): lax.all_to_all(back, ORDER, split_axis=0, concat_axis=0, tiled=True)]
    all_gather x1, blocking collectives: 6.7 us -> 4.89 us  [shards(): sent = lax.all_gather(sibling, 'c', axis=0)]
    pallas_call x8 -> x9, Pallas kernels: 11.8 us -> 12.5 us  [call(): pl.pallas_call(kernel, out_shape=[jax.ShapeDtypeStruct(shape, kind) for s...]
  transfers between devices with their start and end apart: 12 -> 15, of which waited for: 5 -> 7; matrix products, arithmetic and copies ran while one was open for 2% -> 2% of each run, Pallas kernels for 4% -> 5%
where the time goes in v8:
time: 167 us; the launch traced here: 166 us
  starting transfers between devices  75.7 us (45%)
  waiting for transfers between devices  54 us (32%)
  Pallas kernels  14.3 us (9%)
  blocking collectives  13.8 us (8%)
  local copies, waits for them, and re-layouts  4.86 us (3%)
  other arithmetic  2.47 us (1%)
    ppermute x13, starting transfers between devices, shift(): lax.ppermute(value, axis, [(i, (i + step) % size) for i in range(size)])  42.5 us
    ppermute x13, waiting for transfers between devices, shift(): lax.ppermute(value, axis, [(i, (i + step) % size) for i in range(size)])  27.5 us
    all_to_all x1, waiting for transfers between devices, shards(): lax.all_to_all(back, ORDER, split_axis=0, concat_axis=0, tiled=True)  26.5 us
    all_to_all x1, starting transfers between devices, shards(): lax.all_to_all(back, ORDER, split_axis=0, concat_axis=0, tiled=True)  20.4 us
    all_to_all x1, starting transfers between devices, shards(): recv = lax.all_to_all(send, ORDER, split_axis=0, concat_axis=0, tiled=True)  12.9 us
    pallas_call x9, Pallas kernels, call(): pl.pallas_call(kernel, out_shape=[jax.ShapeDtypeStruct(shape, kind) for s...  12.5 us
    all_gather x1, blocking collectives, shards(): lax.all_gather(call_pack(expert_ids.T, layer_input.T, out_grad.T), 'c', a...  8.86 us
    all_gather x1, blocking collectives, shards(): sent = lax.all_gather(sibling, 'c', axis=0)  4.89 us
  transfers between devices with their start and end apart: 15, of which 7 were waited for; matrix products, arithmetic and copies ran while one was open for 2% of the time, Pallas kernels for 5%

profile of v8, /device:TPU:1, one launch (start us, length us, event | category | flops | bytes accessed | tf_op | source)
XLA Modules:
  0.0 165.9 jit_solution(17899561288462043900)
XLA Ops:
  1.8 8.9 %all_gather.7.both_ref = bf16[928,256]{1,0:T(8,128)(2,1)S(1)} all-gather(bf16[464,256]{1,0:T(8,128)(2,1)} %shard_map.73), channel_id=1, replica_groups=mesh['z'=16,'x'=4,'y'=4,'c'=2] {'c'}, dimensions={0}, use_global_device_ids=true | all-gather | bytes 712704 | tf_op jit(solution)/shard_map/all_gather | solution.py:193
  12.3 12.9 %all-to-all-start = ((bf16[64,8,896]{2,1,0:T(8,128)(2,1)}), bf16[64,8,896]{2,1,0:T(8,128)(2,1)S(1)}, u32[]{:S(2)}, u32[]{:S(2)}) async-start(bf16[64,8,896]{2,1,0:T(8,128)(2,1)} %shard_map.74), calls=%async_computation | async-start | bytes 1835008 | tf_op jit(solution)/shard_map/all_to_all | solution.py:198
  27.9 4.8 %collective-permute-start = (bf16[3,896,128]{2,1,0:T(8,128)(2,1)S(1)}, bf16[3,896,128]{2,1,0:T(8,128)(2,1)S(1)}, u32[]{:S(2)}, u32[]{:S(2)}) collective-permute-start(bf16[3,896,128]{2,1,0:T(8,128)(2,1)S(1)} %get-tuple-element.22), channel_id=1, source_target_pairs={{0,4},{2,6},{4,0},{6,2},{1,5},{3,7},{5,1},{7,3},{8,12},{10,14},{12... | collective-permute-start | bytes 2064392 | tf_op jit(solution)/shard_map/ppermute | solution.py:25
  32.7 2.3 %collective-permute-start.4 = (bf16[3,896,128]{2,1,0:T(8,128)(2,1)S(1)}, bf16[3,896,128]{2,1,0:T(8,128)(2,1)S(1)}, u32[]{:S(2)}, u32[]{:S(2)}) collective-permute-start(bf16[3,896,128]{2,1,0:T(8,128)(2,1)S(1)} %get-tuple-element.20), channel_id=1, source_target_pairs={{0,2},{2,4},{4,6},{6,0},{1,3},{3,5},{5,7},{7,1},{8,10},{10,12},{12... | collective-permute-start | bytes 2064392 | tf_op jit(solution)/shard_map/ppermute | solution.py:25
  35.0 4.2 %collective-permute-start.7 = (bf16[3,896,128]{2,1,0:T(8,128)(2,1)S(1)}, bf16[3,896,128]{2,1,0:T(8,128)(2,1)S(1)}, u32[]{:S(2)}, u32[]{:S(2)}) collective-permute-start(bf16[3,896,128]{2,1,0:T(8,128)(2,1)S(1)} %get-tuple-element.19), channel_id=1, source_target_pairs={{0,6},{2,0},{4,2},{6,4},{1,7},{3,1},{5,3},{7,5},{8,14},{10,8},{12,... | collective-permute-start | bytes 2064392 | tf_op jit(solution)/shard_map/ppermute | solution.py:25
  39.2 8.4 %collective-permute-done.block_ref.far_ref = bf16[3,896,128]{2,1,0:T(8,128)(2,1)S(1)} collective-permute-done((bf16[3,896,128]{2,1,0:T(8,128)(2,1)S(1)}, bf16[3,896,128]{2,1,0:T(8,128)(2,1)S(1)}, u32[]{:S(2)}, u32[]{:S(2)}) %collective-permute-start) | collective-permute-done | bytes 688160 | tf_op jit(solution)/shard_map/ppermute | solution.py:25
  47.6 4.5 %collective-permute-start.1 = (bf16[3,896,128]{2,1,0:T(8,128)(2,1)S(1)}, bf16[3,896,128]{2,1,0:T(8,128)(2,1)S(1)}, u32[]{:S(2)}, u32[]{:S(2)}) collective-permute-start(bf16[3,896,128]{2,1,0:T(8,128)(2,1)S(1)} %collective-permute-done.block_ref.far_ref), channel_id=1, source_target_pairs={{0,1},{1,0},{2,3},{3,2},{4,5},{5,4},{6,7},{7,6},{8,9},{9,8},{10,11... | collective-permute-start | bytes 2064392 | tf_op jit(solution)/shard_map/ppermute | solution.py:25
  53.0 10.3 %collective-permute-done.4.block_ref.refs_2_ = bf16[3,896,128]{2,1,0:T(8,128)(2,1)S(1)} collective-permute-done((bf16[3,896,128]{2,1,0:T(8,128)(2,1)S(1)}, bf16[3,896,128]{2,1,0:T(8,128)(2,1)S(1)}, u32[]{:S(2)}, u32[]{:S(2)}) %collective-permute-start.4) | collective-permute-done | bytes 688160 | tf_op jit(solution)/shard_map/ppermute | solution.py:25
  63.4 2.4 %collective-permute-start.5 = (bf16[3,896,128]{2,1,0:T(8,128)(2,1)S(1)}, bf16[3,896,128]{2,1,0:T(8,128)(2,1)}, u32[]{:S(2)}, u32[]{:S(2)}) collective-permute-start(bf16[3,896,128]{2,1,0:T(8,128)(2,1)S(1)} %collective-permute-done.4.block_ref.refs_2_), channel_id=1, source_target_pairs={{0,1},{1,0},{2,3},{3,2},{4,5},{5,4},{6,7},{7,6},{8,9},{9,8},{10,11... | collective-permute-start | bytes 2064392 | tf_op jit(solution)/shard_map/ppermute | solution.py:25
  65.8 1.9 %collective-permute-start.8 = (bf16[3,896,128]{2,1,0:T(8,128)(2,1)S(1)}, bf16[3,896,128]{2,1,0:T(8,128)(2,1)}, u32[]{:S(2)}, u32[]{:S(2)}) collective-permute-start(bf16[3,896,128]{2,1,0:T(8,128)(2,1)S(1)} %collective-permute-done.7.block_ref.refs_3_), channel_id=1, source_target_pairs={{0,1},{1,0},{2,3},{3,2},{4,5},{5,4},{6,7},{7,6},{8,9},{9,8},{10,11... | collective-permute-start | bytes 2064392 | tf_op jit(solution)/shard_map/ppermute | solution.py:25
  67.7 2.4 %collective-permute-start.2 = (bf16[3,896,128]{2,1,0:T(8,128)(2,1)S(1)}, bf16[3,896,128]{2,1,0:T(8,128)(2,1)}, u32[]{:S(2)}, u32[]{:S(2)}) collective-permute-start(bf16[3,896,128]{2,1,0:T(8,128)(2,1)S(1)} %get-tuple-element.21.block_ref), channel_id=1, source_target_pairs={{0,1},{1,0},{2,3},{3,2},{4,5},{5,4},{6,7},{7,6},{8,9},{9,8},{10,11... | collective-permute-start | bytes 2064392 | tf_op jit(solution)/shard_map/ppermute | solution.py:25
  73.8 4.8 %collective-permute-start.3 = (bf16[3,256,256]{2,1,0:T(8,128)(2,1)S(1)}, bf16[3,256,256]{2,1,0:T(8,128)(2,1)S(1)}, u32[]{:S(2)}, u32[]{:S(2)}) collective-permute-start(bf16[3,256,256]{2,1,0:T(8,128)(2,1)S(1)} %get-tuple-element.18), channel_id=1, source_target_pairs={{0,4},{2,6},{4,0},{6,2},{1,5},{3,7},{5,1},{7,3},{8,12},{10,14},{12... | collective-permute-start | bytes 1179656 | tf_op jit(solution)/shard_map/ppermute | solution.py:25
  80.3 2.8 %collective-permute-start.6 = (bf16[3,256,256]{2,1,0:T(8,128)(2,1)S(1)}, bf16[3,256,256]{2,1,0:T(8,128)(2,1)S(1)}, u32[]{:S(2)}, u32[]{:S(2)}) collective-permute-start(bf16[3,256,256]{2,1,0:T(8,128)(2,1)S(1)} %shard_map.77), channel_id=1, source_target_pairs={{0,6},{2,0},{4,2},{6,4},{1,7},{3,1},{5,3},{7,5},{8,14},{10,8},{12,... | collective-permute-start | bytes 1179656 | tf_op jit(solution)/shard_map/ppermute | solution.py:25
  84.9 2.6 %collective-permute-start.9 = (bf16[3,256,256]{2,1,0:T(8,128)(2,1)S(1)}, bf16[3,256,256]{2,1,0:T(8,128)(2,1)S(1)}, u32[]{:S(2)}, u32[]{:S(2)}) collective-permute-start(bf16[3,256,256]{2,1,0:T(8,128)(2,1)S(1)} %shard_map.78), channel_id=1, source_target_pairs={{0,2},{2,4},{4,6},{6,0},{1,3},{3,5},{5,7},{7,1},{8,10},{10,12},{12... | collective-permute-start | bytes 1179656 | tf_op jit(solution)/shard_map/ppermute | solution.py:25
  89.2 4.7 %collective-permute-done.6.next_ref = bf16[3,256,256]{2,1,0:T(8,128)(2,1)S(1)} collective-permute-done((bf16[3,256,256]{2,1,0:T(8,128)(2,1)S(1)}, bf16[3,256,256]{2,1,0:T(8,128)(2,1)S(1)}, u32[]{:S(2)}, u32[]{:S(2)}) %collective-permute-start.6) | collective-permute-done | bytes 393248 | tf_op jit(solution)/shard_map/ppermute | solution.py:25
  95.0 3.0 %collective-permute-start.10 = (bf16[2,256,256]{2,1,0:T(8,128)(2,1)S(1)}, bf16[2,256,256]{2,1,0:T(8,128)(2,1)S(1)}, u32[]{:S(2)}, u32[]{:S(2)}) collective-permute-start(bf16[2,256,256]{2,1,0:T(8,128)(2,1)S(1)} %shard_map.79.own_ref), channel_id=1, source_target_pairs={{0,4},{2,6},{4,0},{6,2},{1,5},{3,7},{5,1},{7,3},{8,12},{10,14},{12... | collective-permute-start | bytes 786440 | tf_op jit(solution)/shard_map/ppermute | solution.py:25
  98.0 3.9 %collective-permute-start.11 = (bf16[2,256,256]{2,1,0:T(8,128)(2,1)S(1)}, bf16[2,256,256]{2,1,0:T(8,128)(2,1)S(1)}, u32[]{:S(2)}, u32[]{:S(2)}) collective-permute-start(bf16[2,256,256]{2,1,0:T(8,128)(2,1)S(1)} %shard_map.79.own_ref), channel_id=1, source_target_pairs={{0,2},{2,4},{4,6},{6,0},{1,3},{3,5},{5,7},{7,1},{8,10},{10,12},{12... | collective-permute-start | bytes 786440 | tf_op jit(solution)/shard_map/ppermute | solution.py:25
  101.9 2.8 %collective-permute-start.12 = (bf16[2,256,256]{2,1,0:T(8,128)(2,1)S(1)}, bf16[2,256,256]{2,1,0:T(8,128)(2,1)S(1)}, u32[]{:S(2)}, u32[]{:S(2)}) collective-permute-start(bf16[2,256,256]{2,1,0:T(8,128)(2,1)S(1)} %shard_map.79.own_ref), channel_id=1, source_target_pairs={{0,6},{2,0},{4,2},{6,4},{1,7},{3,1},{5,3},{7,5},{8,14},{10,8},{12,... | collective-permute-start | bytes 786440 | tf_op jit(solution)/shard_map/ppermute | solution.py:25
  104.7 1.8 %shard_map.80.total_ref = f32[256,896]{1,0:T(8,128)S(1)} custom-call(bf16[2,256,256]{2,1,0:T(8,128)(2,1)S(1)} %shard_map.79.own_ref, bf16[2,256,256]{2,1,0:T(8,128)(2,1)S(1)} %collective-permute-done.10.arrived_ref, bf16[3,896,128]{2,1,0:T(8,128)(2,1)S(1)} %get-tuple-element.21.block_ref, bf16[3,896,128]{2,1,0:T(8,128)(2,1)S(1)} %copy-done.2, ...), custom_call_target="tpu_custom_call" | custom-call | flops 469762048 | bytes 458752 | tf_op jit(solution)/shard_map/pallas_call | solution.py:160
  107.2 2.5 %collective-permute-done.12.refs_1_ = bf16[2,256,256]{2,1,0:T(8,128)(2,1)S(1)} collective-permute-done((bf16[2,256,256]{2,1,0:T(8,128)(2,1)S(1)}, bf16[2,256,256]{2,1,0:T(8,128)(2,1)S(1)}, u32[]{:S(2)}, u32[]{:S(2)}) %collective-permute-start.12) | collective-permute-done | bytes 262176 | tf_op jit(solution)/shard_map/ppermute | solution.py:25
  109.7 2.9 %shard_map.81 = bf16[64,4,896]{2,1,0:T(4,128)(2,1)} custom-call(f32[256,896]{1,0:T(8,128)S(1)} %shard_map.80.total_ref, bf16[2,256,256]{2,1,0:T(8,128)(2,1)S(1)} %collective-permute-done.11.refs_0_, bf16[2,256,256]{2,1,0:T(8,128)(2,1)S(1)} %collective-permute-done.12.refs_1_, bf16[3,896,128]{2,1,0:T(8,128)(2,1)S(1)} %collective-permute-done.4.block_ref.refs_2_, ...), custom_call_target="tpu_custom_call" | custom-call | flops 469762048 | bytes 458752 | tf_op jit(solution)/shard_map/pallas_call | solution.py:160
  112.6 20.4 %all-to-all-start.1 = ((bf16[64,4,896]{2,1,0:T(4,128)(2,1)}), bf16[64,4,896]{2,1,0:T(4,128)(2,1)S(1)}, u32[]{:S(2)}, u32[]{:S(2)}) async-start(bf16[64,4,896]{2,1,0:T(4,128)(2,1)} %shard_map.81), calls=%async_computation.1 | async-start | bytes 917504 | tf_op jit(solution)/shard_map/all_to_all | solution.py:231
  133.3 26.5 %all-to-all-done.1 = bf16[64,4,896]{2,1,0:T(4,128)(2,1)S(1)} async-done(((bf16[64,4,896]{2,1,0:T(4,128)(2,1)}), bf16[64,4,896]{2,1,0:T(4,128)(2,1)S(1)}, u32[]{:S(2)}, u32[]{:S(2)}) %all-to-all-start.1) | async-done | bytes 458784 | tf_op jit(solution)/shard_map/all_to_all | solution.py:231
  160.3 4.9 %all_gather.8 = f32[2,448,128]{2,1,0:T(8,128)S(1)} all-gather(f32[1,448,128]{2,1,0:T(8,128)S(1)} %constant_dynamic-slice_fusion), channel_id=1, replica_groups=mesh['z'=16,'x'=4,'y'=4,'c'=2] {'c'}, dimensions={0}, use_global_device_ids=true | all-gather | bytes 688128 | tf_op jit(solution)/shard_map/all_gather | solution.py:236
  (44 shorter events, 18.9 us)
Async XLA Ops:
  0.0 25.2 %copy-start.8 = (bf16[1,128,3584]{2,1,0:T(8,128)(2,1)S(1)}, bf16[1,128,3584]{2,1,0:T(8,128)(2,1)}, u32[]{:S(2)}) copy-start(bf16[1,128,3584]{2,1,0:T(8,128)(2,1)} %param.13) | copy-start | bytes 2752516
  12.3 58.7 %all-to-all-start = ((bf16[64,8,896]{2,1,0:T(8,128)(2,1)}), bf16[64,8,896]{2,1,0:T(8,128)(2,1)S(1)}, u32[]{:S(2)}, u32[]{:S(2)}) async-start(bf16[64,8,896]{2,1,0:T(8,128)(2,1)} %shard_map.74), calls=%async_computation | async-start | bytes 1835008 | tf_op jit(solution)/shard_map/all_to_all | solution.py:198
  27.9 19.8 %collective-permute-start = (bf16[3,896,128]{2,1,0:T(8,128)(2,1)S(1)}, bf16[3,896,128]{2,1,0:T(8,128)(2,1)S(1)}, u32[]{:S(2)}, u32[]{:S(2)}) collective-permute-start(bf16[3,896,128]{2,1,0:T(8,128)(2,1)S(1)} %get-tuple-element.22), channel_id=1, source_target_pairs={{0,4},{2,6},{4,0},{6,2},{1,5},{3,7},{5,1},{7,3},{8,12},{10,14},{12... | collective-permute-start | bytes 2064392 | tf_op jit(solution)/shard_map/ppermute | solution.py:25
  32.7 30.7 %collective-permute-start.4 = (bf16[3,896,128]{2,1,0:T(8,128)(2,1)S(1)}, bf16[3,896,128]{2,1,0:T(8,128)(2,1)S(1)}, u32[]{:S(2)}, u32[]{:S(2)}) collective-permute-start(bf16[3,896,128]{2,1,0:T(8,128)(2,1)S(1)} %get-tuple-element.20), channel_id=1, source_target_pairs={{0,2},{2,4},{4,6},{6,0},{1,3},{3,5},{5,7},{7,1},{8,10},{10,12},{12... | collective-permute-start | bytes 2064392 | tf_op jit(solution)/shard_map/ppermute | solution.py:25
  35.0 30.8 %collective-permute-start.7 = (bf16[3,896,128]{2,1,0:T(8,128)(2,1)S(1)}, bf16[3,896,128]{2,1,0:T(8,128)(2,1)S(1)}, u32[]{:S(2)}, u32[]{:S(2)}) collective-permute-start(bf16[3,896,128]{2,1,0:T(8,128)(2,1)S(1)} %get-tuple-element.19), channel_id=1, source_target_pairs={{0,6},{2,0},{4,2},{6,4},{1,7},{3,1},{5,3},{7,5},{8,14},{10,8},{12,... | collective-permute-start | bytes 2064392 | tf_op jit(solution)/shard_map/ppermute | solution.py:25
  47.6 22.5 %collective-permute-start.1 = (bf16[3,896,128]{2,1,0:T(8,128)(2,1)S(1)}, bf16[3,896,128]{2,1,0:T(8,128)(2,1)S(1)}, u32[]{:S(2)}, u32[]{:S(2)}) collective-permute-start(bf16[3,896,128]{2,1,0:T(8,128)(2,1)S(1)} %collective-permute-done.block_ref.far_ref), channel_id=1, source_target_pairs={{0,1},{1,0},{2,3},{3,2},{4,5},{5,4},{6,7},{7,6},{8,9},{9,8},{10,11... | collective-permute-start | bytes 2064392 | tf_op jit(solution)/shard_map/ppermute | solution.py:25
  52.2 0.9 copy-start
  63.4 15.3 %collective-permute-start.5 = (bf16[3,896,128]{2,1,0:T(8,128)(2,1)S(1)}, bf16[3,896,128]{2,1,0:T(8,128)(2,1)}, u32[]{:S(2)}, u32[]{:S(2)}) collective-permute-start(bf16[3,896,128]{2,1,0:T(8,128)(2,1)S(1)} %collective-permute-done.4.block_ref.refs_2_), channel_id=1, source_target_pairs={{0,1},{1,0},{2,3},{3,2},{4,5},{5,4},{6,7},{7,6},{8,9},{9,8},{10,11... | collective-permute-start | bytes 2064392 | tf_op jit(solution)/shard_map/ppermute | solution.py:25
  65.8 17.4 %collective-permute-start.8 = (bf16[3,896,128]{2,1,0:T(8,128)(2,1)S(1)}, bf16[3,896,128]{2,1,0:T(8,128)(2,1)}, u32[]{:S(2)}, u32[]{:S(2)}) collective-permute-start(bf16[3,896,128]{2,1,0:T(8,128)(2,1)S(1)} %collective-permute-done.7.block_ref.refs_3_), channel_id=1, source_target_pairs={{0,1},{1,0},{2,3},{3,2},{4,5},{5,4},{6,7},{7,6},{8,9},{9,8},{10,11... | collective-permute-start | bytes 2064392 | tf_op jit(solution)/shard_map/ppermute | solution.py:25
  67.7 19.8 %collective-permute-start.2 = (bf16[3,896,128]{2,1,0:T(8,128)(2,1)S(1)}, bf16[3,896,128]{2,1,0:T(8,128)(2,1)}, u32[]{:S(2)}, u32[]{:S(2)}) collective-permute-start(bf16[3,896,128]{2,1,0:T(8,128)(2,1)S(1)} %get-tuple-element.21.block_ref), channel_id=1, source_target_pairs={{0,1},{1,0},{2,3},{3,2},{4,5},{5,4},{6,7},{7,6},{8,9},{9,8},{10,11... | collective-permute-start | bytes 2064392 | tf_op jit(solution)/shard_map/ppermute | solution.py:25
  70.1 0.9 copy-start.3
  71.0 1.1 copy-start.1
  72.1 1.1 copy-start.4
  73.8 13.7 %collective-permute-start.3 = (bf16[3,256,256]{2,1,0:T(8,128)(2,1)S(1)}, bf16[3,256,256]{2,1,0:T(8,128)(2,1)S(1)}, u32[]{:S(2)}, u32[]{:S(2)}) collective-permute-start(bf16[3,256,256]{2,1,0:T(8,128)(2,1)S(1)} %get-tuple-element.18), channel_id=1, source_target_pairs={{0,4},{2,6},{4,0},{6,2},{1,5},{3,7},{5,1},{7,3},{8,12},{10,14},{12... | collective-permute-start | bytes 1179656 | tf_op jit(solution)/shard_map/ppermute | solution.py:25
  80.3 13.5 %collective-permute-start.6 = (bf16[3,256,256]{2,1,0:T(8,128)(2,1)S(1)}, bf16[3,256,256]{2,1,0:T(8,128)(2,1)S(1)}, u32[]{:S(2)}, u32[]{:S(2)}) collective-permute-start(bf16[3,256,256]{2,1,0:T(8,128)(2,1)S(1)} %shard_map.77), channel_id=1, source_target_pairs={{0,6},{2,0},{4,2},{6,4},{1,7},{3,1},{5,3},{7,5},{8,14},{10,8},{12,... | collective-permute-start | bytes 1179656 | tf_op jit(solution)/shard_map/ppermute | solution.py:25
  84.9 19.8 %copy-start.2 = (bf16[3,896,128]{2,1,0:T(8,128)(2,1)S(1)}, bf16[3,896,128]{2,1,0:T(8,128)(2,1)}, u32[]{:S(2)}) copy-start(bf16[3,896,128]{2,1,0:T(8,128)(2,1)} %copy-done) | copy-start | bytes 2064388
  84.9 19.8 %copy-start.5 = (bf16[3,896,128]{2,1,0:T(8,128)(2,1)S(1)}, bf16[3,896,128]{2,1,0:T(8,128)(2,1)}, u32[]{:S(2)}) copy-start(bf16[3,896,128]{2,1,0:T(8,128)(2,1)} %copy-done.3) | copy-start | bytes 2064388
  84.9 9.9 %collective-permute-start.9 = (bf16[3,256,256]{2,1,0:T(8,128)(2,1)S(1)}, bf16[3,256,256]{2,1,0:T(8,128)(2,1)S(1)}, u32[]{:S(2)}, u32[]{:S(2)}) collective-permute-start(bf16[3,256,256]{2,1,0:T(8,128)(2,1)S(1)} %shard_map.78), channel_id=1, source_target_pairs={{0,2},{2,4},{4,6},{6,0},{1,3},{3,5},{5,7},{7,1},{8,10},{10,12},{12... | collective-permute-start | bytes 1179656 | tf_op jit(solution)/shard_map/ppermute | solution.py:25
  95.0 9.7 %collective-permute-start.10 = (bf16[2,256,256]{2,1,0:T(8,128)(2,1)S(1)}, bf16[2,256,256]{2,1,0:T(8,128)(2,1)S(1)}, u32[]{:S(2)}, u32[]{:S(2)}) collective-permute-start(bf16[2,256,256]{2,1,0:T(8,128)(2,1)S(1)} %shard_map.79.own_ref), channel_id=1, source_target_pairs={{0,4},{2,6},{4,0},{6,2},{1,5},{3,7},{5,1},{7,3},{8,12},{10,14},{12... | collective-permute-start | bytes 786440 | tf_op jit(solution)/shard_map/ppermute | solution.py:25
  98.0 9.2 %collective-permute-start.11 = (bf16[2,256,256]{2,1,0:T(8,128)(2,1)S(1)}, bf16[2,256,256]{2,1,0:T(8,128)(2,1)S(1)}, u32[]{:S(2)}, u32[]{:S(2)}) collective-permute-start(bf16[2,256,256]{2,1,0:T(8,128)(2,1)S(1)} %shard_map.79.own_ref), channel_id=1, source_target_pairs={{0,2},{2,4},{4,6},{6,0},{1,3},{3,5},{5,7},{7,1},{8,10},{10,12},{12... | collective-permute-start | bytes 786440 | tf_op jit(solution)/shard_map/ppermute | solution.py:25
  101.9 7.8 %collective-permute-start.12 = (bf16[2,256,256]{2,1,0:T(8,128)(2,1)S(1)}, bf16[2,256,256]{2,1,0:T(8,128)(2,1)S(1)}, u32[]{:S(2)}, u32[]{:S(2)}) collective-permute-start(bf16[2,256,256]{2,1,0:T(8,128)(2,1)S(1)} %shard_map.79.own_ref), channel_id=1, source_target_pairs={{0,6},{2,0},{4,2},{6,4},{1,7},{3,1},{5,3},{7,5},{8,14},{10,8},{12,... | collective-permute-start | bytes 786440 | tf_op jit(solution)/shard_map/ppermute | solution.py:25
  106.5 26.4 %copy-start.6 = (s32[128,2]{0,1:T(2,128)S(1)}, s32[128,2]{0,1:T(2,128)}, u32[]{:S(2)}) copy-start(s32[128,2]{0,1:T(2,128)} %param.9) | copy-start | bytes 3076
  106.5 26.4 %copy-start.7 = (f32[128,2]{0,1:T(2,128)S(1)}, f32[128,2]{0,1:T(2,128)}, u32[]{:S(2)}) copy-start(f32[128,2]{0,1:T(2,128)} %param.10) | copy-start | bytes 3076
  112.6 47.2 %all-to-all-start.1 = ((bf16[64,4,896]{2,1,0:T(4,128)(2,1)}), bf16[64,4,896]{2,1,0:T(4,128)(2,1)S(1)}, u32[]{:S(2)}, u32[]{:S(2)}) async-start(bf16[64,4,896]{2,1,0:T(4,128)(2,1)} %shard_map.81), calls=%async_computation.1 | async-start | bytes 917504 | tf_op jit(solution)/shard_map/all_to_all | solution.py:231
